TPU v7x, 32 devices: a whole 2x2x4 slice. The times are simulated.
32 devices in a mesh: groups: 2 (over y), variant: 16 (over z, x, core), tensor: 1.
Axes of the slice: x: 2, y: 2, z: 4, core: 2. Of those that a mesh axis runs over, the one named last changes fastest.
Arguments:
- hidden: bfloat16 [512, 8192], P(('groups', 'variant'), 'tensor'), parts along dimension 0, may hold values from -6 to 6
- norm_gain: bfloat16 [8192], P('tensor'), may hold values from 0.5 to 1.5
- base_weight: bfloat16 [8192, 512], P('tensor'), may hold values from -0.0625 to 0.0625
- delta_codes: bfloat16 [1, 32, 1024, 512], P('tensor', ('groups', 'variant')), parts along dimension 1, may hold values from 0 to 15
- delta_scales: float32 [1, 32, 8, 512], P('tensor', ('groups', 'variant')), parts along dimension 1, may hold values from 0.0003 to 0.003
- delta_zeros: float32 [1, 32, 8, 512], P('tensor', ('groups', 'variant')), parts along dimension 1, may hold values from 6 to 9
- variant_ids: int32 [512, 1], P(('groups', 'variant')), parts along dimension 0, may hold values from 0 to 1; in each aligned block of 16 rows (0 to 15, 16 to 31, ...) at most 16 rows name the same one
- positions: int32 [512], P(('groups', 'variant')), parts along dimension 0, may hold values from 0 to 8191
Outputs:
- keys: bfloat16 [512, 512], P(('groups', 'variant'), 'tensor'), parts along dimension 0
There are 2 independent parts, one for each index of `groups`. A program takes and returns all parts, laid end to end along the dimension named above; an argument that names none is the same for every part. Nothing has to cross between parts.
Inputs may be any that keep to these rules, and one draw needn't show every extreme that they name: `variant_ids`: in each aligned block of 16 rows (the rows of one device along `variant`) no variant is named by more than 16 rows, and in some block one variant is named by exactly 16 rows; every variant is named by some row.
All inputs are finite; a program needn't handle non-finite values.
Results may differ from a plain program's by a relative error of at most 0.0075.
Values may be sent and summed in bfloat16 or wider, within the bound.
No kernel may reach another device: no remote copies, remote signals or barrier semaphores. Data moves between devices by JAX's collectives and lax.ppermute only.
A program may use at most 64 MiB of HBM per device.

v0:
```python
import jax
import jax.numpy as jnp
from jax import lax
from jax.sharding import PartitionSpec as P

HEAD = 128
OWNERS = 8


rope_theta = 500000.0
epsilon = 1e-05


def rotate_keys(projected, position):
    row_count = projected.shape[0]
    head_count = projected.shape[1] // HEAD
    half_size = HEAD // 2
    per_head = projected.reshape(row_count, head_count, HEAD)
    frequency = rope_theta ** (-(jnp.arange(half_size, dtype=jnp.float32) * 2.0 / HEAD))
    angles = position.astype(jnp.float32)[:, None] * frequency[None, :]
    cosine = jnp.cos(angles)[:, None, :]
    sine = jnp.sin(angles)[:, None, :]
    first = per_head[:, :, :half_size]
    second = per_head[:, :, half_size:]
    turned = jnp.concatenate(
        [first * cosine - second * sine, second * cosine + first * sine], axis=2
    )
    return turned.reshape(row_count, head_count * HEAD).astype(jnp.bfloat16)


def dequantize(code_block, scale_block, zero_block):
    group_count = scale_block.shape[-2]
    leading_dims = code_block.shape[:-2]
    slice_rows = code_block.shape[-2]
    column_count = code_block.shape[-1]
    grouped = code_block.astype(jnp.float32).reshape(
        leading_dims + (group_count, slice_rows // group_count, column_count)
    )
    values = (grouped - zero_block[..., :, None, :]) * scale_block[..., :, None, :]
    return values.reshape(leading_dims + (slice_rows, column_count))


def per_device(
    hidden, norm_gain, base_weight, delta_codes, delta_scales, delta_zeros, variant_ids, positions
):
    row_count, half_width = hidden.shape
    device_count = lax.axis_size("variant")
    variant_count = device_count // OWNERS
    capacity = min(row_count, max(2, 2 * row_count // variant_count))
    slice_rows = delta_codes.shape[2]
    column_count = base_weight.shape[1]
    floats = hidden.astype(jnp.float32)
    local_squares = jnp.sum(floats * floats, axis=1)
    all_squares = lax.psum(local_squares, "tensor")
    full_width = half_width * lax.axis_size("tensor")
    normed = (
        floats
        * lax.rsqrt(all_squares / full_width + epsilon)[:, None]
        * norm_gain.astype(jnp.float32)[None, :]
    ).astype(jnp.bfloat16)
    chosen = variant_ids[:, 0]
    labels = jnp.arange(variant_count, dtype=jnp.int32)
    member = (chosen[:, None] == labels[None, :]).astype(jnp.int32)
    earlier = jnp.cumsum(member, axis=0) - member
    ranking = jnp.sum(earlier * member, axis=1)
    target_slot = chosen * capacity + ranking
    slot_labels = jnp.arange(variant_count * capacity, dtype=jnp.int32)
    placing = slot_labels[:, None] == target_slot[None, :]
    place_send = placing.astype(jnp.bfloat16).reshape(variant_count, capacity, row_count)
    place_back = placing.astype(jnp.float32)
    feature_pieces = normed.reshape(row_count, OWNERS, slice_rows)
    outgoing = jnp.einsum(
        "vcr,rjs->vjcs", place_send, feature_pieces, preferred_element_type=jnp.float32
    )
    outgoing = outgoing.astype(jnp.bfloat16).reshape(device_count, capacity, slice_rows)
    local_delta = dequantize(delta_codes[0, 0], delta_scales[0, 0], delta_zeros[0, 0]).astype(
        jnp.bfloat16
    )
    products = jnp.einsum(
        "acs,sk->ack",
        lax.all_to_all(outgoing, "variant", split_axis=0, concat_axis=0, tiled=True),
        local_delta,
        preferred_element_type=jnp.float32,
    )
    base_part = jnp.dot(normed, base_weight, preferred_element_type=jnp.float32)
    returned = lax.all_to_all(products, "variant", split_axis=0, concat_axis=0, tiled=True)
    summed = jnp.sum(returned.reshape(variant_count, OWNERS, capacity, column_count), axis=1)
    summed = summed.reshape(variant_count * capacity, column_count)
    delta_rows = jnp.einsum("sr,sk->rk", place_back, summed, precision=lax.Precision.HIGHEST)
    combined = lax.psum_scatter(base_part + delta_rows, "tensor", scatter_dimension=1, tiled=True)
    return rotate_keys(combined, positions)


def solution(mesh):
    in_specs = (
        P(("groups", "variant"), "tensor"),
        P("tensor"),
        P("tensor", None),
        P("tensor", ("groups", "variant"), None, None),
        P("tensor", ("groups", "variant"), None, None),
        P("tensor", ("groups", "variant"), None, None),
        P(("groups", "variant"), None),
        P(("groups", "variant")),
    )
    out_specs = P(("groups", "variant"), "tensor")
    return jax.shard_map(
        per_device, mesh=mesh, in_specs=in_specs, out_specs=out_specs, check_vma=False
    )
```

profile of v0, /device:TPU:0, one launch (start us, length us, event | category | flops | bytes accessed | tf_op | source)
XLA Modules:
  0.0 49.4 jit_solution(2011244778409729965)
XLA Ops:
  0.0 0.7 %convert_element_type.39 = f32[8192]{0:T(1024)S(1)} convert(bf16[8192]{0:T(1024)(128)(2,1)} %param.9) | non-fusion elementwise | flops 8192 | bytes 49152 | tf_op jit(solution)/shard_map/convert_element_type | solution.py:59
  0.7 1.2 %fusion.5 = f32[16]{0:T(128)S(1)} fusion(bf16[16,8192]{1,0:T(8,128)(2,1)} %param.8), kind=kLoop, calls=%fused_computation.10 | loop fusion | flops 393200 | bytes 262208 | tf_op jit(solution)/shard_map/reduce_sum | solution.py:53
  2.0 1.1 %fusion.7 = bf16[16,8192]{1,0:T(8,128)(2,1)S(1)} fusion(bf16[16,8192]{1,0:T(8,128)(2,1)} %param.8, f32[8192]{0:T(1024)S(1)} %convert_element_type.39, f32[16]{0:T(128)S(1)} %add_rsqrt_fusion), kind=kLoop, calls=%fused_computation.12 | loop fusion | flops 524288 | bytes 557120 | tf_op jit(solution)/shard_map/convert_element_type | solution.py:60
  3.1 0.2 copy.15
  3.2 0.7 %fusion.14 = s32[16,2]{1,0:T(8,128)S(1)} fusion(s32[16]{0:T(128)} %bitcast.41), kind=kLoop, calls=%fused_computation.29 | loop fusion | flops 64 | bytes 192 | tf_op jit(solution)/shard_map/convert_element_type | solution.py:63
  4.0 0.8 %select_reduce_fusion = s32[16]{0:T(128)S(1)} fusion(s32[16,2]{1,0:T(8,128)S(1)} %reduce_window_sum.11, s32[16]{0:T(128)} %bitcast.42), kind=kLoop, calls=%fused_computation.27 | loop fusion | flops 144 | bytes 256 | tf_op jit(solution)/shard_map/reduce_sum | solution.py:65
  4.8 0.7 %multiply_add_fusion.1 = s32[16]{0:T(128)S(1)} fusion(s32[16]{0:T(128)S(1)} %select_reduce_fusion, s32[16,1]{0,1:T(1,128)} %param.14), kind=kLoop, calls=%fused_computation.32 | loop fusion | flops 32 | bytes 192 | tf_op jit(solution)/shard_map/add | solution.py:66
  5.5 0.4 fusion.2
  5.8 0.8 %copy.11 = bf16[2,8,16,1024]{3,2,1,0:T(8,128)(2,1)} copy(bf16[2,8,16,1024]{3,2,0,1:T(8,128)(2,1)S(1)} %fusion.2) | data formatting | bytes 1048576 | tf_op jit(solution)/shard_map/convert_element_type | solution.py:75
  6.7 7.4 %all-to-all-start = ((bf16[16,16,1024]{2,1,0:T(8,128)(2,1)}), bf16[16,16,1024]{2,1,0:T(8,128)(2,1)S(1)}, u32[]{:S(2)}, u32[]{:S(2)}) async-start(bf16[16,16,1024]{2,1,0:T(8,128)(2,1)} %bitcast.4), calls=%async_computation | async-start | bytes 1048576 | tf_op jit(solution)/shard_map/all_to_all | solution.py:81
  14.0 0.0 copy-done
  14.0 0.0 copy-done.1
  14.1 0.3 fusion.1
  14.3 0.0 copy-start.3
  14.3 14.2 %all-to-all-done = bf16[16,16,1024]{2,1,0:T(8,128)(2,1)S(1)} async-done(((bf16[16,16,1024]{2,1,0:T(8,128)(2,1)}), bf16[16,16,1024]{2,1,0:T(8,128)(2,1)S(1)}, u32[]{:S(2)}, u32[]{:S(2)}) %all-to-all-start) | async-done | bytes 524320 | tf_op jit(solution)/shard_map/all_to_all | solution.py:81
  28.5 1.2 %fusion.3 = f32[16,16,512]{2,1,0:T(8,128)} fusion(bf16[16,16,1024]{2,1,0:T(8,128)(2,1)S(1)} %all-to-all-done, bf16[1024,512]{1,0:T(8,128)(2,1)S(1)} %fusion.1), kind=kOutput, calls=%fused_computation.6 | convolution fusion | flops 268435456 | bytes 2097152 | tf_op jit(solution)/shard_map/acs,sk->ack/dot_general | solution.py:79
  29.7 4.1 %all-to-all-start.1 = ((f32[16,16,512]{2,1,0:T(8,128)}), f32[16,16,512]{2,1,0:T(8,128)S(1)}, u32[]{:S(2)}, u32[]{:S(2)}) async-start(f32[16,16,512]{2,1,0:T(8,128)} %fusion.3), calls=%async_computation.1 | async-start | bytes 1048576 | tf_op jit(solution)/shard_map/all_to_all | solution.py:86
  33.9 0.1 multiply_cosine_fusion
  34.0 4.6 %fusion.15 = f32[16,512]{1,0:T(8,128)S(1)} fusion(bf16[16,8192]{1,0:T(8,128)(2,1)S(1)} %fusion.7, bf16[8192,512]{1,0:T(8,128)(2,1)} %param.10), kind=kOutput, calls=%fused_computation.34 | convolution fusion | flops 134217728 | bytes 8683520 | tf_op jit(solution)/shard_map/dot_general | solution.py:85
  38.6 9.7 %all-to-all-done.1 = f32[16,16,512]{2,1,0:T(8,128)S(1)} async-done(((f32[16,16,512]{2,1,0:T(8,128)}), f32[16,16,512]{2,1,0:T(8,128)S(1)}, u32[]{:S(2)}, u32[]{:S(2)}) %all-to-all-start.1) | async-done | bytes 524320 | tf_op jit(solution)/shard_map/all_to_all | solution.py:86
  48.3 0.2 convolution_add_fusion
  48.6 0.1 subtract_convert_fusion
  48.7 0.1 pad_maximum_fusion
  48.8 0.6 %copy.20 = bf16[2,8,4,128]{3,1,2,0:T(8,128)(2,1)} copy(bf16[2,8,4,128]{3,2,1,0:T(4,128)(2,1)S(1)} %bitcast.38) | data formatting | bytes 32768
  (12 shorter events, 0.1 us)
Async XLA Ops:
  0.7 13.3 %copy-start = (bf16[1,1,1024,512]{3,2,1,0:T(8,128)(2,1)S(1)}, bf16[1,1,1024,512]{3,2,1,0:T(8,128)(2,1)}, u32[]{:S(2)}) copy-start(bf16[1,1,1024,512]{3,2,1,0:T(8,128)(2,1)} %param.11) | copy-start | bytes 3145732
  0.7 13.3 %copy-start.1 = (f32[1,1,8,512]{3,2,1,0:T(8,128)S(1)}, f32[1,1,8,512]{3,2,1,0:T(8,128)}, u32[]{:S(2)}) copy-start(f32[1,1,8,512]{3,2,1,0:T(8,128)} %param.12) | copy-start | bytes 49156
  0.7 13.3 %copy-start.2 = (f32[1,1,8,512]{3,2,1,0:T(8,128)S(1)}, f32[1,1,8,512]{3,2,1,0:T(8,128)}, u32[]{:S(2)}) copy-start(f32[1,1,8,512]{3,2,1,0:T(8,128)} %param.13) | copy-start | bytes 49156
  6.7 21.8 %all-to-all-start = ((bf16[16,16,1024]{2,1,0:T(8,128)(2,1)}), bf16[16,16,1024]{2,1,0:T(8,128)(2,1)S(1)}, u32[]{:S(2)}, u32[]{:S(2)}) async-start(bf16[16,16,1024]{2,1,0:T(8,128)(2,1)} %bitcast.4), calls=%async_computation | async-start | bytes 1048576 | tf_op jit(solution)/shard_map/all_to_all | solution.py:81
  14.3 19.5 %copy-start.3 = (s32[16]{0:T(128)S(1)}, s32[16]{0:T(128)}, u32[]{:S(2)}) copy-start(s32[16]{0:T(128)} %param.15) | copy-start | bytes 196
  29.7 18.6 %all-to-all-start.1 = ((f32[16,16,512]{2,1,0:T(8,128)}), f32[16,16,512]{2,1,0:T(8,128)S(1)}, u32[]{:S(2)}, u32[]{:S(2)}) async-start(f32[16,16,512]{2,1,0:T(8,128)} %fusion.3), calls=%async_computation.1 | async-start | bytes 1048576 | tf_op jit(solution)/shard_map/all_to_all | solution.py:86
where the time goes:
time: 49.8 us; the launch traced here: 49.4 us
  waiting for transfers between devices  23.9 us (48%)
  starting transfers between devices  11.5 us (23%)
  matrix products  6.34 us (13%)
  other arithmetic  5.9 us (12%)
  local copies, waits for them, and re-layouts  1.62 us (3%)
    all_to_all x1, waiting for transfers between devices, per_device(): lax.all_to_all(outgoing, 'variant', split_axis=0, concat_axis=0, tiled=True)  14.2 us
    all_to_all x1, waiting for transfers between devices, per_device(): lax.all_to_all(products, 'variant', split_axis=0, concat_axis=0, tiled=True)  9.74 us
    all_to_all x1, starting transfers between devices, per_device(): lax.all_to_all(outgoing, 'variant', split_axis=0, concat_axis=0, tiled=True)  7.36 us
    dot_general x1, matrix products, per_device(): base_part = jnp.dot(normed, base_weight, preferred_element_type=jnp.float32)  4.56 us
    all_to_all x1, starting transfers between devices, per_device(): lax.all_to_all(products, 'variant', split_axis=0, concat_axis=0, tiled=True)  4.1 us
    dot_general x1, matrix products, per_device(): jnp.einsum('acs,sk->ack', lax.all_to_all(outgoing, 'variant', split_axis=...  1.23 us
    reduce_sum x1, other arithmetic, per_device(): local_squares = jnp.sum(floats * floats, axis=1)  1.22 us
    convert_element_type x1, other arithmetic, per_device(): normed = (floats * lax.rsqrt(all_squares / full_width + epsilon)[:, None]...  1.09 us
  transfers between devices with their start and end apart: 2, of which 2 were waited for; matrix products, arithmetic and copies ran while one was open for 10% of the time, Pallas kernels for 0%

commit v1 on v0

--- a/solution.py
+++ b/solution.py
@@ -1,6 +1,10 @@
+import functools
+
 import jax
 import jax.numpy as jnp
 from jax import lax
+from jax.experimental import pallas as pl
+from jax.experimental.pallas import tpu as pltpu
 from jax.sharding import PartitionSpec as P
 
 HEAD = 128
@@ -40,7 +44,7 @@
     return values.reshape(leading_dims + (slice_rows, column_count))
 
 
-def per_device(
+def general(
     hidden, norm_gain, base_weight, delta_codes, delta_scales, delta_zeros, variant_ids, positions
 ):
     row_count, half_width = hidden.shape
@@ -91,7 +95,154 @@
     return rotate_keys(combined, positions)
 
 
+def prepare_kernel(pieces, ids_ref, hidden_ref, gain_ref, out_ref):
+    floats = hidden_ref[...].astype(jnp.float32)
+    row_count, width = floats.shape
+    mean_square = jnp.sum(floats * floats, axis=1, keepdims=True) / width
+    normed = floats * lax.rsqrt(mean_square + epsilon) * gain_ref[...].astype(jnp.float32)
+    square = (row_count, row_count)
+    diagonal = lax.broadcasted_iota(jnp.int32, square, 0) == lax.broadcasted_iota(jnp.int32, square, 1)
+    ids = jnp.sum(jnp.where(diagonal, ids_ref[...], 0), axis=1, keepdims=True)
+    piece_width = width // pieces
+    for variant in range(out_ref.shape[0] // pieces):
+        kept = jnp.where(ids == variant, normed, 0.0).astype(jnp.bfloat16)
+        for piece in range(pieces):
+            out_ref[variant * pieces + piece] = kept[:, piece * piece_width : (piece + 1) * piece_width]
+
+
+def weight_kernel(
+    core_ref, own_codes, other_codes, own_groups, other_groups, base, out_ref, codes, groups, arrived
+):
+    slice_rows = codes.shape[1]
+    core = core_ref[0]
+    copies = [
+        pltpu.make_async_copy(own_groups, groups.at[core], arrived.at[0]),
+        pltpu.make_async_copy(other_groups, groups.at[1 - core], arrived.at[1]),
+        pltpu.make_async_copy(own_codes, codes.at[core], arrived.at[2]),
+        pltpu.make_async_copy(other_codes, codes.at[1 - core], arrived.at[3]),
+    ]
+    for copy in copies:
+        copy.start()
+    for copy in copies:
+        copy.wait()
+    group_count = groups.shape[1] // 2
+    size = slice_rows // group_count
+    for half in range(2):
+        for group in range(group_count):
+            rows = slice(group * size, (group + 1) * size)
+            scale = groups[half, group : group + 1]
+            zero = groups[half, group_count + group : group_count + group + 1]
+            delta = (codes[half, rows].astype(jnp.float32) - zero) * scale
+            rows = slice(half * slice_rows + group * size, half * slice_rows + (group + 1) * size)
+            out_ref[rows] = (base[rows].astype(jnp.float32) + delta).astype(jnp.bfloat16)
+
+
+def product_kernel(rows_ref, weight_ref, out_ref):
+    count, size, width = rows_ref.shape
+    rows = rows_ref[...].reshape(count * size, width)
+    total = jnp.dot(rows, weight_ref[...], preferred_element_type=jnp.float32)
+    out_ref[...] = total.reshape(out_ref.shape).astype(out_ref.dtype)
+
+
+def finish_kernel(parts_ref, cosine_ref, sine_ref, out_ref):
+    total = jnp.sum(parts_ref[...].astype(jnp.float32), axis=0)
+    for head in range(total.shape[1] // HEAD):
+        columns = slice(head * HEAD, (head + 1) * HEAD)
+        block = total[:, columns]
+        swapped = pltpu.roll(block, HEAD // 2, 1)
+        out_ref[:, columns] = (block * cosine_ref[...] + swapped * sine_ref[...]).astype(out_ref.dtype)
+
+
+def turn_factors(position):
+    half_size = HEAD // 2
+    frequency = rope_theta ** (-(jnp.arange(half_size, dtype=jnp.float32) * 2.0 / HEAD))
+    angles = position.astype(jnp.float32)[:, None] * frequency[None, :]
+    cosine, sine = jnp.cos(angles), jnp.sin(angles)
+    return jnp.concatenate([cosine, cosine], axis=1), jnp.concatenate([-sine, sine], axis=1)
+
+
+VMEM = pl.BlockSpec(memory_space=pltpu.VMEM)
+SMEM = pl.BlockSpec(memory_space=pltpu.SMEM)
+HBM = pl.BlockSpec(memory_space=pltpu.HBM)
+
+
+def paired(
+    hidden, norm_gain, base_weight, delta_codes, delta_scales, delta_zeros, variant_ids, positions
+):
+    row_count, width = hidden.shape
+    device_count = lax.axis_size("variant")
+    variant_count = device_count // OWNERS
+    pieces = OWNERS // 2
+    slice_rows, column_count = delta_codes.shape[2:]
+    place = lax.axis_index("variant")
+    parity = [list(range(first, device_count, 2)) for first in range(2)]
+    swap = [(index, index ^ 1) for index in range(device_count)]
+
+    own_codes = delta_codes[0, 0]
+    own_groups = jnp.concatenate([delta_scales[0, 0], delta_zeros[0, 0]], axis=0)
+    other_codes = lax.ppermute(own_codes, "variant", swap)
+    other_groups = lax.ppermute(own_groups, "variant", swap)
+    outgoing = pl.pallas_call(
+        functools.partial(prepare_kernel, pieces),
+        out_shape=jax.ShapeDtypeStruct((variant_count * pieces, row_count, width // pieces), jnp.bfloat16),
+        in_specs=[VMEM] * 3,
+        out_specs=VMEM,
+        compiler_params=pltpu.CompilerParams(vmem_limit_bytes=16 << 20),
+        name="prepare",
+    )(variant_ids.T, hidden, norm_gain[None, :])
+    both_rows = 2 * slice_rows
+    weight = pl.pallas_call(
+        weight_kernel,
+        out_shape=jax.ShapeDtypeStruct((both_rows, column_count), jnp.bfloat16),
+        in_specs=[SMEM] + [pl.BlockSpec(memory_space=pl.ANY)] * 4 + [VMEM],
+        out_specs=VMEM,
+        scratch_shapes=[
+            pltpu.VMEM((2, slice_rows, column_count), jnp.bfloat16),
+            pltpu.VMEM((2,) + own_groups.shape, jnp.float32),
+            pltpu.SemaphoreType.DMA((4,)),
+        ],
+        compiler_params=pltpu.CompilerParams(vmem_limit_bytes=16 << 20),
+        cost_estimate=pl.CostEstimate(
+            flops=4 * both_rows * column_count, bytes_accessed=6 * both_rows * column_count, transcendentals=0
+        ),
+        name="weight",
+    )(
+        lax.rem(place, 2)[None],
+        own_codes,
+        other_codes,
+        own_groups,
+        other_groups,
+        lax.dynamic_slice_in_dim(base_weight, lax.div(lax.rem(place, OWNERS), 2) * both_rows, both_rows, 0),
+    )
+    incoming = lax.all_to_all(
+        outgoing, "variant", split_axis=0, concat_axis=0, tiled=True, axis_index_groups=parity
+    )
+    products = pl.pallas_call(
+        product_kernel,
+        out_shape=jax.ShapeDtypeStruct((device_count // 2, row_count, column_count), jnp.bfloat16),
+        in_specs=[VMEM, VMEM],
+        out_specs=VMEM,
+        compiler_params=pltpu.CompilerParams(vmem_limit_bytes=16 << 20),
+        name="product",
+    )(incoming, weight)
+    returned = lax.all_to_all(
+        products, "variant", split_axis=0, concat_axis=0, tiled=True, axis_index_groups=parity
+    )
+    cosine, sine = turn_factors(positions)
+    return pl.pallas_call(
+        finish_kernel,
+        out_shape=jax.ShapeDtypeStruct((row_count, column_count), jnp.bfloat16),
+        in_specs=[VMEM] * 3,
+        out_specs=VMEM,
+        compiler_params=pltpu.CompilerParams(vmem_limit_bytes=8 << 20),
+        name="finish",
+    )(returned, cosine, sine)
+
+
 def solution(mesh):
+    devices = mesh.shape["variant"]
+    small = mesh.shape["tensor"] == 1 and devices == 2 * OWNERS
+    per_device = paired if small else general
     in_specs = (
         P(("groups", "variant"), "tensor"),
         P("tensor"),

time: 49.8 us -> 40.8 us (0.82)
  waiting for transfers between devices: 23.9 us -> 14.9 us
  local copies, waits for them, and re-layouts: 1.62 us -> 8.21 us
  matrix products: 6.34 us -> 0 us
  Pallas kernels: 0 us -> 5.04 us
  other arithmetic: 5.9 us -> 0.95 us
    all_to_all x2, waiting for transfers between devices: 23.9 us -> 14.8 us  [the longest x1 7.7 us: paired(): lax.all_to_all(outgoing, 'variant', split_axis=0, concat_axis=0, tiled=Tr...]
    dot_general x4 -> x0, matrix products: 6.34 us -> none  [the longest x1 4.56 us: per_device(): base_part = jnp.dot(normed, base_weight, preferred_element_type=jnp.float32)]
    pallas_call x0 -> x4, Pallas kernels: none -> 5.04 us  [the longest x1 2.13 us: paired(): pl.pallas_call(weight_kernel, out_shape=jax.ShapeDtypeStruct((both_rows,...]
    unnamed x10 -> x12, local copies, waits for them, and re-layouts: 0.78 us -> 5.73 us
    convert_element_type x5 -> x1, other arithmetic: 2.8 us -> 0.01 us  [turn_factors(): angles = position.astype(jnp.float32)[:, None] * frequency[None, :]]
    reduce_sum x3 -> x0, other arithmetic: 2.09 us -> none  [the longest x1 1.22 us: per_device(): local_squares = jnp.sum(floats * floats, axis=1)]
    dynamic_slice x0 -> x1, local copies, waits for them, and re-layouts: none -> 1.74 us  [paired(): lax.dynamic_slice_in_dim(base_weight, lax.div(lax.rem(place, OWNERS), 2)...]
    all_to_all x2, starting transfers between devices: 11.5 us -> 10.4 us  [the longest x1 6.8 us: paired(): lax.all_to_all(outgoing, 'variant', split_axis=0, concat_axis=0, tiled=Tr...]
  transfers between devices with their start and end apart: 2 -> 4, of which waited for: 2 -> 2; matrix products, arithmetic and copies ran while one was open for 10% -> 8% of each run, Pallas kernels for 0% -> 8%
where the time goes in v1:
time: 40.8 us; the launch traced here: 40.3 us
  waiting for transfers between devices  14.9 us (37%)
  starting transfers between devices  11.1 us (27%)
  local copies, waits for them, and re-layouts  8.21 us (20%)
  Pallas kernels  5.04 us (12%)
  other arithmetic  0.95 us (2%)
    all_to_all x1, waiting for transfers between devices, paired(): lax.all_to_all(outgoing, 'variant', split_axis=0, concat_axis=0, tiled=Tr...  7.7 us
    all_to_all x1, waiting for transfers between devices, paired(): lax.all_to_all(products, 'variant', split_axis=0, concat_axis=0, tiled=Tr...  7.15 us
    all_to_all x1, starting transfers between devices, paired(): lax.all_to_all(outgoing, 'variant', split_axis=0, concat_axis=0, tiled=Tr...  6.8 us
    unnamed x12, local copies, waits for them, and re-layouts  5.73 us
    all_to_all x1, starting transfers between devices, paired(): lax.all_to_all(products, 'variant', split_axis=0, concat_axis=0, tiled=Tr...  3.64 us
    pallas_call x1, Pallas kernels, paired(): pl.pallas_call(weight_kernel, out_shape=jax.ShapeDtypeStruct((both_rows,...  2.13 us
    dynamic_slice x1, local copies, waits for them, and re-layouts, paired(): lax.dynamic_slice_in_dim(base_weight, lax.div(lax.rem(place, OWNERS), 2)...  1.74 us
    pallas_call x1, Pallas kernels, paired(): pl.pallas_call(functools.partial(prepare_kernel, pieces), out_shape=jax.S...  1.12 us
  transfers between devices with their start and end apart: 4, of which 2 were waited for; matrix products, arithmetic and copies ran while one was open for 8% of the time, Pallas kernels for 8%

profile of v1, /device:TPU:0, one launch (start us, length us, event | category | flops | bytes accessed | tf_op | source)
XLA Modules:
  0.0 40.3 jit_solution(11677767126544164727)
XLA Ops:
  0.0 0.5 %collective-permute-start = (bf16[1024,512]{1,0:T(8,128)(2,1)}, bf16[1024,512]{1,0:T(8,128)(2,1)}, u32[]{:S(2)}, u32[]{:S(2)}) collective-permute-start(bf16[1024,512]{1,0:T(8,128)(2,1)} %bitcast.5), channel_id=1, source_target_pairs={{0,1},{1,0},{2,3},{3,2},{4,5},{5,4},{6,7},{7,6},{8,9},{9,8},{10,11... | collective-permute-start | bytes 3145736 | tf_op jit(solution)/shard_map/ppermute | solution.py:183
  0.5 0.7 %broadcast_in_dim.8.gain_ref = bf16[1,8192]{1,0:T(2,128)(2,1)S(1)} reshape(bf16[8192]{0:T(1024)(128)(2,1)} %param.9) | data formatting | bytes 32768 | tf_op jit(solution)/shard_map/broadcast_in_dim | solution.py:192
  1.2 0.0 copy-start.3
  1.2 0.9 %copy-done.3 = bf16[16,8192]{1,0:T(8,128)(2,1)S(1)} copy-done((bf16[16,8192]{1,0:T(8,128)(2,1)S(1)}, bf16[16,8192]{1,0:T(8,128)(2,1)}, u32[]{:S(2)}) %copy-start.3) | copy-done | bytes 262168
  2.1 0.7 %copy-done.4 = s32[16,1]{0,1:T(1,128)S(1)} copy-done((s32[16,1]{0,1:T(1,128)S(1)}, s32[16,1]{0,1:T(1,128)}, u32[]{:S(2)}) %copy-start.4) | copy-done | bytes 88
  2.8 1.1 %prepare.1 = bf16[8,16,2048]{2,1,0:T(8,128)(2,1)} custom-call(s32[1,16]{1,0:T(1,128)S(1)} %bitcast.7, bf16[16,8192]{1,0:T(8,128)(2,1)S(1)} %copy-done.3, bf16[1,8192]{1,0:T(2,128)(2,1)S(1)} %broadcast_in_dim.8.gain_ref), custom_call_target="tpu_custom_call" | custom-call | tf_op jit(solution)/shard_map/prepare/pallas_call | solution.py:185
  3.9 6.8 %all-to-all-start = ((bf16[8,16,2048]{2,1,0:T(8,128)(2,1)}), bf16[8,16,2048]{2,1,0:T(8,128)(2,1)S(1)}, u32[]{:S(2)}, u32[]{:S(2)}) async-start(bf16[8,16,2048]{2,1,0:T(8,128)(2,1)} %prepare.1), calls=%async_computation | async-start | bytes 1048576 | tf_op jit(solution)/shard_map/all_to_all | solution.py:217
  10.7 0.7 %pad_maximum_fusion.own_groups = f32[16,512]{1,0:T(8,128)S(1)} fusion(f32[8,512]{1,0:T(8,128)} %bitcast.8, f32[8,512]{1,0:T(8,128)} %bitcast.9), kind=kLoop, calls=%fused_computation | loop fusion | flops 8192 | bytes 65536 | tf_op jit(solution)/shard_map/concatenate | solution.py:182
  11.5 0.2 collective-permute-start.1
  11.7 1.7 %constant_dynamic-slice_fusion.base = bf16[2048,512]{1,0:T(8,128)(2,1)S(1)} fusion(bf16[8192,512]{1,0:T(8,128)(2,1)} %param.10, s32[]{:T(128)S(6)} %select_n.3), kind=kLoop, calls=%fused_computation.7 | loop fusion | bytes 4194308 | tf_op jit(solution)/shard_map/dynamic_slice | solution.py:215
  13.5 0.0 collective-permute-done.1.other_groups
  13.5 0.0 collective-permute-done.other_codes
  13.5 0.0 copy-start.2
  13.5 1.2 %copy-done.2 = bf16[1,1,1024,512]{3,2,1,0:T(8,128)(2,1)S(1)} copy-done((bf16[1,1,1024,512]{3,2,1,0:T(8,128)(2,1)S(1)}, bf16[1,1,1024,512]{3,2,1,0:T(8,128)(2,1)}, u32[]{:S(2)}) %copy-start.2) | copy-done | bytes 1048600
  14.7 2.1 %weight.1.weight_ref = bf16[2048,512]{1,0:T(8,128)(2,1)S(1)} custom-call(s32[1]{0:T(128)} %bitcast.1.core_ref, bf16[1024,512]{1,0:T(8,128)(2,1)S(1)} %bitcast.6, bf16[1024,512]{1,0:T(8,128)(2,1)} %collective-permute-done.other_codes, f32[16,512]{1,0:T(8,128)S(1)} %pad_maximum_fusion.own_groups, f32[16,512]{1,0:T(8,128)S(1)} %collective-permute-done.1.other_groups, ...), custom_call_target="tpu_custom_call" | custom-call | flops 4194304 | bytes 6291456 | tf_op jit(solution)/shard_map/weight/pallas_call | solution.py:194
  16.9 1.3 %copy-done = bf16[2048,512]{1,0:T(8,128)(2,1)} copy-done((bf16[2048,512]{1,0:T(8,128)(2,1)}, bf16[2048,512]{1,0:T(8,128)(2,1)S(1)}, u32[]{:S(2)}) %copy-start) | copy-done | bytes 2097176
  18.2 7.7 %all-to-all-done.rows_ref = bf16[8,16,2048]{2,1,0:T(8,128)(2,1)S(1)} async-done(((bf16[8,16,2048]{2,1,0:T(8,128)(2,1)}), bf16[8,16,2048]{2,1,0:T(8,128)(2,1)S(1)}, u32[]{:S(2)}, u32[]{:S(2)}) %all-to-all-start) | async-done | bytes 524320 | tf_op jit(solution)/shard_map/all_to_all | solution.py:217
  25.9 1.6 %copy-done.1 = bf16[2048,512]{1,0:T(8,128)(2,1)S(1)} copy-done((bf16[2048,512]{1,0:T(8,128)(2,1)S(1)}, bf16[2048,512]{1,0:T(8,128)(2,1)}, u32[]{:S(2)}) %copy-start.1) | copy-done | bytes 2097176
  27.5 1.1 %product.1 = bf16[8,16,512]{2,1,0:T(8,128)(2,1)} custom-call(bf16[8,16,2048]{2,1,0:T(8,128)(2,1)S(1)} %all-to-all-done.rows_ref, bf16[2048,512]{1,0:T(8,128)(2,1)S(1)} %copy-done.1), custom_call_target="tpu_custom_call" | custom-call | tf_op jit(solution)/shard_map/product/pallas_call | solution.py:220
  28.6 3.6 %all-to-all-start.1 = ((bf16[8,16,512]{2,1,0:T(8,128)(2,1)}), bf16[8,16,512]{2,1,0:T(8,128)(2,1)S(1)}, u32[]{:S(2)}, u32[]{:S(2)}) async-start(bf16[8,16,512]{2,1,0:T(8,128)(2,1)} %product.1), calls=%async_computation.1 | async-start | bytes 262144 | tf_op jit(solution)/shard_map/all_to_all | solution.py:228
  32.2 0.1 fusion
  32.3 0.1 pad_maximum_fusion.1
  32.4 7.1 %all-to-all-done.1.parts_ref = bf16[8,16,512]{2,1,0:T(8,128)(2,1)S(1)} async-done(((bf16[8,16,512]{2,1,0:T(8,128)(2,1)}), bf16[8,16,512]{2,1,0:T(8,128)(2,1)S(1)}, u32[]{:S(2)}, u32[]{:S(2)}) %all-to-all-start.1) | async-done | bytes 131104 | tf_op jit(solution)/shard_map/all_to_all | solution.py:228
  39.6 0.7 %finish.1 = bf16[16,512]{1,0:T(8,128)(2,1)} custom-call(bf16[8,16,512]{2,1,0:T(8,128)(2,1)S(1)} %all-to-all-done.1.parts_ref, f32[16,128]{1,0:T(8,128)S(1)} %get-tuple-element.8.cosine_ref, f32[16,128]{1,0:T(8,128)S(1)} %get-tuple-element.9.sine_ref), custom_call_target="tpu_custom_call" | custom-call | tf_op jit(solution)/shard_map/finish/pallas_call | solution.py:232
  (7 shorter events, 0.0 us)
Async XLA Ops:
  0.0 13.5 %collective-permute-start = (bf16[1024,512]{1,0:T(8,128)(2,1)}, bf16[1024,512]{1,0:T(8,128)(2,1)}, u32[]{:S(2)}, u32[]{:S(2)}) collective-permute-start(bf16[1024,512]{1,0:T(8,128)(2,1)} %bitcast.5), channel_id=1, source_target_pairs={{0,1},{1,0},{2,3},{3,2},{4,5},{5,4},{6,7},{7,6},{8,9},{9,8},{10,11... | collective-permute-start | bytes 3145736 | tf_op jit(solution)/shard_map/ppermute | solution.py:183
  1.2 1.0 %copy-start.3 = (bf16[16,8192]{1,0:T(8,128)(2,1)S(1)}, bf16[16,8192]{1,0:T(8,128)(2,1)}, u32[]{:S(2)}) copy-start(bf16[16,8192]{1,0:T(8,128)(2,1)} %hidden_ref.1) | copy-start | bytes 786436
  2.1 0.7 %copy-start.4 = (s32[16,1]{0,1:T(1,128)S(1)}, s32[16,1]{0,1:T(1,128)}, u32[]{:S(2)}) copy-start(s32[16,1]{0,1:T(1,128)} %param.14) | copy-start | bytes 196
  3.9 22.0 %all-to-all-start = ((bf16[8,16,2048]{2,1,0:T(8,128)(2,1)}), bf16[8,16,2048]{2,1,0:T(8,128)(2,1)S(1)}, u32[]{:S(2)}, u32[]{:S(2)}) async-start(bf16[8,16,2048]{2,1,0:T(8,128)(2,1)} %prepare.1), calls=%async_computation | async-start | bytes 1048576 | tf_op jit(solution)/shard_map/all_to_all | solution.py:217
  11.5 2.0 %collective-permute-start.1 = (f32[16,512]{1,0:T(8,128)S(1)}, f32[16,512]{1,0:T(8,128)S(1)}, u32[]{:S(2)}, u32[]{:S(2)}) collective-permute-start(f32[16,512]{1,0:T(8,128)S(1)} %pad_maximum_fusion.own_groups), channel_id=1, source_target_pairs={{0,1},{1,0},{2,3},{3,2},{4,5},{5,4},{6,7},{7,6},{8,9},{9,8},{10,11... | collective-permute-start | bytes 98312 | tf_op jit(solution)/shard_map/ppermute | solution.py:184
  11.7 1.8 %copy-start.5 = (s32[16]{0:T(128)S(1)}, s32[16]{0:T(128)}, u32[]{:S(2)}) copy-start(s32[16]{0:T(128)} %param.15) | copy-start | bytes 196
  13.5 1.2 %copy-start.2 = (bf16[1,1,1024,512]{3,2,1,0:T(8,128)(2,1)S(1)}, bf16[1,1,1024,512]{3,2,1,0:T(8,128)(2,1)}, u32[]{:S(2)}) copy-start(bf16[1,1,1024,512]{3,2,1,0:T(8,128)(2,1)} %param.11) | copy-start | bytes 3145732
  16.9 1.3 %copy-start = (bf16[2048,512]{1,0:T(8,128)(2,1)}, bf16[2048,512]{1,0:T(8,128)(2,1)S(1)}, u32[]{:S(2)}) copy-start(bf16[2048,512]{1,0:T(8,128)(2,1)S(1)} %weight.1.weight_ref) | copy-start | bytes 6291460
  25.9 1.6 %copy-start.1 = (bf16[2048,512]{1,0:T(8,128)(2,1)S(1)}, bf16[2048,512]{1,0:T(8,128)(2,1)}, u32[]{:S(2)}) copy-start(bf16[2048,512]{1,0:T(8,128)(2,1)} %copy-done) | copy-start | bytes 6291460
  28.6 11.0 %all-to-all-start.1 = ((bf16[8,16,512]{2,1,0:T(8,128)(2,1)}), bf16[8,16,512]{2,1,0:T(8,128)(2,1)S(1)}, u32[]{:S(2)}, u32[]{:S(2)}) async-start(bf16[8,16,512]{2,1,0:T(8,128)(2,1)} %product.1), calls=%async_computation.1 | async-start | bytes 262144 | tf_op jit(solution)/shard_map/all_to_all | solution.py:228

commit v2 on v1

--- a/solution.py
+++ b/solution.py
@@ -95,31 +95,23 @@
     return rotate_keys(combined, positions)
 
 
-def prepare_kernel(pieces, ids_ref, hidden_ref, gain_ref, out_ref):
-    floats = hidden_ref[...].astype(jnp.float32)
-    row_count, width = floats.shape
-    mean_square = jnp.sum(floats * floats, axis=1, keepdims=True) / width
-    normed = floats * lax.rsqrt(mean_square + epsilon) * gain_ref[...].astype(jnp.float32)
-    square = (row_count, row_count)
-    diagonal = lax.broadcasted_iota(jnp.int32, square, 0) == lax.broadcasted_iota(jnp.int32, square, 1)
-    ids = jnp.sum(jnp.where(diagonal, ids_ref[...], 0), axis=1, keepdims=True)
-    piece_width = width // pieces
-    for variant in range(out_ref.shape[0] // pieces):
-        kept = jnp.where(ids == variant, normed, 0.0).astype(jnp.bfloat16)
-        for piece in range(pieces):
-            out_ref[variant * pieces + piece] = kept[:, piece * piece_width : (piece + 1) * piece_width]
+def norm_kernel(rows_ref, gain_ref, out_ref, gains_ref):
+    gains_ref[...] = gain_ref[...].astype(jnp.float32).reshape(gains_ref.shape)
+    out_ref[...] = norm_rows(rows_ref[...], gains_ref[...])
 
 
 def weight_kernel(
-    core_ref, own_codes, other_codes, own_groups, other_groups, base, out_ref, codes, groups, arrived
+    core_ref, first_ref, own_codes, other_codes, own_groups, other_groups, base_ref, out_ref, codes, groups, base, arrived
 ):
     slice_rows = codes.shape[1]
     core = core_ref[0]
+    start = pl.multiple_of(first_ref[0] * slice_rows, slice_rows)
     copies = [
         pltpu.make_async_copy(own_groups, groups.at[core], arrived.at[0]),
         pltpu.make_async_copy(other_groups, groups.at[1 - core], arrived.at[1]),
         pltpu.make_async_copy(own_codes, codes.at[core], arrived.at[2]),
-        pltpu.make_async_copy(other_codes, codes.at[1 - core], arrived.at[3]),
+        pltpu.make_async_copy(base_ref.at[pl.ds(start, 2 * slice_rows)], base, arrived.at[3]),
+        pltpu.make_async_copy(other_codes, codes.at[1 - core], arrived.at[4]),
     ]
     for copy in copies:
         copy.start()
@@ -137,16 +129,46 @@
             out_ref[rows] = (base[rows].astype(jnp.float32) + delta).astype(jnp.bfloat16)
 
 
+def norm_rows(rows, gain):
+    floats = rows.astype(jnp.float32)
+    mean_square = jnp.sum(floats * floats, axis=1, keepdims=True) / rows.shape[1]
+    return (floats * lax.rsqrt(mean_square + epsilon) * gain).astype(jnp.bfloat16)
+
+
+def pieces_kernel(first_ref, core_ref, own_ref, other_ref, gain_ref, *rest):
+    outs, normed_ref = rest[:-1], rest[-1]
+    row_count = own_ref.shape[0]
+    core = core_ref[0]
+    normed_ref[pl.ds(pl.multiple_of(core * row_count, row_count), row_count)] = own_ref[...]
+    other_rows = pl.ds(pl.multiple_of((1 - core) * row_count, row_count), row_count)
+    normed_ref[other_rows] = norm_rows(other_ref[...], gain_ref[...])
+    for index, out_ref in enumerate(outs):
+        piece_width = out_ref.shape[1]
+        start = pl.multiple_of((first_ref[0] ^ index) * piece_width, piece_width)
+        out_ref[...] = normed_ref[:, pl.ds(start, piece_width)]
+
+
 def product_kernel(rows_ref, weight_ref, out_ref):
-    count, size, width = rows_ref.shape
-    rows = rows_ref[...].reshape(count * size, width)
-    total = jnp.dot(rows, weight_ref[...], preferred_element_type=jnp.float32)
-    out_ref[...] = total.reshape(out_ref.shape).astype(out_ref.dtype)
-
-
-def finish_kernel(parts_ref, cosine_ref, sine_ref, out_ref):
-    total = jnp.sum(parts_ref[...].astype(jnp.float32), axis=0)
-    for head in range(total.shape[1] // HEAD):
+    out_ref[...] = jnp.dot(rows_ref[...], weight_ref[...], preferred_element_type=jnp.float32).astype(out_ref.dtype)
+
+
+def sum_kernel(core_ref, far_a, far_b, near_a, near_b, kept_ref, sent_ref, total_ref):
+    total_ref[0] = far_a[...].astype(jnp.float32) + far_b[...].astype(jnp.float32)
+    total_ref[1] = near_a[...].astype(jnp.float32) + near_b[...].astype(jnp.float32)
+    row_count = kept_ref.shape[1]
+    core = core_ref[0]
+    kept_ref[...] = total_ref[:, pl.ds(pl.multiple_of(core * row_count, row_count), row_count)]
+    sent_ref[...] = total_ref[:, pl.ds(pl.multiple_of((1 - core) * row_count, row_count), row_count)]
+
+
+def finish_kernel(variant_ref, ids_ref, kept_ref, received_ref, cosine_ref, sine_ref, out_ref):
+    row_count, column_count = out_ref.shape
+    square = (row_count, row_count)
+    diagonal = lax.broadcasted_iota(jnp.int32, square, 0) == lax.broadcasted_iota(jnp.int32, square, 1)
+    ids = jnp.sum(jnp.where(diagonal, ids_ref[...], 0), axis=1, keepdims=True)
+    near = ids == variant_ref[0]
+    total = jnp.where(near, kept_ref[1] + received_ref[1], kept_ref[0] + received_ref[0])
+    for head in range(column_count // HEAD):
         columns = slice(head * HEAD, (head + 1) * HEAD)
         block = total[:, columns]
         swapped = pltpu.roll(block, HEAD // 2, 1)
@@ -163,7 +185,7 @@
 
 VMEM = pl.BlockSpec(memory_space=pltpu.VMEM)
 SMEM = pl.BlockSpec(memory_space=pltpu.SMEM)
-HBM = pl.BlockSpec(memory_space=pltpu.HBM)
+ANY = pl.BlockSpec(memory_space=pl.ANY)
 
 
 def paired(
@@ -171,72 +193,90 @@
 ):
     row_count, width = hidden.shape
     device_count = lax.axis_size("variant")
-    variant_count = device_count // OWNERS
     pieces = OWNERS // 2
     slice_rows, column_count = delta_codes.shape[2:]
     place = lax.axis_index("variant")
-    parity = [list(range(first, device_count, 2)) for first in range(2)]
+    core = lax.rem(place, 2)
+    piece = lax.div(lax.rem(place, OWNERS), 2)
+    variant = lax.div(place, OWNERS)
     swap = [(index, index ^ 1) for index in range(device_count)]
-
+    far = pieces
+    steps = [(0, far, far + 2), (1, far + 1, far + 3), (1, 1, 3), (0, 0, 2)]
+    routes = [
+        [(index, index ^ (2 * distances[index % 2])) for index in range(device_count)] for _, *distances in steps
+    ]
+
+    slice_shape = (slice_rows, column_count)
     own_codes = delta_codes[0, 0]
     own_groups = jnp.concatenate([delta_scales[0, 0], delta_zeros[0, 0]], axis=0)
-    other_codes = lax.ppermute(own_codes, "variant", swap)
+    other_hidden = lax.ppermute(hidden, "variant", swap)
     other_groups = lax.ppermute(own_groups, "variant", swap)
-    outgoing = pl.pallas_call(
-        functools.partial(prepare_kernel, pieces),
-        out_shape=jax.ShapeDtypeStruct((variant_count * pieces, row_count, width // pieces), jnp.bfloat16),
-        in_specs=[VMEM] * 3,
-        out_specs=VMEM,
+    normed, gains = pl.pallas_call(
+        norm_kernel,
+        out_shape=[jax.ShapeDtypeStruct((row_count, width), jnp.bfloat16), jax.ShapeDtypeStruct((1, width), jnp.float32)],
+        in_specs=[VMEM] * 2,
+        out_specs=[VMEM] * 2,
         compiler_params=pltpu.CompilerParams(vmem_limit_bytes=16 << 20),
-        name="prepare",
-    )(variant_ids.T, hidden, norm_gain[None, :])
-    both_rows = 2 * slice_rows
+        name="norm",
+    )(hidden, norm_gain)
+    other_hidden, other_groups, codes, normed = lax.optimization_barrier(
+        (other_hidden, other_groups, own_codes, normed)
+    )
+    other_codes = lax.ppermute(codes, "variant", swap)
+    first, second = pl.pallas_call(
+        pieces_kernel,
+        out_shape=[jax.ShapeDtypeStruct((2 * row_count, width // pieces), jnp.bfloat16)] * 2,
+        in_specs=[SMEM, SMEM, VMEM, VMEM, VMEM],
+        out_specs=[VMEM] * 2,
+        scratch_shapes=[pltpu.VMEM((2 * row_count, width), jnp.bfloat16)],
+        compiler_params=pltpu.CompilerParams(vmem_limit_bytes=16 << 20),
+        name="pieces",
+    )((piece ^ (2 * core))[None], core[None], normed, other_hidden, gains)
     weight = pl.pallas_call(
         weight_kernel,
-        out_shape=jax.ShapeDtypeStruct((both_rows, column_count), jnp.bfloat16),
-        in_specs=[SMEM] + [pl.BlockSpec(memory_space=pl.ANY)] * 4 + [VMEM],
+        out_shape=jax.ShapeDtypeStruct((2 * slice_rows, column_count), jnp.bfloat16),
+        in_specs=[SMEM, SMEM] + [ANY] * 5,
         out_specs=VMEM,
         scratch_shapes=[
-            pltpu.VMEM((2, slice_rows, column_count), jnp.bfloat16),
+            pltpu.VMEM((2,) + slice_shape, jnp.bfloat16),
             pltpu.VMEM((2,) + own_groups.shape, jnp.float32),
-            pltpu.SemaphoreType.DMA((4,)),
+            pltpu.VMEM((2 * slice_rows, column_count), jnp.bfloat16),
+            pltpu.SemaphoreType.DMA((5,)),
         ],
-        compiler_params=pltpu.CompilerParams(vmem_limit_bytes=16 << 20),
-        cost_estimate=pl.CostEstimate(
-            flops=4 * both_rows * column_count, bytes_accessed=6 * both_rows * column_count, transcendentals=0
-        ),
+        compiler_params=pltpu.CompilerParams(vmem_limit_bytes=48 << 20),
         name="weight",
-    )(
-        lax.rem(place, 2)[None],
-        own_codes,
-        other_codes,
-        own_groups,
-        other_groups,
-        lax.dynamic_slice_in_dim(base_weight, lax.div(lax.rem(place, OWNERS), 2) * both_rows, both_rows, 0),
-    )
-    incoming = lax.all_to_all(
-        outgoing, "variant", split_axis=0, concat_axis=0, tiled=True, axis_index_groups=parity
-    )
-    products = pl.pallas_call(
-        product_kernel,
-        out_shape=jax.ShapeDtypeStruct((device_count // 2, row_count, column_count), jnp.bfloat16),
-        in_specs=[VMEM, VMEM],
-        out_specs=VMEM,
-        compiler_params=pltpu.CompilerParams(vmem_limit_bytes=16 << 20),
-        name="product",
-    )(incoming, weight)
-    returned = lax.all_to_all(
-        products, "variant", split_axis=0, concat_axis=0, tiled=True, axis_index_groups=parity
-    )
+    )(core[None], (piece * 2)[None], own_codes, other_codes, own_groups, other_groups, base_weight)
+    incoming = [lax.ppermute((first, second)[index], "variant", route) for (index, _, _), route in zip(steps, routes)]
+    parts = [None] * len(steps)
+    for step in (2, 3, 0, 1):
+        product = pl.pallas_call(
+            product_kernel,
+            out_shape=jax.ShapeDtypeStruct((2 * row_count, column_count), jnp.bfloat16),
+            in_specs=[VMEM, VMEM],
+            out_specs=VMEM,
+            compiler_params=pltpu.CompilerParams(vmem_limit_bytes=16 << 20),
+            name="product",
+        )(incoming[step], weight)
+        parts[step] = lax.ppermute(product, "variant", routes[step])
+    kept, sent = pl.pallas_call(
+        sum_kernel,
+        out_shape=[jax.ShapeDtypeStruct((2, row_count, column_count), jnp.float32)] * 2,
+        in_specs=[SMEM] + [VMEM] * len(parts),
+        out_specs=[VMEM] * 2,
+        scratch_shapes=[pltpu.VMEM((2, 2 * row_count, column_count), jnp.float32)],
+        compiler_params=pltpu.CompilerParams(vmem_limit_bytes=8 << 20),
+        name="sum",
+    )(core[None], *parts)
+    received = lax.ppermute(sent, "variant", swap)
     cosine, sine = turn_factors(positions)
     return pl.pallas_call(
         finish_kernel,
         out_shape=jax.ShapeDtypeStruct((row_count, column_count), jnp.bfloat16),
-        in_specs=[VMEM] * 3,
+        in_specs=[SMEM] + [VMEM] * 5,
         out_specs=VMEM,
         compiler_params=pltpu.CompilerParams(vmem_limit_bytes=8 << 20),
         name="finish",
-    )(returned, cosine, sine)
+    )(variant[None], variant_ids.T, kept, received, cosine, sine)
 
 
 def solution(mesh):

time: 40.8 us -> 30.7 us (0.75)
  local copies, waits for them, and re-layouts: 8.21 us -> 2.89 us
  waiting for transfers between devices: 14.9 us -> 10.9 us
  starting transfers between devices: 11.1 us -> 9.13 us
  other arithmetic: 0.95 us -> 1.6 us
  Pallas kernels: 5.04 us -> 5.58 us
    all_to_all x2 -> x0, waiting for transfers between devices: 14.8 us -> none  [the longest x1 7.7 us: paired(): lax.all_to_all(outgoing, 'variant', split_axis=0, concat_axis=0, tiled=Tr...]
    ppermute x1 -> x11, waiting for transfers between devices: 0.01 us -> 10.9 us  [the longest x4 6.56 us: paired(): lax.ppermute((first, second)[index], 'variant', route)]
    all_to_all x2 -> x0, starting transfers between devices: 10.4 us -> none  [the longest x1 6.8 us: paired(): lax.all_to_all(outgoing, 'variant', split_axis=0, concat_axis=0, tiled=Tr...]
    ppermute x1 -> x11, starting transfers between devices: 0.45 us -> 9.07 us  [the longest x4 5.88 us: paired(): lax.ppermute((first, second)[index], 'variant', route)]
    unnamed x12 -> x8, local copies, waits for them, and re-layouts: 5.73 us -> 2.89 us
    dynamic_slice x1 -> x0, local copies, waits for them, and re-layouts: 1.74 us -> none  [paired(): lax.dynamic_slice_in_dim(base_weight, lax.div(lax.rem(place, OWNERS), 2)...]
    broadcast_in_dim x1 -> x0, local copies, waits for them, and re-layouts: 0.74 us -> none  [paired(): norm_gain[None, :]]
    convert_element_type x1, other arithmetic: 0.01 us -> 0.66 us  [turn_factors(): angles = position.astype(jnp.float32)[:, None] * frequency[None, :]]
  transfers between devices with their start and end apart: 4 -> 12, of which waited for: 2 -> 5; matrix products, arithmetic and copies ran while one was open for 8% -> 5% of each run, Pallas kernels for 8% -> 16%
where the time goes in v2:
time: 30.7 us; the launch traced here: 30.2 us
  waiting for transfers between devices  10.9 us (36%)
  starting transfers between devices  9.13 us (30%)
  Pallas kernels  5.58 us (18%)
  local copies, waits for them, and re-layouts  2.89 us (9%)
  other arithmetic  1.6 us (5%)
    ppermute x4, waiting for transfers between devices, paired(): lax.ppermute((first, second)[index], 'variant', route)  6.56 us
    ppermute x4, starting transfers between devices, paired(): lax.ppermute((first, second)[index], 'variant', route)  5.88 us
    ppermute x4, waiting for transfers between devices, paired(): parts[step] = lax.ppermute(product, 'variant', routes[step])  3.41 us
    unnamed x8, local copies, waits for them, and re-layouts  2.89 us
    pallas_call x1, Pallas kernels, paired(): pl.pallas_call(weight_kernel, out_shape=jax.ShapeDtypeStruct((2 * slice_r...  2.51 us
    ppermute x4, starting transfers between devices, paired(): parts[step] = lax.ppermute(product, 'variant', routes[step])  1.88 us
    pallas_call x4, Pallas kernels, paired(): pl.pallas_call(product_kernel, out_shape=jax.ShapeDtypeStruct((2 * row_co...  1.79 us
    ppermute x1, waiting for transfers between devices, paired(): received = lax.ppermute(sent, 'variant', swap)  0.9 us
  transfers between devices with their start and end apart: 12, of which 5 were waited for; matrix products, arithmetic and copies ran while one was open for 5% of the time, Pallas kernels for 16%

profile of v2, /device:TPU:0, one launch (start us, length us, event | category | flops | bytes accessed | tf_op | source)
XLA Modules:
  0.0 30.2 jit_solution(6446843434596152850)
XLA Ops:
  0.0 0.5 %collective-permute-start = (bf16[16,8192]{1,0:T(8,128)(2,1)}, bf16[16,8192]{1,0:T(8,128)(2,1)S(1)}, u32[]{:S(2)}, u32[]{:S(2)}) collective-permute-start(bf16[16,8192]{1,0:T(8,128)(2,1)} %rows_ref.1), channel_id=1, source_target_pairs={{0,1},{1,0},{2,3},{3,2},{4,5},{5,4},{6,7},{7,6},{8,9},{9,8},{10,11... | collective-permute-start | bytes 786440 | tf_op jit(solution)/shard_map/ppermute | solution.py:212
  0.5 0.7 %pad_maximum_fusion.own_groups = f32[16,512]{1,0:T(8,128)S(1)} fusion(f32[8,512]{1,0:T(8,128)} %bitcast.11, f32[8,512]{1,0:T(8,128)} %bitcast.12), kind=kLoop, calls=%fused_computation | loop fusion | flops 8192 | bytes 65536 | tf_op jit(solution)/shard_map/concatenate | solution.py:211
  1.3 0.9 %copy-done.1 = bf16[16,8192]{1,0:T(8,128)(2,1)S(1)} copy-done((bf16[16,8192]{1,0:T(8,128)(2,1)S(1)}, bf16[16,8192]{1,0:T(8,128)(2,1)}, u32[]{:S(2)}) %copy-start.1) | copy-done | bytes 262168
  2.2 0.7 %copy-done.2 = bf16[8192]{0:T(1024)(128)(2,1)S(1)} copy-done((bf16[8192]{0:T(1024)(128)(2,1)S(1)}, bf16[8192]{0:T(1024)(128)(2,1)}, u32[]{:S(2)}) %copy-start.2) | copy-done | bytes 16408
  3.2 0.5 %collective-permute-start.3 = (bf16[1024,512]{1,0:T(8,128)(2,1)}, bf16[1024,512]{1,0:T(8,128)(2,1)S(1)}, u32[]{:S(2)}, u32[]{:S(2)}) collective-permute-start(bf16[1024,512]{1,0:T(8,128)(2,1)} %bitcast.8), channel_id=1, source_target_pairs={{0,1},{1,0},{2,3},{3,2},{4,5},{5,4},{6,7},{7,6},{8,9},{9,8},{10,11... | collective-permute-start | bytes 3145736 | tf_op jit(solution)/shard_map/ppermute | solution.py:225
  3.9 3.7 %collective-permute-start.2 = (bf16[32,2048]{1,0:T(8,128)(2,1)S(1)}, bf16[32,2048]{1,0:T(8,128)(2,1)S(1)}, u32[]{:S(2)}, u32[]{:S(2)}) collective-permute-start(bf16[32,2048]{1,0:T(8,128)(2,1)S(1)} %get-tuple-element.19), channel_id=1, source_target_pairs={{0,8},{1,13},{2,10},{3,15},{4,12},{5,9},{6,14},{7,11},{8,0},{9,5},... | collective-permute-start | bytes 393224 | tf_op jit(solution)/shard_map/ppermute | solution.py:249
  7.6 1.3 %collective-permute-start.5 = (bf16[32,2048]{1,0:T(8,128)(2,1)S(1)}, bf16[32,2048]{1,0:T(8,128)(2,1)S(1)}, u32[]{:S(2)}, u32[]{:S(2)}) collective-permute-start(bf16[32,2048]{1,0:T(8,128)(2,1)S(1)} %get-tuple-element.22), channel_id=1, source_target_pairs={{0,10},{1,15},{2,8},{3,13},{4,14},{5,11},{6,12},{7,9},{8,2},{9,7},... | collective-permute-start | bytes 393224 | tf_op jit(solution)/shard_map/ppermute | solution.py:249
  9.2 0.7 %collective-permute-start.9 = (bf16[32,2048]{1,0:T(8,128)(2,1)S(1)}, bf16[32,2048]{1,0:T(8,128)(2,1)S(1)}, u32[]{:S(2)}, u32[]{:S(2)}) collective-permute-start(bf16[32,2048]{1,0:T(8,128)(2,1)S(1)} %get-tuple-element.19), channel_id=1, source_target_pairs={{0,0},{1,5},{2,2},{3,7},{4,4},{5,1},{6,6},{7,3},{8,8},{9,13},{10,1... | collective-permute-start | bytes 393224 | tf_op jit(solution)/shard_map/ppermute | solution.py:249
  9.8 0.7 %convert_element_type.3 = f32[16]{0:T(128)S(1)} convert(s32[16]{0:T(128)} %param.15) | non-fusion elementwise | flops 16 | bytes 128 | tf_op jit(solution)/shard_map/convert_element_type | solution.py:181
  10.5 1.2 %copy-done = bf16[1,1,1024,512]{3,2,1,0:T(8,128)(2,1)S(1)} copy-done((bf16[1,1,1024,512]{3,2,1,0:T(8,128)(2,1)S(1)}, bf16[1,1,1024,512]{3,2,1,0:T(8,128)(2,1)}, u32[]{:S(2)}) %copy-start) | copy-done | bytes 1048600
  11.7 2.5 %weight.1.weight_ref = bf16[2048,512]{1,0:T(8,128)(2,1)S(1)} custom-call(s32[1]{0:T(128)} %bitcast.2.core_ref, s32[1]{0:T(128)} %bitcast.7.first_ref, bf16[1024,512]{1,0:T(8,128)(2,1)S(1)} %bitcast.9, bf16[1024,512]{1,0:T(8,128)(2,1)S(1)} %collective-permute-done.3.other_codes, f32[16,512]{1,0:T(8,128)S(1)} %pad_maximum_fusion.own_groups, ...), custom_call_target="tpu_custom_call" | custom-call | tf_op jit(solution)/shard_map/weight/pallas_call | solution.py:235
  14.3 3.3 %collective-permute-done.2.rows_ref = bf16[32,2048]{1,0:T(8,128)(2,1)S(1)} collective-permute-done((bf16[32,2048]{1,0:T(8,128)(2,1)S(1)}, bf16[32,2048]{1,0:T(8,128)(2,1)S(1)}, u32[]{:S(2)}, u32[]{:S(2)}) %collective-permute-start.2) | collective-permute-done | bytes 131104 | tf_op jit(solution)/shard_map/ppermute | solution.py:249
  17.6 0.4 %product.4 = bf16[32,512]{1,0:T(8,128)(2,1)S(1)} custom-call(bf16[32,2048]{1,0:T(8,128)(2,1)S(1)} %collective-permute-done.2.rows_ref, bf16[2048,512]{1,0:T(8,128)(2,1)S(1)} %weight.1.weight_ref), custom_call_target="tpu_custom_call" | custom-call | tf_op jit(solution)/shard_map/product/pallas_call | solution.py:252
  18.1 3.2 %collective-permute-done.5.rows_ref = bf16[32,2048]{1,0:T(8,128)(2,1)S(1)} collective-permute-done((bf16[32,2048]{1,0:T(8,128)(2,1)S(1)}, bf16[32,2048]{1,0:T(8,128)(2,1)S(1)}, u32[]{:S(2)}, u32[]{:S(2)}) %collective-permute-start.5) | collective-permute-done | bytes 131104 | tf_op jit(solution)/shard_map/ppermute | solution.py:249
  21.3 0.4 %product.5 = bf16[32,512]{1,0:T(8,128)(2,1)S(1)} custom-call(bf16[32,2048]{1,0:T(8,128)(2,1)S(1)} %collective-permute-done.5.rows_ref, bf16[2048,512]{1,0:T(8,128)(2,1)S(1)} %weight.1.weight_ref), custom_call_target="tpu_custom_call" | custom-call | tf_op jit(solution)/shard_map/product/pallas_call | solution.py:252
  21.7 0.9 %collective-permute-start.6 = (bf16[32,512]{1,0:T(8,128)(2,1)S(1)}, bf16[32,512]{1,0:T(8,128)(2,1)S(1)}, u32[]{:S(2)}, u32[]{:S(2)}) collective-permute-start(bf16[32,512]{1,0:T(8,128)(2,1)S(1)} %product.5), channel_id=1, source_target_pairs={{0,10},{1,15},{2,8},{3,13},{4,14},{5,11},{6,12},{7,9},{8,2},{9,7},... | collective-permute-start | bytes 98312 | tf_op jit(solution)/shard_map/ppermute | solution.py:260
  22.6 0.4 %product.6 = bf16[32,512]{1,0:T(8,128)(2,1)S(1)} custom-call(bf16[32,2048]{1,0:T(8,128)(2,1)S(1)} %collective-permute-done.7.rows_ref, bf16[2048,512]{1,0:T(8,128)(2,1)S(1)} %weight.1.weight_ref), custom_call_target="tpu_custom_call" | custom-call | tf_op jit(solution)/shard_map/product/pallas_call | solution.py:252
  23.1 0.3 %collective-permute-start.8 = (bf16[32,512]{1,0:T(8,128)(2,1)S(1)}, bf16[32,512]{1,0:T(8,128)(2,1)S(1)}, u32[]{:S(2)}, u32[]{:S(2)}) collective-permute-start(bf16[32,512]{1,0:T(8,128)(2,1)S(1)} %product.6), channel_id=1, source_target_pairs={{0,2},{1,7},{2,0},{3,5},{4,6},{5,3},{6,4},{7,1},{8,10},{9,15},{10,... | collective-permute-start | bytes 98312 | tf_op jit(solution)/shard_map/ppermute | solution.py:260
  23.4 0.4 %product.7 = bf16[32,512]{1,0:T(8,128)(2,1)S(1)} custom-call(bf16[32,2048]{1,0:T(8,128)(2,1)S(1)} %collective-permute-done.9.rows_ref, bf16[2048,512]{1,0:T(8,128)(2,1)S(1)} %weight.1.weight_ref), custom_call_target="tpu_custom_call" | custom-call | tf_op jit(solution)/shard_map/product/pallas_call | solution.py:252
  23.9 0.7 %collective-permute-start.10 = (bf16[32,512]{1,0:T(8,128)(2,1)S(1)}, bf16[32,512]{1,0:T(8,128)(2,1)S(1)}, u32[]{:S(2)}, u32[]{:S(2)}) collective-permute-start(bf16[32,512]{1,0:T(8,128)(2,1)S(1)} %product.7), channel_id=1, source_target_pairs={{0,0},{1,5},{2,2},{3,7},{4,4},{5,1},{6,6},{7,3},{8,8},{9,13},{10,1... | collective-permute-start | bytes 98312 | tf_op jit(solution)/shard_map/ppermute | solution.py:260
  24.7 3.2 %collective-permute-done.6.far_b = bf16[32,512]{1,0:T(8,128)(2,1)S(1)} collective-permute-done((bf16[32,512]{1,0:T(8,128)(2,1)S(1)}, bf16[32,512]{1,0:T(8,128)(2,1)S(1)}, u32[]{:S(2)}, u32[]{:S(2)}) %collective-permute-start.6) | collective-permute-done | bytes 32800 | tf_op jit(solution)/shard_map/ppermute | solution.py:260
  28.1 0.3 %collective-permute-start.11 = (f32[2,16,512]{2,1,0:T(8,128)S(1)}, f32[2,16,512]{2,1,0:T(8,128)S(1)}, u32[]{:S(2)}, u32[]{:S(2)}) collective-permute-start(f32[2,16,512]{2,1,0:T(8,128)S(1)} %get-tuple-element.24), channel_id=1, source_target_pairs={{0,1},{1,0},{2,3},{3,2},{4,5},{5,4},{6,7},{7,6},{8,9},{9,8},{10,11... | collective-permute-start | bytes 196616 | tf_op jit(solution)/shard_map/ppermute | solution.py:270
  28.5 0.9 %collective-permute-done.11.received_ref = f32[2,16,512]{2,1,0:T(8,128)S(1)} collective-permute-done((f32[2,16,512]{2,1,0:T(8,128)S(1)}, f32[2,16,512]{2,1,0:T(8,128)S(1)}, u32[]{:S(2)}, u32[]{:S(2)}) %collective-permute-start.11) | collective-permute-done | bytes 65568 | tf_op jit(solution)/shard_map/ppermute | solution.py:270
  29.4 0.8 %finish.1 = bf16[16,512]{1,0:T(8,128)(2,1)} custom-call(s32[1]{0:T(128)} %bitcast.variant_ref, s32[1,16]{1,0:T(1,128)S(1)} %bitcast.10, f32[2,16,512]{2,1,0:T(8,128)S(1)} %get-tuple-element.23.kept_ref, f32[2,16,512]{2,1,0:T(8,128)S(1)} %collective-permute-done.11.received_ref, f32[16,128]{1,0:T(8,128)S(1)} %get-tuple-element.28.cosine_ref, ...), custom_call_target="tpu_custom_call" | custom-call | tf_op jit(solution)/shard_map/finish/pallas_call | solution.py:272
  (22 shorter events, 1.3 us)
Async XLA Ops:
  0.0 3.2 %collective-permute-start = (bf16[16,8192]{1,0:T(8,128)(2,1)}, bf16[16,8192]{1,0:T(8,128)(2,1)S(1)}, u32[]{:S(2)}, u32[]{:S(2)}) collective-permute-start(bf16[16,8192]{1,0:T(8,128)(2,1)} %rows_ref.1), channel_id=1, source_target_pairs={{0,1},{1,0},{2,3},{3,2},{4,5},{5,4},{6,7},{7,6},{8,9},{9,8},{10,11... | collective-permute-start | bytes 786440 | tf_op jit(solution)/shard_map/ppermute | solution.py:212
  1.2 2.0 %collective-permute-start.1 = (f32[16,512]{1,0:T(8,128)S(1)}, f32[16,512]{1,0:T(8,128)S(1)}, u32[]{:S(2)}, u32[]{:S(2)}) collective-permute-start(f32[16,512]{1,0:T(8,128)S(1)} %pad_maximum_fusion.own_groups), channel_id=1, source_target_pairs={{0,1},{1,0},{2,3},{3,2},{4,5},{5,4},{6,7},{7,6},{8,9},{9,8},{10,11... | collective-permute-start | bytes 98312 | tf_op jit(solution)/shard_map/ppermute | solution.py:213
  1.2 0.9 %copy-start.1 = (bf16[16,8192]{1,0:T(8,128)(2,1)S(1)}, bf16[16,8192]{1,0:T(8,128)(2,1)}, u32[]{:S(2)}) copy-start(bf16[16,8192]{1,0:T(8,128)(2,1)} %rows_ref.1) | copy-start | bytes 786436
  2.2 0.7 %copy-start.2 = (bf16[8192]{0:T(1024)(128)(2,1)S(1)}, bf16[8192]{0:T(1024)(128)(2,1)}, u32[]{:S(2)}) copy-start(bf16[8192]{0:T(1024)(128)(2,1)} %gain_ref.1) | copy-start | bytes 49156
  3.2 7.3 %collective-permute-start.3 = (bf16[1024,512]{1,0:T(8,128)(2,1)}, bf16[1024,512]{1,0:T(8,128)(2,1)S(1)}, u32[]{:S(2)}, u32[]{:S(2)}) collective-permute-start(bf16[1024,512]{1,0:T(8,128)(2,1)} %bitcast.8), channel_id=1, source_target_pairs={{0,1},{1,0},{2,3},{3,2},{4,5},{5,4},{6,7},{7,6},{8,9},{9,8},{10,11... | collective-permute-start | bytes 3145736 | tf_op jit(solution)/shard_map/ppermute | solution.py:225
  3.9 13.7 %collective-permute-start.2 = (bf16[32,2048]{1,0:T(8,128)(2,1)S(1)}, bf16[32,2048]{1,0:T(8,128)(2,1)S(1)}, u32[]{:S(2)}, u32[]{:S(2)}) collective-permute-start(bf16[32,2048]{1,0:T(8,128)(2,1)S(1)} %get-tuple-element.19), channel_id=1, source_target_pairs={{0,8},{1,13},{2,10},{3,15},{4,12},{5,9},{6,14},{7,11},{8,0},{9,5},... | collective-permute-start | bytes 393224 | tf_op jit(solution)/shard_map/ppermute | solution.py:249
  7.6 13.7 %collective-permute-start.5 = (bf16[32,2048]{1,0:T(8,128)(2,1)S(1)}, bf16[32,2048]{1,0:T(8,128)(2,1)S(1)}, u32[]{:S(2)}, u32[]{:S(2)}) collective-permute-start(bf16[32,2048]{1,0:T(8,128)(2,1)S(1)} %get-tuple-element.22), channel_id=1, source_target_pairs={{0,10},{1,15},{2,8},{3,13},{4,14},{5,11},{6,12},{7,9},{8,2},{9,7},... | collective-permute-start | bytes 393224 | tf_op jit(solution)/shard_map/ppermute | solution.py:249
  8.9 13.7 %collective-permute-start.7 = (bf16[32,2048]{1,0:T(8,128)(2,1)S(1)}, bf16[32,2048]{1,0:T(8,128)(2,1)S(1)}, u32[]{:S(2)}, u32[]{:S(2)}) collective-permute-start(bf16[32,2048]{1,0:T(8,128)(2,1)S(1)} %get-tuple-element.22), channel_id=1, source_target_pairs={{0,2},{1,7},{2,0},{3,5},{4,6},{5,3},{6,4},{7,1},{8,10},{9,15},{10,... | collective-permute-start | bytes 393224 | tf_op jit(solution)/shard_map/ppermute | solution.py:249
  9.2 14.2 %collective-permute-start.9 = (bf16[32,2048]{1,0:T(8,128)(2,1)S(1)}, bf16[32,2048]{1,0:T(8,128)(2,1)S(1)}, u32[]{:S(2)}, u32[]{:S(2)}) collective-permute-start(bf16[32,2048]{1,0:T(8,128)(2,1)S(1)} %get-tuple-element.19), channel_id=1, source_target_pairs={{0,0},{1,5},{2,2},{3,7},{4,4},{5,1},{6,6},{7,3},{8,8},{9,13},{10,1... | collective-permute-start | bytes 393224 | tf_op jit(solution)/shard_map/ppermute | solution.py:249
  10.5 1.2 %copy-start = (bf16[1,1,1024,512]{3,2,1,0:T(8,128)(2,1)S(1)}, bf16[1,1,1024,512]{3,2,1,0:T(8,128)(2,1)}, u32[]{:S(2)}) copy-start(bf16[1,1,1024,512]{3,2,1,0:T(8,128)(2,1)} %param.11) | copy-start | bytes 3145732
  11.7 17.7 %copy-start.3 = (s32[16,1]{0,1:T(1,128)S(1)}, s32[16,1]{0,1:T(1,128)}, u32[]{:S(2)}) copy-start(s32[16,1]{0,1:T(1,128)} %param.14) | copy-start | bytes 196
  18.0 6.6 %collective-permute-start.4 = (bf16[32,512]{1,0:T(8,128)(2,1)S(1)}, bf16[32,512]{1,0:T(8,128)(2,1)S(1)}, u32[]{:S(2)}, u32[]{:S(2)}) collective-permute-start(bf16[32,512]{1,0:T(8,128)(2,1)S(1)} %product.4), channel_id=1, source_target_pairs={{0,8},{1,13},{2,10},{3,15},{4,12},{5,9},{6,14},{7,11},{8,0},{9,5},... | collective-permute-start | bytes 98312 | tf_op jit(solution)/shard_map/ppermute | solution.py:260
  21.7 6.1 %collective-permute-start.6 = (bf16[32,512]{1,0:T(8,128)(2,1)S(1)}, bf16[32,512]{1,0:T(8,128)(2,1)S(1)}, u32[]{:S(2)}, u32[]{:S(2)}) collective-permute-start(bf16[32,512]{1,0:T(8,128)(2,1)S(1)} %product.5), channel_id=1, source_target_pairs={{0,10},{1,15},{2,8},{3,13},{4,14},{5,11},{6,12},{7,9},{8,2},{9,7},... | collective-permute-start | bytes 98312 | tf_op jit(solution)/shard_map/ppermute | solution.py:260
  23.1 5.0 %collective-permute-start.8 = (bf16[32,512]{1,0:T(8,128)(2,1)S(1)}, bf16[32,512]{1,0:T(8,128)(2,1)S(1)}, u32[]{:S(2)}, u32[]{:S(2)}) collective-permute-start(bf16[32,512]{1,0:T(8,128)(2,1)S(1)} %product.6), channel_id=1, source_target_pairs={{0,2},{1,7},{2,0},{3,5},{4,6},{5,3},{6,4},{7,1},{8,10},{9,15},{10,... | collective-permute-start | bytes 98312 | tf_op jit(solution)/shard_map/ppermute | solution.py:260
  23.9 4.2 %collective-permute-start.10 = (bf16[32,512]{1,0:T(8,128)(2,1)S(1)}, bf16[32,512]{1,0:T(8,128)(2,1)S(1)}, u32[]{:S(2)}, u32[]{:S(2)}) collective-permute-start(bf16[32,512]{1,0:T(8,128)(2,1)S(1)} %product.7), channel_id=1, source_target_pairs={{0,0},{1,5},{2,2},{3,7},{4,4},{5,1},{6,6},{7,3},{8,8},{9,13},{10,1... | collective-permute-start | bytes 98312 | tf_op jit(solution)/shard_map/ppermute | solution.py:260
  28.1 1.3 %collective-permute-start.11 = (f32[2,16,512]{2,1,0:T(8,128)S(1)}, f32[2,16,512]{2,1,0:T(8,128)S(1)}, u32[]{:S(2)}, u32[]{:S(2)}) collective-permute-start(f32[2,16,512]{2,1,0:T(8,128)S(1)} %get-tuple-element.24), channel_id=1, source_target_pairs={{0,1},{1,0},{2,3},{3,2},{4,5},{5,4},{6,7},{7,6},{8,9},{9,8},{10,11... | collective-permute-start | bytes 196616 | tf_op jit(solution)/shard_map/ppermute | solution.py:270

commit v3 on v2

--- a/solution.py
+++ b/solution.py
@@ -95,38 +95,65 @@
     return rotate_keys(combined, positions)
 
 
-def norm_kernel(rows_ref, gain_ref, out_ref, gains_ref):
-    gains_ref[...] = gain_ref[...].astype(jnp.float32).reshape(gains_ref.shape)
-    out_ref[...] = norm_rows(rows_ref[...], gains_ref[...])
-
-
-def weight_kernel(
-    core_ref, first_ref, own_codes, other_codes, own_groups, other_groups, base_ref, out_ref, codes, groups, base, arrived
-):
-    slice_rows = codes.shape[1]
-    core = core_ref[0]
-    start = pl.multiple_of(first_ref[0] * slice_rows, slice_rows)
+def norm_kernel(rows_ref, gain_ref, out_ref, gains_ref, rows, gain, arrived):
     copies = [
-        pltpu.make_async_copy(own_groups, groups.at[core], arrived.at[0]),
-        pltpu.make_async_copy(other_groups, groups.at[1 - core], arrived.at[1]),
-        pltpu.make_async_copy(own_codes, codes.at[core], arrived.at[2]),
-        pltpu.make_async_copy(base_ref.at[pl.ds(start, 2 * slice_rows)], base, arrived.at[3]),
-        pltpu.make_async_copy(other_codes, codes.at[1 - core], arrived.at[4]),
+        pltpu.make_async_copy(gain_ref, gain, arrived.at[0]),
+        pltpu.make_async_copy(rows_ref, rows, arrived.at[1]),
     ]
     for copy in copies:
         copy.start()
+    copies[0].wait()
+    gains_ref[...] = gain[...].astype(jnp.float32).reshape(gains_ref.shape)
+    copies[1].wait()
+    out_ref[...] = norm_rows(rows[...], gains_ref[...])
+
+
+def weight_kernel(
+    core_ref,
+    first_ref,
+    own_codes,
+    own_scales,
+    own_zeros,
+    base_ref,
+    other_codes,
+    other_scales,
+    other_zeros,
+    out_ref,
+    codes,
+    scales,
+    zeros,
+    base,
+    arrived,
+):
+    slice_rows = codes.shape[0]
+    core = core_ref[0]
+    starts = [pl.multiple_of((1 - core) * slice_rows, slice_rows), pl.multiple_of(core * slice_rows, slice_rows)]
+    first = first_ref[0] * slice_rows
+    copies = [
+        pltpu.make_async_copy(
+            base_ref.at[pl.ds(pl.multiple_of(first + starts[0], slice_rows), slice_rows)], base.at[0], arrived.at[0]
+        ),
+        pltpu.make_async_copy(own_scales, scales, arrived.at[1]),
+        pltpu.make_async_copy(own_zeros, zeros, arrived.at[2]),
+        pltpu.make_async_copy(own_codes, codes, arrived.at[3]),
+        pltpu.make_async_copy(
+            base_ref.at[pl.ds(pl.multiple_of(first + starts[1], slice_rows), slice_rows)], base.at[1], arrived.at[4]
+        ),
+    ]
     for copy in copies:
-        copy.wait()
-    group_count = groups.shape[1] // 2
+        copy.start()
+    group_count = scales.shape[0]
     size = slice_rows // group_count
-    for half in range(2):
+    sources = [(other_codes, other_scales, other_zeros), (codes, scales, zeros)]
+    for member, (member_codes, member_scales, member_zeros) in enumerate(sources):
+        for copy in copies[1:] if member else copies[:1]:
+            copy.wait()
         for group in range(group_count):
             rows = slice(group * size, (group + 1) * size)
-            scale = groups[half, group : group + 1]
-            zero = groups[half, group_count + group : group_count + group + 1]
-            delta = (codes[half, rows].astype(jnp.float32) - zero) * scale
-            rows = slice(half * slice_rows + group * size, half * slice_rows + (group + 1) * size)
-            out_ref[rows] = (base[rows].astype(jnp.float32) + delta).astype(jnp.bfloat16)
+            delta = member_codes[rows].astype(jnp.float32) - member_zeros[group : group + 1]
+            delta = delta * member_scales[group : group + 1]
+            target = pl.ds(pl.multiple_of(starts[member] + group * size, size), size)
+            out_ref[target] = (base[member, rows].astype(jnp.float32) + delta).astype(jnp.bfloat16)
 
 
 def norm_rows(rows, gain):
@@ -152,7 +179,7 @@
     out_ref[...] = jnp.dot(rows_ref[...], weight_ref[...], preferred_element_type=jnp.float32).astype(out_ref.dtype)
 
 
-def sum_kernel(core_ref, far_a, far_b, near_a, near_b, kept_ref, sent_ref, total_ref):
+def sum_kernel(core_ref, far_a, near_a, far_b, near_b, kept_ref, sent_ref, total_ref):
     total_ref[0] = far_a[...].astype(jnp.float32) + far_b[...].astype(jnp.float32)
     total_ref[1] = near_a[...].astype(jnp.float32) + near_b[...].astype(jnp.float32)
     row_count = kept_ref.shape[1]
@@ -186,6 +213,10 @@
 VMEM = pl.BlockSpec(memory_space=pltpu.VMEM)
 SMEM = pl.BlockSpec(memory_space=pltpu.SMEM)
 ANY = pl.BlockSpec(memory_space=pl.ANY)
+
+
+def in_hbm(array):
+    return pltpu.with_memory_space_constraint(array, pltpu.HBM)
 
 
 def paired(
@@ -201,26 +232,31 @@
     variant = lax.div(place, OWNERS)
     swap = [(index, index ^ 1) for index in range(device_count)]
     far = pieces
-    steps = [(0, far, far + 2), (1, far + 1, far + 3), (1, 1, 3), (0, 0, 2)]
+    steps = [(0, far, far + 2), (1, 1, 3), (1, far + 1, far + 3), (0, 0, 2)]
     routes = [
         [(index, index ^ (2 * distances[index % 2])) for index in range(device_count)] for _, *distances in steps
     ]
 
-    slice_shape = (slice_rows, column_count)
-    own_codes = delta_codes[0, 0]
-    own_groups = jnp.concatenate([delta_scales[0, 0], delta_zeros[0, 0]], axis=0)
+    slice_shape, group_shape = (slice_rows, column_count), delta_scales.shape[2:]
+    own_codes, own_scales, own_zeros = delta_codes[0, 0], delta_scales[0, 0], delta_zeros[0, 0]
     other_hidden = lax.ppermute(hidden, "variant", swap)
-    other_groups = lax.ppermute(own_groups, "variant", swap)
+    other_scales = lax.ppermute(own_scales, "variant", swap)
+    other_zeros = lax.ppermute(own_zeros, "variant", swap)
     normed, gains = pl.pallas_call(
         norm_kernel,
         out_shape=[jax.ShapeDtypeStruct((row_count, width), jnp.bfloat16), jax.ShapeDtypeStruct((1, width), jnp.float32)],
-        in_specs=[VMEM] * 2,
+        in_specs=[ANY] * 2,
         out_specs=[VMEM] * 2,
+        scratch_shapes=[
+            pltpu.VMEM((row_count, width), jnp.bfloat16),
+            pltpu.VMEM((width,), jnp.bfloat16),
+            pltpu.SemaphoreType.DMA((2,)),
+        ],
         compiler_params=pltpu.CompilerParams(vmem_limit_bytes=16 << 20),
         name="norm",
-    )(hidden, norm_gain)
-    other_hidden, other_groups, codes, normed = lax.optimization_barrier(
-        (other_hidden, other_groups, own_codes, normed)
+    )(in_hbm(hidden), in_hbm(norm_gain))
+    other_hidden, other_scales, other_zeros, codes, normed = lax.optimization_barrier(
+        (other_hidden, other_scales, other_zeros, own_codes, normed)
     )
     other_codes = lax.ppermute(codes, "variant", swap)
     first, second = pl.pallas_call(
@@ -235,20 +271,32 @@
     weight = pl.pallas_call(
         weight_kernel,
         out_shape=jax.ShapeDtypeStruct((2 * slice_rows, column_count), jnp.bfloat16),
-        in_specs=[SMEM, SMEM] + [ANY] * 5,
+        in_specs=[SMEM, SMEM] + [ANY] * 4 + [VMEM] * 3,
         out_specs=VMEM,
         scratch_shapes=[
+            pltpu.VMEM(slice_shape, jnp.bfloat16),
+            pltpu.VMEM(group_shape, jnp.float32),
+            pltpu.VMEM(group_shape, jnp.float32),
             pltpu.VMEM((2,) + slice_shape, jnp.bfloat16),
-            pltpu.VMEM((2,) + own_groups.shape, jnp.float32),
-            pltpu.VMEM((2 * slice_rows, column_count), jnp.bfloat16),
             pltpu.SemaphoreType.DMA((5,)),
         ],
-        compiler_params=pltpu.CompilerParams(vmem_limit_bytes=48 << 20),
+        compiler_params=pltpu.CompilerParams(vmem_limit_bytes=16 << 20),
         name="weight",
-    )(core[None], (piece * 2)[None], own_codes, other_codes, own_groups, other_groups, base_weight)
+    )(
+        core[None],
+        (piece * 2)[None],
+        in_hbm(own_codes),
+        in_hbm(own_scales),
+        in_hbm(own_zeros),
+        in_hbm(base_weight),
+        other_codes,
+        other_scales,
+        other_zeros,
+    )
+    weight, positions = lax.optimization_barrier((weight, positions))
     incoming = [lax.ppermute((first, second)[index], "variant", route) for (index, _, _), route in zip(steps, routes)]
     parts = [None] * len(steps)
-    for step in (2, 3, 0, 1):
+    for step in range(len(steps)):
         product = pl.pallas_call(
             product_kernel,
             out_shape=jax.ShapeDtypeStruct((2 * row_count, column_count), jnp.bfloat16),

time: 30.7 us -> 29.3 us (0.954)
  local copies, waits for them, and re-layouts: 2.89 us -> 0.01 us
  starting transfers between devices: 9.13 us -> 11.3 us
  other arithmetic: 1.6 us -> 0.21 us
  Pallas kernels: 5.58 us -> 6.37 us
    unnamed x8 -> x4, local copies, waits for them, and re-layouts: 2.89 us -> 0.01 us
    ppermute x4, starting transfers between devices: 1.88 us -> 3.83 us  [paired(): parts[step] = lax.ppermute(product, 'variant', routes[step])]
    pallas_call x1, Pallas kernels: 0.23 us -> 1.22 us  [paired(): pl.pallas_call(norm_kernel, out_shape=[jax.ShapeDtypeStruct((row_count, w...]
    concatenate x1 -> x0, other arithmetic: 0.74 us -> none  [paired(): jnp.concatenate([delta_scales[0, 0], delta_zeros[0, 0]], axis=0)]
    convert_element_type x1, other arithmetic: 0.66 us -> 0.01 us  [turn_factors(): angles = position.astype(jnp.float32)[:, None] * frequency[None, :]]
    ppermute x1 -> x2, starting transfers between devices: 0.06 us -> 0.51 us  [the longest x1 0.45 us: paired(): other_zeros = lax.ppermute(own_zeros, 'variant', swap)]
    ppermute x4, starting transfers between devices: 5.88 us -> 6.28 us  [paired(): lax.ppermute((first, second)[index], 'variant', route)]
    ppermute x1, starting transfers between devices: 0.52 us -> 0.14 us  [paired(): other_codes = lax.ppermute(codes, 'variant', swap)]
  transfers between devices with their start and end apart: 12 -> 13, of which waited for: 5 -> 4; matrix products, arithmetic and copies ran while one was open for 5% -> 1% of each run, Pallas kernels for 16% -> 19%
where the time goes in v3:
time: 29.3 us; the launch traced here: 29 us
  starting transfers between devices  11.3 us (39%)
  waiting for transfers between devices  10.9 us (37%)
  Pallas kernels  6.37 us (22%)
    ppermute x4, waiting for transfers between devices, paired(): lax.ppermute((first, second)[index], 'variant', route)  6.58 us
    ppermute x4, starting transfers between devices, paired(): lax.ppermute((first, second)[index], 'variant', route)  6.28 us
    ppermute x4, starting transfers between devices, paired(): parts[step] = lax.ppermute(product, 'variant', routes[step])  3.83 us
    ppermute x4, waiting for transfers between devices, paired(): parts[step] = lax.ppermute(product, 'variant', routes[step])  3.17 us
    pallas_call x1, Pallas kernels, paired(): pl.pallas_call(weight_kernel, out_shape=jax.ShapeDtypeStruct((2 * slice_r...  2.32 us
    pallas_call x4, Pallas kernels, paired(): pl.pallas_call(product_kernel, out_shape=jax.ShapeDtypeStruct((2 * row_co...  1.8 us
    pallas_call x1, Pallas kernels, paired(): pl.pallas_call(norm_kernel, out_shape=[jax.ShapeDtypeStruct((row_count, w...  1.22 us
    ppermute x1, waiting for transfers between devices, paired(): received = lax.ppermute(sent, 'variant', swap)  1.16 us
  transfers between devices with their start and end apart: 13, of which 4 were waited for; matrix products, arithmetic and copies ran while one was open for 1% of the time, Pallas kernels for 19%

profile of v3, /device:TPU:0, one launch (start us, length us, event | category | flops | bytes accessed | tf_op | source)
XLA Modules:
  0.0 29.0 jit_solution(15535553037324381253)
XLA Ops:
  0.0 0.5 %collective-permute-start = (bf16[16,8192]{1,0:T(8,128)(2,1)}, bf16[16,8192]{1,0:T(8,128)(2,1)S(1)}, u32[]{:S(2)}, u32[]{:S(2)}) collective-permute-start(bf16[16,8192]{1,0:T(8,128)(2,1)} %rows_ref.1), channel_id=1, source_target_pairs={{0,1},{1,0},{2,3},{3,2},{4,5},{5,4},{6,7},{7,6},{8,9},{9,8},{10,11... | collective-permute-start | bytes 786440 | tf_op jit(solution)/shard_map/ppermute | solution.py:242
  0.5 0.5 %collective-permute-start.2 = (f32[8,512]{1,0:T(8,128)}, f32[8,512]{1,0:T(8,128)S(1)}, u32[]{:S(2)}, u32[]{:S(2)}) collective-permute-start(f32[8,512]{1,0:T(8,128)} %bitcast.13), channel_id=1, source_target_pairs={{0,1},{1,0},{2,3},{3,2},{4,5},{5,4},{6,7},{7,6},{8,9},{9,8},{10,11... | collective-permute-start | bytes 49160 | tf_op jit(solution)/shard_map/ppermute | solution.py:244
  1.0 1.2 %norm.1 = (bf16[16,8192]{1,0:T(8,128)(2,1)S(1)}, f32[1,8192]{1,0:T(1,128)S(1)}) custom-call(bf16[16,8192]{1,0:T(8,128)(2,1)} %rows_ref.1, bf16[8192]{0:T(1024)(128)(2,1)} %gain_ref.1), custom_call_target="tpu_custom_call" | custom-call | tf_op jit(solution)/shard_map/norm/pallas_call | solution.py:245
  2.2 0.1 collective-permute-start.4
  2.4 0.2 pieces.1
  2.6 4.1 %collective-permute-start.3 = (bf16[32,2048]{1,0:T(8,128)(2,1)S(1)}, bf16[32,2048]{1,0:T(8,128)(2,1)S(1)}, u32[]{:S(2)}, u32[]{:S(2)}) collective-permute-start(bf16[32,2048]{1,0:T(8,128)(2,1)S(1)} %get-tuple-element.22), channel_id=1, source_target_pairs={{0,8},{1,13},{2,10},{3,15},{4,12},{5,9},{6,14},{7,11},{8,0},{9,5},... | collective-permute-start | bytes 393224 | tf_op jit(solution)/shard_map/ppermute | solution.py:297
  6.7 1.5 %collective-permute-start.6 = (bf16[32,2048]{1,0:T(8,128)(2,1)S(1)}, bf16[32,2048]{1,0:T(8,128)(2,1)S(1)}, u32[]{:S(2)}, u32[]{:S(2)}) collective-permute-start(bf16[32,2048]{1,0:T(8,128)(2,1)S(1)} %get-tuple-element.27), channel_id=1, source_target_pairs={{0,2},{1,7},{2,0},{3,5},{4,6},{5,3},{6,4},{7,1},{8,10},{9,15},{10,... | collective-permute-start | bytes 393224 | tf_op jit(solution)/shard_map/ppermute | solution.py:297
  8.2 0.7 %collective-permute-start.10 = (bf16[32,2048]{1,0:T(8,128)(2,1)S(1)}, bf16[32,2048]{1,0:T(8,128)(2,1)S(1)}, u32[]{:S(2)}, u32[]{:S(2)}) collective-permute-start(bf16[32,2048]{1,0:T(8,128)(2,1)S(1)} %get-tuple-element.22), channel_id=1, source_target_pairs={{0,0},{1,5},{2,2},{3,7},{4,4},{5,1},{6,6},{7,3},{8,8},{9,13},{10,1... | collective-permute-start | bytes 393224 | tf_op jit(solution)/shard_map/ppermute | solution.py:297
  9.0 2.3 %weight.1.weight_ref = bf16[2048,512]{1,0:T(8,128)(2,1)S(1)} custom-call(s32[1]{0:T(128)} %bitcast.2.core_ref, s32[1]{0:T(128)} %bitcast.7.first_ref, bf16[1024,512]{1,0:T(8,128)(2,1)} %bitcast.10, f32[8,512]{1,0:T(8,128)} %bitcast.12, f32[8,512]{1,0:T(8,128)} %bitcast.14, bf16[8192,512]{1,0:T(8,128)(2,1)} %base_ref.1, ...), custom_call_target="tpu_custom_call" | custom-call | tf_op jit(solution)/shard_map/weight/pallas_call | solution.py:271
  11.3 5.3 %collective-permute-done.3.rows_ref = bf16[32,2048]{1,0:T(8,128)(2,1)S(1)} collective-permute-done((bf16[32,2048]{1,0:T(8,128)(2,1)S(1)}, bf16[32,2048]{1,0:T(8,128)(2,1)S(1)}, u32[]{:S(2)}, u32[]{:S(2)}) %collective-permute-start.3) | collective-permute-done | bytes 131104 | tf_op jit(solution)/shard_map/ppermute | solution.py:297
  16.6 0.4 %product.4 = bf16[32,512]{1,0:T(8,128)(2,1)S(1)} custom-call(bf16[32,2048]{1,0:T(8,128)(2,1)S(1)} %collective-permute-done.3.rows_ref, bf16[2048,512]{1,0:T(8,128)(2,1)S(1)} %weight.1.weight_ref), custom_call_target="tpu_custom_call" | custom-call | tf_op jit(solution)/shard_map/product/pallas_call | solution.py:300
  17.1 0.5 %product.5 = bf16[32,512]{1,0:T(8,128)(2,1)S(1)} custom-call(bf16[32,2048]{1,0:T(8,128)(2,1)S(1)} %collective-permute-done.6.rows_ref, bf16[2048,512]{1,0:T(8,128)(2,1)S(1)} %weight.1.weight_ref), custom_call_target="tpu_custom_call" | custom-call | tf_op jit(solution)/shard_map/product/pallas_call | solution.py:300
  17.5 1.9 %collective-permute-start.7 = (bf16[32,512]{1,0:T(8,128)(2,1)S(1)}, bf16[32,512]{1,0:T(8,128)(2,1)S(1)}, u32[]{:S(2)}, u32[]{:S(2)}) collective-permute-start(bf16[32,512]{1,0:T(8,128)(2,1)S(1)} %product.5), channel_id=1, source_target_pairs={{0,2},{1,7},{2,0},{3,5},{4,6},{5,3},{6,4},{7,1},{8,10},{9,15},{10,... | collective-permute-start | bytes 98312 | tf_op jit(solution)/shard_map/ppermute | solution.py:308
  19.4 1.3 %collective-permute-done.8.rows_ref = bf16[32,2048]{1,0:T(8,128)(2,1)S(1)} collective-permute-done((bf16[32,2048]{1,0:T(8,128)(2,1)S(1)}, bf16[32,2048]{1,0:T(8,128)(2,1)S(1)}, u32[]{:S(2)}, u32[]{:S(2)}) %collective-permute-start.8) | collective-permute-done | bytes 131104 | tf_op jit(solution)/shard_map/ppermute | solution.py:297
  20.7 0.4 %product.6 = bf16[32,512]{1,0:T(8,128)(2,1)S(1)} custom-call(bf16[32,2048]{1,0:T(8,128)(2,1)S(1)} %collective-permute-done.8.rows_ref, bf16[2048,512]{1,0:T(8,128)(2,1)S(1)} %weight.1.weight_ref), custom_call_target="tpu_custom_call" | custom-call | tf_op jit(solution)/shard_map/product/pallas_call | solution.py:300
  21.1 1.3 %collective-permute-start.9 = (bf16[32,512]{1,0:T(8,128)(2,1)S(1)}, bf16[32,512]{1,0:T(8,128)(2,1)S(1)}, u32[]{:S(2)}, u32[]{:S(2)}) collective-permute-start(bf16[32,512]{1,0:T(8,128)(2,1)S(1)} %product.6), channel_id=1, source_target_pairs={{0,10},{1,15},{2,8},{3,13},{4,14},{5,11},{6,12},{7,9},{8,2},{9,7},... | collective-permute-start | bytes 98312 | tf_op jit(solution)/shard_map/ppermute | solution.py:308
  22.4 0.4 %product.7 = bf16[32,512]{1,0:T(8,128)(2,1)S(1)} custom-call(bf16[32,2048]{1,0:T(8,128)(2,1)S(1)} %collective-permute-done.10.rows_ref, bf16[2048,512]{1,0:T(8,128)(2,1)S(1)} %weight.1.weight_ref), custom_call_target="tpu_custom_call" | custom-call | tf_op jit(solution)/shard_map/product/pallas_call | solution.py:300
  22.8 0.7 %collective-permute-start.11 = (bf16[32,512]{1,0:T(8,128)(2,1)S(1)}, bf16[32,512]{1,0:T(8,128)(2,1)S(1)}, u32[]{:S(2)}, u32[]{:S(2)}) collective-permute-start(bf16[32,512]{1,0:T(8,128)(2,1)S(1)} %product.7), channel_id=1, source_target_pairs={{0,0},{1,5},{2,2},{3,7},{4,4},{5,1},{6,6},{7,3},{8,8},{9,13},{10,1... | collective-permute-start | bytes 98312 | tf_op jit(solution)/shard_map/ppermute | solution.py:308
  23.5 0.1 fusion
  23.7 3.2 %collective-permute-done.9.far_b = bf16[32,512]{1,0:T(8,128)(2,1)S(1)} collective-permute-done((bf16[32,512]{1,0:T(8,128)(2,1)S(1)}, bf16[32,512]{1,0:T(8,128)(2,1)S(1)}, u32[]{:S(2)}, u32[]{:S(2)}) %collective-permute-start.9) | collective-permute-done | bytes 32800 | tf_op jit(solution)/shard_map/ppermute | solution.py:308
  26.9 0.1 collective-permute-start.12
  27.0 0.1 pad_maximum_fusion
  27.0 1.2 %collective-permute-done.12.received_ref = f32[2,16,512]{2,1,0:T(8,128)S(1)} collective-permute-done((f32[2,16,512]{2,1,0:T(8,128)S(1)}, f32[2,16,512]{2,1,0:T(8,128)S(1)}, u32[]{:S(2)}, u32[]{:S(2)}) %collective-permute-start.12) | collective-permute-done | bytes 65568 | tf_op jit(solution)/shard_map/ppermute | solution.py:318
  28.2 0.8 %finish.1 = bf16[16,512]{1,0:T(8,128)(2,1)} custom-call(s32[1]{0:T(128)} %bitcast.variant_ref, s32[1,16]{1,0:T(1,128)S(1)} %bitcast.8, f32[2,16,512]{2,1,0:T(8,128)S(1)} %get-tuple-element.28.kept_ref, f32[2,16,512]{2,1,0:T(8,128)S(1)} %collective-permute-done.12.received_ref, f32[16,128]{1,0:T(8,128)S(1)} %get-tuple-element.34.cosine_ref, ...), custom_call_target="tpu_custom_call" | custom-call | tf_op jit(solution)/shard_map/finish/pallas_call | solution.py:320
  (19 shorter events, 0.2 us)
Async XLA Ops:
  0.0 2.2 %collective-permute-start = (bf16[16,8192]{1,0:T(8,128)(2,1)}, bf16[16,8192]{1,0:T(8,128)(2,1)S(1)}, u32[]{:S(2)}, u32[]{:S(2)}) collective-permute-start(bf16[16,8192]{1,0:T(8,128)(2,1)} %rows_ref.1), channel_id=1, source_target_pairs={{0,1},{1,0},{2,3},{3,2},{4,5},{5,4},{6,7},{7,6},{8,9},{9,8},{10,11... | collective-permute-start | bytes 786440 | tf_op jit(solution)/shard_map/ppermute | solution.py:242
  0.5 1.7 %collective-permute-start.1 = (f32[8,512]{1,0:T(8,128)}, f32[8,512]{1,0:T(8,128)S(1)}, u32[]{:S(2)}, u32[]{:S(2)}) collective-permute-start(f32[8,512]{1,0:T(8,128)} %bitcast.11), channel_id=1, source_target_pairs={{0,1},{1,0},{2,3},{3,2},{4,5},{5,4},{6,7},{7,6},{8,9},{9,8},{10,11... | collective-permute-start | bytes 49160 | tf_op jit(solution)/shard_map/ppermute | solution.py:243
  0.5 1.7 %collective-permute-start.2 = (f32[8,512]{1,0:T(8,128)}, f32[8,512]{1,0:T(8,128)S(1)}, u32[]{:S(2)}, u32[]{:S(2)}) collective-permute-start(f32[8,512]{1,0:T(8,128)} %bitcast.13), channel_id=1, source_target_pairs={{0,1},{1,0},{2,3},{3,2},{4,5},{5,4},{6,7},{7,6},{8,9},{9,8},{10,11... | collective-permute-start | bytes 49160 | tf_op jit(solution)/shard_map/ppermute | solution.py:244
  2.2 6.7 %collective-permute-start.4 = (bf16[1024,512]{1,0:T(8,128)(2,1)}, bf16[1024,512]{1,0:T(8,128)(2,1)S(1)}, u32[]{:S(2)}, u32[]{:S(2)}) collective-permute-start(bf16[1024,512]{1,0:T(8,128)(2,1)} %bitcast.9), channel_id=1, source_target_pairs={{0,1},{1,0},{2,3},{3,2},{4,5},{5,4},{6,7},{7,6},{8,9},{9,8},{10,11... | collective-permute-start | bytes 3145736 | tf_op jit(solution)/shard_map/ppermute | solution.py:261
  2.6 14.0 %collective-permute-start.3 = (bf16[32,2048]{1,0:T(8,128)(2,1)S(1)}, bf16[32,2048]{1,0:T(8,128)(2,1)S(1)}, u32[]{:S(2)}, u32[]{:S(2)}) collective-permute-start(bf16[32,2048]{1,0:T(8,128)(2,1)S(1)} %get-tuple-element.22), channel_id=1, source_target_pairs={{0,8},{1,13},{2,10},{3,15},{4,12},{5,9},{6,14},{7,11},{8,0},{9,5},... | collective-permute-start | bytes 393224 | tf_op jit(solution)/shard_map/ppermute | solution.py:297
  6.7 10.4 %collective-permute-start.6 = (bf16[32,2048]{1,0:T(8,128)(2,1)S(1)}, bf16[32,2048]{1,0:T(8,128)(2,1)S(1)}, u32[]{:S(2)}, u32[]{:S(2)}) collective-permute-start(bf16[32,2048]{1,0:T(8,128)(2,1)S(1)} %get-tuple-element.27), channel_id=1, source_target_pairs={{0,2},{1,7},{2,0},{3,5},{4,6},{5,3},{6,4},{7,1},{8,10},{9,15},{10,... | collective-permute-start | bytes 393224 | tf_op jit(solution)/shard_map/ppermute | solution.py:297
  8.2 12.5 %collective-permute-start.8 = (bf16[32,2048]{1,0:T(8,128)(2,1)S(1)}, bf16[32,2048]{1,0:T(8,128)(2,1)S(1)}, u32[]{:S(2)}, u32[]{:S(2)}) collective-permute-start(bf16[32,2048]{1,0:T(8,128)(2,1)S(1)} %get-tuple-element.27), channel_id=1, source_target_pairs={{0,10},{1,15},{2,8},{3,13},{4,14},{5,11},{6,12},{7,9},{8,2},{9,7},... | collective-permute-start | bytes 393224 | tf_op jit(solution)/shard_map/ppermute | solution.py:297
  8.2 14.1 %collective-permute-start.10 = (bf16[32,2048]{1,0:T(8,128)(2,1)S(1)}, bf16[32,2048]{1,0:T(8,128)(2,1)S(1)}, u32[]{:S(2)}, u32[]{:S(2)}) collective-permute-start(bf16[32,2048]{1,0:T(8,128)(2,1)S(1)} %get-tuple-element.22), channel_id=1, source_target_pairs={{0,0},{1,5},{2,2},{3,7},{4,4},{5,1},{6,6},{7,3},{8,8},{9,13},{10,1... | collective-permute-start | bytes 393224 | tf_op jit(solution)/shard_map/ppermute | solution.py:297
  8.9 14.6 %copy-start.1 = (s32[16]{0:T(128)S(1)}, s32[16]{0:T(128)}, u32[]{:S(2)}) copy-start(s32[16]{0:T(128)} %param.15) | copy-start | bytes 196
  8.9 19.3 %copy-start = (s32[16,1]{0,1:T(1,128)S(1)}, s32[16,1]{0,1:T(1,128)}, u32[]{:S(2)}) copy-start(s32[16,1]{0,1:T(1,128)} %param.14) | copy-start | bytes 196
  17.0 6.6 %collective-permute-start.5 = (bf16[32,512]{1,0:T(8,128)(2,1)S(1)}, bf16[32,512]{1,0:T(8,128)(2,1)S(1)}, u32[]{:S(2)}, u32[]{:S(2)}) collective-permute-start(bf16[32,512]{1,0:T(8,128)(2,1)S(1)} %product.4), channel_id=1, source_target_pairs={{0,8},{1,13},{2,10},{3,15},{4,12},{5,9},{6,14},{7,11},{8,0},{9,5},... | collective-permute-start | bytes 98312 | tf_op jit(solution)/shard_map/ppermute | solution.py:308
  17.5 6.2 %collective-permute-start.7 = (bf16[32,512]{1,0:T(8,128)(2,1)S(1)}, bf16[32,512]{1,0:T(8,128)(2,1)S(1)}, u32[]{:S(2)}, u32[]{:S(2)}) collective-permute-start(bf16[32,512]{1,0:T(8,128)(2,1)S(1)} %product.5), channel_id=1, source_target_pairs={{0,2},{1,7},{2,0},{3,5},{4,6},{5,3},{6,4},{7,1},{8,10},{9,15},{10,... | collective-permute-start | bytes 98312 | tf_op jit(solution)/shard_map/ppermute | solution.py:308
  21.1 5.7 %collective-permute-start.9 = (bf16[32,512]{1,0:T(8,128)(2,1)S(1)}, bf16[32,512]{1,0:T(8,128)(2,1)S(1)}, u32[]{:S(2)}, u32[]{:S(2)}) collective-permute-start(bf16[32,512]{1,0:T(8,128)(2,1)S(1)} %product.6), channel_id=1, source_target_pairs={{0,10},{1,15},{2,8},{3,13},{4,14},{5,11},{6,12},{7,9},{8,2},{9,7},... | collective-permute-start | bytes 98312 | tf_op jit(solution)/shard_map/ppermute | solution.py:308
  22.8 4.0 %collective-permute-start.11 = (bf16[32,512]{1,0:T(8,128)(2,1)S(1)}, bf16[32,512]{1,0:T(8,128)(2,1)S(1)}, u32[]{:S(2)}, u32[]{:S(2)}) collective-permute-start(bf16[32,512]{1,0:T(8,128)(2,1)S(1)} %product.7), channel_id=1, source_target_pairs={{0,0},{1,5},{2,2},{3,7},{4,4},{5,1},{6,6},{7,3},{8,8},{9,13},{10,1... | collective-permute-start | bytes 98312 | tf_op jit(solution)/shard_map/ppermute | solution.py:308
  26.9 1.3 %collective-permute-start.12 = (f32[2,16,512]{2,1,0:T(8,128)S(1)}, f32[2,16,512]{2,1,0:T(8,128)S(1)}, u32[]{:S(2)}, u32[]{:S(2)}) collective-permute-start(f32[2,16,512]{2,1,0:T(8,128)S(1)} %get-tuple-element.29), channel_id=1, source_target_pairs={{0,1},{1,0},{2,3},{3,2},{4,5},{5,4},{6,7},{7,6},{8,9},{9,8},{10,11... | collective-permute-start | bytes 196616 | tf_op jit(solution)/shard_map/ppermute | solution.py:318

commit v4 on v2

--- a/solution.py
+++ b/solution.py
@@ -95,38 +95,57 @@
     return rotate_keys(combined, positions)
 
 
-def norm_kernel(rows_ref, gain_ref, out_ref, gains_ref):
-    gains_ref[...] = gain_ref[...].astype(jnp.float32).reshape(gains_ref.shape)
-    out_ref[...] = norm_rows(rows_ref[...], gains_ref[...])
-
-
-def weight_kernel(
-    core_ref, first_ref, own_codes, other_codes, own_groups, other_groups, base_ref, out_ref, codes, groups, base, arrived
+def front_kernel(
+    place_ref,
+    hidden_ref,
+    gain_ref,
+    codes_ref,
+    scales_ref,
+    zeros_ref,
+    base_ref,
+    normed_ref,
+    gains_ref,
+    weight_ref,
+    hidden,
+    gain,
+    codes,
+    scales,
+    zeros,
+    base,
+    arrived,
 ):
-    slice_rows = codes.shape[1]
-    core = core_ref[0]
-    start = pl.multiple_of(first_ref[0] * slice_rows, slice_rows)
+    slice_rows = codes.shape[0]
+    half = slice_rows // 2
+    start = place_ref[0] * slice_rows
     copies = [
-        pltpu.make_async_copy(own_groups, groups.at[core], arrived.at[0]),
-        pltpu.make_async_copy(other_groups, groups.at[1 - core], arrived.at[1]),
-        pltpu.make_async_copy(own_codes, codes.at[core], arrived.at[2]),
-        pltpu.make_async_copy(base_ref.at[pl.ds(start, 2 * slice_rows)], base, arrived.at[3]),
-        pltpu.make_async_copy(other_codes, codes.at[1 - core], arrived.at[4]),
+        pltpu.make_async_copy(hidden_ref, hidden, arrived.at[0]),
+        pltpu.make_async_copy(gain_ref, gain, arrived.at[1]),
+        pltpu.make_async_copy(scales_ref, scales, arrived.at[2]),
+        pltpu.make_async_copy(zeros_ref, zeros, arrived.at[3]),
     ]
+    for part in range(2):
+        rows = pl.ds(part * half, half)
+        base_rows = pl.ds(pl.multiple_of(start + part * half, half), half)
+        copies.append(pltpu.make_async_copy(codes_ref.at[rows], codes.at[rows], arrived.at[4 + 2 * part]))
+        copies.append(pltpu.make_async_copy(base_ref.at[base_rows], base.at[rows], arrived.at[5 + 2 * part]))
     for copy in copies:
         copy.start()
-    for copy in copies:
+    for copy in copies[:2]:
         copy.wait()
-    group_count = groups.shape[1] // 2
+    gains_ref[...] = gain[...].astype(jnp.float32).reshape(gains_ref.shape)
+    normed_ref[...] = norm_rows(hidden[...], gains_ref[...])
+    for copy in copies[2:4]:
+        copy.wait()
+    group_count = scales.shape[0]
     size = slice_rows // group_count
-    for half in range(2):
-        for group in range(group_count):
-            rows = slice(group * size, (group + 1) * size)
-            scale = groups[half, group : group + 1]
-            zero = groups[half, group_count + group : group_count + group + 1]
-            delta = (codes[half, rows].astype(jnp.float32) - zero) * scale
-            rows = slice(half * slice_rows + group * size, half * slice_rows + (group + 1) * size)
-            out_ref[rows] = (base[rows].astype(jnp.float32) + delta).astype(jnp.bfloat16)
+    for group in range(group_count):
+        if group == 0 or group == group_count // 2:
+            part = 4 + 2 * (group > 0)
+            for copy in copies[part : part + 2]:
+                copy.wait()
+        rows = slice(group * size, (group + 1) * size)
+        delta = (codes[rows].astype(jnp.float32) - zeros[group : group + 1]) * scales[group : group + 1]
+        weight_ref[rows] = (base[rows].astype(jnp.float32) + delta).astype(jnp.bfloat16)
 
 
 def norm_rows(rows, gain):
@@ -135,7 +154,7 @@
     return (floats * lax.rsqrt(mean_square + epsilon) * gain).astype(jnp.bfloat16)
 
 
-def pieces_kernel(first_ref, core_ref, own_ref, other_ref, gain_ref, *rest):
+def pieces_kernel(orders, piece_ref, core_ref, own_ref, other_ref, gain_ref, *rest):
     outs, normed_ref = rest[:-1], rest[-1]
     row_count = own_ref.shape[0]
     core = core_ref[0]
@@ -144,19 +163,40 @@
     normed_ref[other_rows] = norm_rows(other_ref[...], gain_ref[...])
     for index, out_ref in enumerate(outs):
         piece_width = out_ref.shape[1]
-        start = pl.multiple_of((first_ref[0] ^ index) * piece_width, piece_width)
+        offset = jnp.where(core == 0, orders[0][index] % len(outs), orders[1][index] % len(outs))
+        start = pl.multiple_of((piece_ref[0] ^ offset) * piece_width, piece_width)
         out_ref[...] = normed_ref[:, pl.ds(start, piece_width)]
 
 
-def product_kernel(rows_ref, weight_ref, out_ref):
-    out_ref[...] = jnp.dot(rows_ref[...], weight_ref[...], preferred_element_type=jnp.float32).astype(out_ref.dtype)
-
-
-def sum_kernel(core_ref, far_a, far_b, near_a, near_b, kept_ref, sent_ref, total_ref):
-    total_ref[0] = far_a[...].astype(jnp.float32) + far_b[...].astype(jnp.float32)
-    total_ref[1] = near_a[...].astype(jnp.float32) + near_b[...].astype(jnp.float32)
+def product_kernel(core_ref, rows_ref, own_ref, other_ref, out_ref):
+    half = rows_ref.shape[1] // 2
+
+    def run(low, high):
+        total = jnp.dot(rows_ref[:, :half], low[...], preferred_element_type=jnp.float32)
+        total += jnp.dot(rows_ref[:, half:], high[...], preferred_element_type=jnp.float32)
+        out_ref[...] = total.astype(out_ref.dtype)
+
+    @pl.when(core_ref[0] == 0)
+    def _():
+        run(own_ref, other_ref)
+
+    @pl.when(core_ref[0] == 1)
+    def _():
+        run(other_ref, own_ref)
+
+
+def sum_kernel(orders, core_ref, *rest):
+    parts, (kept_ref, sent_ref, total_ref) = rest[:-3], rest[-3:]
+    core = core_ref[0]
+    for member, order in enumerate(orders):
+
+        @pl.when(core == member)
+        def _(order=order):
+            for kind in range(2):
+                chosen = [part for part, distance in zip(parts, order) if (distance < len(order)) == bool(kind)]
+                total_ref[kind] = sum((part[...].astype(jnp.float32) for part in chosen), jnp.zeros(total_ref.shape[1:], jnp.float32))
+
     row_count = kept_ref.shape[1]
-    core = core_ref[0]
     kept_ref[...] = total_ref[:, pl.ds(pl.multiple_of(core * row_count, row_count), row_count)]
     sent_ref[...] = total_ref[:, pl.ds(pl.multiple_of((1 - core) * row_count, row_count), row_count)]
 
@@ -188,6 +228,10 @@
 ANY = pl.BlockSpec(memory_space=pl.ANY)
 
 
+def in_hbm(array):
+    return pltpu.with_memory_space_constraint(array, pltpu.HBM)
+
+
 def paired(
     hidden, norm_gain, base_weight, delta_codes, delta_scales, delta_zeros, variant_ids, positions
 ):
@@ -200,66 +244,65 @@
     piece = lax.div(lax.rem(place, OWNERS), 2)
     variant = lax.div(place, OWNERS)
     swap = [(index, index ^ 1) for index in range(device_count)]
-    far = pieces
-    steps = [(0, far, far + 2), (1, far + 1, far + 3), (1, 1, 3), (0, 0, 2)]
+    orders = ((4, 5, 6, 0), (7, 2, 3, 1))
+    steps = list(zip(*orders))
     routes = [
-        [(index, index ^ (2 * distances[index % 2])) for index in range(device_count)] for _, *distances in steps
+        [(index, index ^ (2 * distances[index % 2])) for index in range(device_count)] for distances in steps
     ]
 
-    slice_shape = (slice_rows, column_count)
-    own_codes = delta_codes[0, 0]
-    own_groups = jnp.concatenate([delta_scales[0, 0], delta_zeros[0, 0]], axis=0)
+    slice_shape, group_shape = (slice_rows, column_count), delta_scales.shape[2:]
+    own_codes, own_scales, own_zeros = delta_codes[0, 0], delta_scales[0, 0], delta_zeros[0, 0]
     other_hidden = lax.ppermute(hidden, "variant", swap)
-    other_groups = lax.ppermute(own_groups, "variant", swap)
-    normed, gains = pl.pallas_call(
-        norm_kernel,
-        out_shape=[jax.ShapeDtypeStruct((row_count, width), jnp.bfloat16), jax.ShapeDtypeStruct((1, width), jnp.float32)],
-        in_specs=[VMEM] * 2,
-        out_specs=[VMEM] * 2,
+    normed, gains, own_weight = pl.pallas_call(
+        front_kernel,
+        out_shape=[
+            jax.ShapeDtypeStruct((row_count, width), jnp.bfloat16),
+            jax.ShapeDtypeStruct((1, width), jnp.float32),
+            jax.ShapeDtypeStruct(slice_shape, jnp.bfloat16),
+        ],
+        in_specs=[SMEM] + [ANY] * 6,
+        out_specs=[VMEM] * 3,
+        scratch_shapes=[
+            pltpu.VMEM((row_count, width), jnp.bfloat16),
+            pltpu.VMEM((width,), jnp.bfloat16),
+            pltpu.VMEM(slice_shape, jnp.bfloat16),
+            pltpu.VMEM(group_shape, jnp.float32),
+            pltpu.VMEM(group_shape, jnp.float32),
+            pltpu.VMEM(slice_shape, jnp.bfloat16),
+            pltpu.SemaphoreType.DMA((8,)),
+        ],
         compiler_params=pltpu.CompilerParams(vmem_limit_bytes=16 << 20),
-        name="norm",
-    )(hidden, norm_gain)
-    other_hidden, other_groups, codes, normed = lax.optimization_barrier(
-        (other_hidden, other_groups, own_codes, normed)
-    )
-    other_codes = lax.ppermute(codes, "variant", swap)
-    first, second = pl.pallas_call(
-        pieces_kernel,
-        out_shape=[jax.ShapeDtypeStruct((2 * row_count, width // pieces), jnp.bfloat16)] * 2,
+        name="front",
+    )(
+        lax.rem(place, OWNERS)[None],
+        *[in_hbm(array) for array in (hidden, norm_gain, own_codes, own_scales, own_zeros, base_weight)],
+    )
+    other_hidden, normed = lax.optimization_barrier((other_hidden, normed))
+    outgoing = pl.pallas_call(
+        functools.partial(pieces_kernel, orders),
+        out_shape=[jax.ShapeDtypeStruct((2 * row_count, width // pieces), jnp.bfloat16)] * len(steps),
         in_specs=[SMEM, SMEM, VMEM, VMEM, VMEM],
-        out_specs=[VMEM] * 2,
+        out_specs=[VMEM] * len(steps),
         scratch_shapes=[pltpu.VMEM((2 * row_count, width), jnp.bfloat16)],
         compiler_params=pltpu.CompilerParams(vmem_limit_bytes=16 << 20),
         name="pieces",
-    )((piece ^ (2 * core))[None], core[None], normed, other_hidden, gains)
-    weight = pl.pallas_call(
-        weight_kernel,
-        out_shape=jax.ShapeDtypeStruct((2 * slice_rows, column_count), jnp.bfloat16),
-        in_specs=[SMEM, SMEM] + [ANY] * 5,
-        out_specs=VMEM,
-        scratch_shapes=[
-            pltpu.VMEM((2,) + slice_shape, jnp.bfloat16),
-            pltpu.VMEM((2,) + own_groups.shape, jnp.float32),
-            pltpu.VMEM((2 * slice_rows, column_count), jnp.bfloat16),
-            pltpu.SemaphoreType.DMA((5,)),
-        ],
-        compiler_params=pltpu.CompilerParams(vmem_limit_bytes=48 << 20),
-        name="weight",
-    )(core[None], (piece * 2)[None], own_codes, other_codes, own_groups, other_groups, base_weight)
-    incoming = [lax.ppermute((first, second)[index], "variant", route) for (index, _, _), route in zip(steps, routes)]
+    )(piece[None], core[None], normed, other_hidden, gains)
+    *outgoing, own_weight = lax.optimization_barrier((*outgoing, own_weight))
+    other_weight, positions = lax.optimization_barrier((lax.ppermute(own_weight, "variant", swap), positions))
+    incoming = [lax.ppermute(rows, "variant", route) for rows, route in zip(outgoing, routes)]
     parts = [None] * len(steps)
-    for step in (2, 3, 0, 1):
+    for step in range(len(steps)):
         product = pl.pallas_call(
             product_kernel,
             out_shape=jax.ShapeDtypeStruct((2 * row_count, column_count), jnp.bfloat16),
-            in_specs=[VMEM, VMEM],
+            in_specs=[SMEM, VMEM, VMEM, VMEM],
             out_specs=VMEM,
             compiler_params=pltpu.CompilerParams(vmem_limit_bytes=16 << 20),
             name="product",
-        )(incoming[step], weight)
+        )(core[None], incoming[step], own_weight, other_weight)
         parts[step] = lax.ppermute(product, "variant", routes[step])
     kept, sent = pl.pallas_call(
-        sum_kernel,
+        functools.partial(sum_kernel, orders),
         out_shape=[jax.ShapeDtypeStruct((2, row_count, column_count), jnp.float32)] * 2,
         in_specs=[SMEM] + [VMEM] * len(parts),
         out_specs=[VMEM] * 2,

time: 30.7 us -> 27.8 us (0.906)
  starting transfers between devices: 9.13 us -> 14.9 us
  waiting for transfers between devices: 10.9 us -> 7.54 us
  local copies, waits for them, and re-layouts: 2.89 us -> 0.01 us
  other arithmetic: 1.6 us -> 0.21 us
  Pallas kernels: 5.58 us -> 4.78 us
    ppermute x6 -> x5, starting transfers between devices: 6.46 us -> 9.68 us  [the longest x4 9.56 us: paired(): lax.ppermute(rows, 'variant', route)]
    unnamed x8 -> x4, local copies, waits for them, and re-layouts: 2.89 us -> 0.01 us
    ppermute x4, starting transfers between devices: 1.88 us -> 4.66 us  [paired(): parts[step] = lax.ppermute(product, 'variant', routes[step])]
    ppermute x4, waiting for transfers between devices: 3.41 us -> 0.64 us  [paired(): parts[step] = lax.ppermute(product, 'variant', routes[step])]
    pallas_call x4 -> x3, Pallas kernels: 3.01 us -> 2.22 us  [the longest x1 1.92 us: paired(): pl.pallas_call(front_kernel, out_shape=[jax.ShapeDtypeStruct((row_count,...]
    ppermute x6 -> x5, waiting for transfers between devices: 6.57 us -> 5.79 us  [the longest x4 5.79 us: paired(): lax.ppermute(rows, 'variant', route)]
    concatenate x1 -> x0, other arithmetic: 0.74 us -> none  [paired(): jnp.concatenate([delta_scales[0, 0], delta_zeros[0, 0]], axis=0)]
    convert_element_type x1, other arithmetic: 0.66 us -> 0.01 us  [turn_factors(): angles = position.astype(jnp.float32)[:, None] * frequency[None, :]]
  transfers between devices with their start and end apart: 12 -> 11, of which waited for: 5 -> 4; matrix products, arithmetic and copies ran while one was open for 5% -> 1% of each run, Pallas kernels for 16% -> 13%
where the time goes in v4:
time: 27.8 us; the launch traced here: 27.6 us
  starting transfers between devices  14.9 us (54%)
  waiting for transfers between devices  7.54 us (27%)
  Pallas kernels  4.78 us (17%)
    ppermute x4, starting transfers between devices, paired(): lax.ppermute(rows, 'variant', route)  9.56 us
    ppermute x4, waiting for transfers between devices, paired(): lax.ppermute(rows, 'variant', route)  5.79 us
    ppermute x4, starting transfers between devices, paired(): parts[step] = lax.ppermute(product, 'variant', routes[step])  4.66 us
    pallas_call x1, Pallas kernels, paired(): pl.pallas_call(front_kernel, out_shape=[jax.ShapeDtypeStruct((row_count,...  1.92 us
    pallas_call x4, Pallas kernels, paired(): pl.pallas_call(product_kernel, out_shape=jax.ShapeDtypeStruct((2 * row_co...  1.79 us
    ppermute x1, waiting for transfers between devices, paired(): received = lax.ppermute(sent, 'variant', swap)  1.1 us
    pallas_call x1, Pallas kernels, paired(): pl.pallas_call(finish_kernel, out_shape=jax.ShapeDtypeStruct((row_count,...  0.77 us
    ppermute x4, waiting for transfers between devices, paired(): parts[step] = lax.ppermute(product, 'variant', routes[step])  0.64 us
  transfers between devices with their start and end apart: 11, of which 4 were waited for; matrix products, arithmetic and copies ran while one was open for 1% of the time, Pallas kernels for 13%

profile of v4, /device:TPU:0, one launch (start us, length us, event | category | flops | bytes accessed | tf_op | source)
XLA Modules:
  0.0 27.6 jit_solution(17182778026504088205)
XLA Ops:
  0.0 0.5 %collective-permute-start = (bf16[16,8192]{1,0:T(8,128)(2,1)}, bf16[16,8192]{1,0:T(8,128)(2,1)S(1)}, u32[]{:S(2)}, u32[]{:S(2)}) collective-permute-start(bf16[16,8192]{1,0:T(8,128)(2,1)} %hidden_ref.1), channel_id=1, source_target_pairs={{0,1},{1,0},{2,3},{3,2},{4,5},{5,4},{6,7},{7,6},{8,9},{9,8},{10,11... | collective-permute-start | bytes 786440 | tf_op jit(solution)/shard_map/ppermute | solution.py:255
  0.5 1.9 %front.1 = (bf16[16,8192]{1,0:T(8,128)(2,1)S(1)}, f32[1,8192]{1,0:T(1,128)S(1)}, bf16[1024,512]{1,0:T(8,128)(2,1)S(1)}) custom-call(s32[1]{0:T(128)} %bitcast.4.place_ref, bf16[16,8192]{1,0:T(8,128)(2,1)} %hidden_ref.1, bf16[8192]{0:T(1024)(128)(2,1)} %gain_ref.1, bf16[1024,512]{1,0:T(8,128)(2,1)} %bitcast.9, f32[8,512]{1,0:T(8,128)} %bitcast.10, ...), custom_call_target="tpu_custom_call" | custom-call | tf_op jit(solution)/shard_map/front/pallas_call | solution.py:256
  2.4 0.3 pieces.1
  2.7 0.1 collective-permute-start.2
  2.8 4.0 %collective-permute-start.1 = (bf16[32,2048]{1,0:T(8,128)(2,1)S(1)}, bf16[32,2048]{1,0:T(8,128)(2,1)S(1)}, u32[]{:S(2)}, u32[]{:S(2)}) collective-permute-start(bf16[32,2048]{1,0:T(8,128)(2,1)S(1)} %get-tuple-element.32), channel_id=1, source_target_pairs={{0,8},{1,15},{2,10},{3,13},{4,12},{5,11},{6,14},{7,9},{8,0},{9,7},... | collective-permute-start | bytes 393224 | tf_op jit(solution)/shard_map/ppermute | solution.py:292
  6.8 1.3 %collective-permute-start.4 = (bf16[32,2048]{1,0:T(8,128)(2,1)S(1)}, bf16[32,2048]{1,0:T(8,128)(2,1)S(1)}, u32[]{:S(2)}, u32[]{:S(2)}) collective-permute-start(bf16[32,2048]{1,0:T(8,128)(2,1)S(1)} %get-tuple-element.35), channel_id=1, source_target_pairs={{0,10},{1,5},{2,8},{3,7},{4,14},{5,1},{6,12},{7,3},{8,2},{9,13},{1... | collective-permute-start | bytes 393224 | tf_op jit(solution)/shard_map/ppermute | solution.py:292
  8.1 3.6 %collective-permute-start.6 = (bf16[32,2048]{1,0:T(8,128)(2,1)S(1)}, bf16[32,2048]{1,0:T(8,128)(2,1)S(1)}, u32[]{:S(2)}, u32[]{:S(2)}) collective-permute-start(bf16[32,2048]{1,0:T(8,128)(2,1)S(1)} %get-tuple-element.36), channel_id=1, source_target_pairs={{0,12},{1,7},{2,14},{3,5},{4,8},{5,3},{6,10},{7,1},{8,4},{9,15},{1... | collective-permute-start | bytes 393224 | tf_op jit(solution)/shard_map/ppermute | solution.py:292
  11.7 0.7 %collective-permute-start.8 = (bf16[32,2048]{1,0:T(8,128)(2,1)S(1)}, bf16[32,2048]{1,0:T(8,128)(2,1)S(1)}, u32[]{:S(2)}, u32[]{:S(2)}) collective-permute-start(bf16[32,2048]{1,0:T(8,128)(2,1)S(1)} %get-tuple-element.37), channel_id=1, source_target_pairs={{0,0},{1,3},{2,2},{3,1},{4,4},{5,7},{6,6},{7,5},{8,8},{9,11},{10,1... | collective-permute-start | bytes 393224 | tf_op jit(solution)/shard_map/ppermute | solution.py:292
  12.4 1.5 %collective-permute-done.1.rows_ref = bf16[32,2048]{1,0:T(8,128)(2,1)S(1)} collective-permute-done((bf16[32,2048]{1,0:T(8,128)(2,1)S(1)}, bf16[32,2048]{1,0:T(8,128)(2,1)S(1)}, u32[]{:S(2)}, u32[]{:S(2)}) %collective-permute-start.1) | collective-permute-done | bytes 131104 | tf_op jit(solution)/shard_map/ppermute | solution.py:292
  13.9 0.4 %product.4 = bf16[32,512]{1,0:T(8,128)(2,1)S(1)} custom-call(s32[1]{0:T(128)} %bitcast.2.core_ref, bf16[32,2048]{1,0:T(8,128)(2,1)S(1)} %collective-permute-done.1.rows_ref, bf16[1024,512]{1,0:T(8,128)(2,1)S(1)} %get-tuple-element.33.own_ref, bf16[1024,512]{1,0:T(8,128)(2,1)S(1)} %collective-permute-done.2.other_ref), custom_call_target="tpu_custom_call" | custom-call | tf_op jit(solution)/shard_map/product/pallas_call | solution.py:295
  14.3 4.3 %collective-permute-done.4.rows_ref = bf16[32,2048]{1,0:T(8,128)(2,1)S(1)} collective-permute-done((bf16[32,2048]{1,0:T(8,128)(2,1)S(1)}, bf16[32,2048]{1,0:T(8,128)(2,1)S(1)}, u32[]{:S(2)}, u32[]{:S(2)}) %collective-permute-start.4) | collective-permute-done | bytes 131104 | tf_op jit(solution)/shard_map/ppermute | solution.py:292
  18.7 0.4 %product.5 = bf16[32,512]{1,0:T(8,128)(2,1)S(1)} custom-call(s32[1]{0:T(128)} %bitcast.2.core_ref, bf16[32,2048]{1,0:T(8,128)(2,1)S(1)} %collective-permute-done.4.rows_ref, bf16[1024,512]{1,0:T(8,128)(2,1)S(1)} %get-tuple-element.33.own_ref, bf16[1024,512]{1,0:T(8,128)(2,1)S(1)} %collective-permute-done.2.other_ref), custom_call_target="tpu_custom_call" | custom-call | tf_op jit(solution)/shard_map/product/pallas_call | solution.py:295
  19.1 0.2 collective-permute-start.5
  19.3 0.4 %product.6 = bf16[32,512]{1,0:T(8,128)(2,1)S(1)} custom-call(s32[1]{0:T(128)} %bitcast.2.core_ref, bf16[32,2048]{1,0:T(8,128)(2,1)S(1)} %collective-permute-done.6.rows_ref, bf16[1024,512]{1,0:T(8,128)(2,1)S(1)} %get-tuple-element.33.own_ref, bf16[1024,512]{1,0:T(8,128)(2,1)S(1)} %collective-permute-done.2.other_ref), custom_call_target="tpu_custom_call" | custom-call | tf_op jit(solution)/shard_map/product/pallas_call | solution.py:295
  19.7 3.8 %collective-permute-start.7 = (bf16[32,512]{1,0:T(8,128)(2,1)S(1)}, bf16[32,512]{1,0:T(8,128)(2,1)S(1)}, u32[]{:S(2)}, u32[]{:S(2)}) collective-permute-start(bf16[32,512]{1,0:T(8,128)(2,1)S(1)} %product.6), channel_id=1, source_target_pairs={{0,12},{1,7},{2,14},{3,5},{4,8},{5,3},{6,10},{7,1},{8,4},{9,15},{1... | collective-permute-start | bytes 98312 | tf_op jit(solution)/shard_map/ppermute | solution.py:303
  23.6 0.4 %product.7 = bf16[32,512]{1,0:T(8,128)(2,1)S(1)} custom-call(s32[1]{0:T(128)} %bitcast.2.core_ref, bf16[32,2048]{1,0:T(8,128)(2,1)S(1)} %collective-permute-done.8.rows_ref, bf16[1024,512]{1,0:T(8,128)(2,1)S(1)} %get-tuple-element.33.own_ref, bf16[1024,512]{1,0:T(8,128)(2,1)S(1)} %collective-permute-done.2.other_ref), custom_call_target="tpu_custom_call" | custom-call | tf_op jit(solution)/shard_map/product/pallas_call | solution.py:295
  24.0 0.7 %collective-permute-start.9 = (bf16[32,512]{1,0:T(8,128)(2,1)S(1)}, bf16[32,512]{1,0:T(8,128)(2,1)S(1)}, u32[]{:S(2)}, u32[]{:S(2)}) collective-permute-start(bf16[32,512]{1,0:T(8,128)(2,1)S(1)} %product.7), channel_id=1, source_target_pairs={{0,0},{1,3},{2,2},{3,1},{4,4},{5,7},{6,6},{7,5},{8,8},{9,11},{10,1... | collective-permute-start | bytes 98312 | tf_op jit(solution)/shard_map/ppermute | solution.py:303
  24.7 0.1 fusion
  24.8 0.0 collective-permute-done.5.rest_1_
  24.8 0.6 %collective-permute-done.7.rest_2_ = bf16[32,512]{1,0:T(8,128)(2,1)S(1)} collective-permute-done((bf16[32,512]{1,0:T(8,128)(2,1)S(1)}, bf16[32,512]{1,0:T(8,128)(2,1)S(1)}, u32[]{:S(2)}, u32[]{:S(2)}) %collective-permute-start.7) | collective-permute-done | bytes 32800 | tf_op jit(solution)/shard_map/ppermute | solution.py:303
  25.5 0.1 collective-permute-start.10
  25.6 0.1 pad_maximum_fusion
  25.7 1.1 %collective-permute-done.10.received_ref = f32[2,16,512]{2,1,0:T(8,128)S(1)} collective-permute-done((f32[2,16,512]{2,1,0:T(8,128)S(1)}, f32[2,16,512]{2,1,0:T(8,128)S(1)}, u32[]{:S(2)}, u32[]{:S(2)}) %collective-permute-start.10) | collective-permute-done | bytes 65568 | tf_op jit(solution)/shard_map/ppermute | solution.py:313
  26.8 0.8 %finish.1 = bf16[16,512]{1,0:T(8,128)(2,1)} custom-call(s32[1]{0:T(128)} %bitcast.variant_ref, s32[1,16]{1,0:T(1,128)S(1)} %bitcast.8, f32[2,16,512]{2,1,0:T(8,128)S(1)} %get-tuple-element.38.kept_ref, f32[2,16,512]{2,1,0:T(8,128)S(1)} %collective-permute-done.10.received_ref, f32[16,128]{1,0:T(8,128)S(1)} %get-tuple-element.44.cosine_ref, ...), custom_call_target="tpu_custom_call" | custom-call | tf_op jit(solution)/shard_map/finish/pallas_call | solution.py:315
  (14 shorter events, 0.1 us)
Async XLA Ops:
  0.0 12.4 %copy-start.1 = (s32[16]{0:T(128)S(1)}, s32[16]{0:T(128)}, u32[]{:S(2)}) copy-start(s32[16]{0:T(128)} %param.15) | copy-start | bytes 196
  0.0 2.4 %collective-permute-start = (bf16[16,8192]{1,0:T(8,128)(2,1)}, bf16[16,8192]{1,0:T(8,128)(2,1)S(1)}, u32[]{:S(2)}, u32[]{:S(2)}) collective-permute-start(bf16[16,8192]{1,0:T(8,128)(2,1)} %hidden_ref.1), channel_id=1, source_target_pairs={{0,1},{1,0},{2,3},{3,2},{4,5},{5,4},{6,7},{7,6},{8,9},{9,8},{10,11... | collective-permute-start | bytes 786440 | tf_op jit(solution)/shard_map/ppermute | solution.py:255
  0.5 26.4 %copy-start = (s32[16,1]{0,1:T(1,128)S(1)}, s32[16,1]{0,1:T(1,128)}, u32[]{:S(2)}) copy-start(s32[16,1]{0,1:T(1,128)} %param.14) | copy-start | bytes 196
  2.7 9.7 %collective-permute-start.2 = (bf16[1024,512]{1,0:T(8,128)(2,1)S(1)}, bf16[1024,512]{1,0:T(8,128)(2,1)S(1)}, u32[]{:S(2)}, u32[]{:S(2)}) collective-permute-start(bf16[1024,512]{1,0:T(8,128)(2,1)S(1)} %get-tuple-element.33.own_ref), channel_id=1, source_target_pairs={{0,1},{1,0},{2,3},{3,2},{4,5},{5,4},{6,7},{7,6},{8,9},{9,8},{10,11... | collective-permute-start | bytes 3145736 | tf_op jit(solution)/shard_map/ppermute | solution.py:291
  2.8 11.1 %collective-permute-start.1 = (bf16[32,2048]{1,0:T(8,128)(2,1)S(1)}, bf16[32,2048]{1,0:T(8,128)(2,1)S(1)}, u32[]{:S(2)}, u32[]{:S(2)}) collective-permute-start(bf16[32,2048]{1,0:T(8,128)(2,1)S(1)} %get-tuple-element.32), channel_id=1, source_target_pairs={{0,8},{1,15},{2,10},{3,13},{4,12},{5,11},{6,14},{7,9},{8,0},{9,7},... | collective-permute-start | bytes 393224 | tf_op jit(solution)/shard_map/ppermute | solution.py:292
  6.8 11.8 %collective-permute-start.4 = (bf16[32,2048]{1,0:T(8,128)(2,1)S(1)}, bf16[32,2048]{1,0:T(8,128)(2,1)S(1)}, u32[]{:S(2)}, u32[]{:S(2)}) collective-permute-start(bf16[32,2048]{1,0:T(8,128)(2,1)S(1)} %get-tuple-element.35), channel_id=1, source_target_pairs={{0,10},{1,5},{2,8},{3,7},{4,14},{5,1},{6,12},{7,3},{8,2},{9,13},{1... | collective-permute-start | bytes 393224 | tf_op jit(solution)/shard_map/ppermute | solution.py:292
  8.1 11.2 %collective-permute-start.6 = (bf16[32,2048]{1,0:T(8,128)(2,1)S(1)}, bf16[32,2048]{1,0:T(8,128)(2,1)S(1)}, u32[]{:S(2)}, u32[]{:S(2)}) collective-permute-start(bf16[32,2048]{1,0:T(8,128)(2,1)S(1)} %get-tuple-element.36), channel_id=1, source_target_pairs={{0,12},{1,7},{2,14},{3,5},{4,8},{5,3},{6,10},{7,1},{8,4},{9,15},{1... | collective-permute-start | bytes 393224 | tf_op jit(solution)/shard_map/ppermute | solution.py:292
  11.7 11.9 %collective-permute-start.8 = (bf16[32,2048]{1,0:T(8,128)(2,1)S(1)}, bf16[32,2048]{1,0:T(8,128)(2,1)S(1)}, u32[]{:S(2)}, u32[]{:S(2)}) collective-permute-start(bf16[32,2048]{1,0:T(8,128)(2,1)S(1)} %get-tuple-element.37), channel_id=1, source_target_pairs={{0,0},{1,3},{2,2},{3,1},{4,4},{5,7},{6,6},{7,5},{8,8},{9,11},{10,1... | collective-permute-start | bytes 393224 | tf_op jit(solution)/shard_map/ppermute | solution.py:292
  14.3 10.5 %collective-permute-start.3 = (bf16[32,512]{1,0:T(8,128)(2,1)S(1)}, bf16[32,512]{1,0:T(8,128)(2,1)S(1)}, u32[]{:S(2)}, u32[]{:S(2)}) collective-permute-start(bf16[32,512]{1,0:T(8,128)(2,1)S(1)} %product.4), channel_id=1, source_target_pairs={{0,8},{1,15},{2,10},{3,13},{4,12},{5,11},{6,14},{7,9},{8,0},{9,7},... | collective-permute-start | bytes 98312 | tf_op jit(solution)/shard_map/ppermute | solution.py:303
  19.1 5.7 %collective-permute-start.5 = (bf16[32,512]{1,0:T(8,128)(2,1)S(1)}, bf16[32,512]{1,0:T(8,128)(2,1)S(1)}, u32[]{:S(2)}, u32[]{:S(2)}) collective-permute-start(bf16[32,512]{1,0:T(8,128)(2,1)S(1)} %product.5), channel_id=1, source_target_pairs={{0,10},{1,5},{2,8},{3,7},{4,14},{5,1},{6,12},{7,3},{8,2},{9,13},{1... | collective-permute-start | bytes 98312 | tf_op jit(solution)/shard_map/ppermute | solution.py:303
  19.7 5.7 %collective-permute-start.7 = (bf16[32,512]{1,0:T(8,128)(2,1)S(1)}, bf16[32,512]{1,0:T(8,128)(2,1)S(1)}, u32[]{:S(2)}, u32[]{:S(2)}) collective-permute-start(bf16[32,512]{1,0:T(8,128)(2,1)S(1)} %product.6), channel_id=1, source_target_pairs={{0,12},{1,7},{2,14},{3,5},{4,8},{5,3},{6,10},{7,1},{8,4},{9,15},{1... | collective-permute-start | bytes 98312 | tf_op jit(solution)/shard_map/ppermute | solution.py:303
  24.0 1.5 %collective-permute-start.9 = (bf16[32,512]{1,0:T(8,128)(2,1)S(1)}, bf16[32,512]{1,0:T(8,128)(2,1)S(1)}, u32[]{:S(2)}, u32[]{:S(2)}) collective-permute-start(bf16[32,512]{1,0:T(8,128)(2,1)S(1)} %product.7), channel_id=1, source_target_pairs={{0,0},{1,3},{2,2},{3,1},{4,4},{5,7},{6,6},{7,5},{8,8},{9,11},{10,1... | collective-permute-start | bytes 98312 | tf_op jit(solution)/shard_map/ppermute | solution.py:303
  25.5 1.3 %collective-permute-start.10 = (f32[2,16,512]{2,1,0:T(8,128)S(1)}, f32[2,16,512]{2,1,0:T(8,128)S(1)}, u32[]{:S(2)}, u32[]{:S(2)}) collective-permute-start(f32[2,16,512]{2,1,0:T(8,128)S(1)} %get-tuple-element.39), channel_id=1, source_target_pairs={{0,1},{1,0},{2,3},{3,2},{4,5},{5,4},{6,7},{7,6},{8,9},{9,8},{10,11... | collective-permute-start | bytes 196616 | tf_op jit(solution)/shard_map/ppermute | solution.py:313

commit v5 on v3

--- a/solution.py
+++ b/solution.py
@@ -162,7 +162,7 @@
     return (floats * lax.rsqrt(mean_square + epsilon) * gain).astype(jnp.bfloat16)
 
 
-def pieces_kernel(first_ref, core_ref, own_ref, other_ref, gain_ref, *rest):
+def pieces_kernel(orders, piece_ref, core_ref, own_ref, other_ref, gain_ref, *rest):
     outs, normed_ref = rest[:-1], rest[-1]
     row_count = own_ref.shape[0]
     core = core_ref[0]
@@ -171,7 +171,8 @@
     normed_ref[other_rows] = norm_rows(other_ref[...], gain_ref[...])
     for index, out_ref in enumerate(outs):
         piece_width = out_ref.shape[1]
-        start = pl.multiple_of((first_ref[0] ^ index) * piece_width, piece_width)
+        offset = jnp.where(core == 0, orders[0][index] % len(outs), orders[1][index] % len(outs))
+        start = pl.multiple_of((piece_ref[0] ^ offset) * piece_width, piece_width)
         out_ref[...] = normed_ref[:, pl.ds(start, piece_width)]
 
 
@@ -179,11 +180,18 @@
     out_ref[...] = jnp.dot(rows_ref[...], weight_ref[...], preferred_element_type=jnp.float32).astype(out_ref.dtype)
 
 
-def sum_kernel(core_ref, far_a, near_a, far_b, near_b, kept_ref, sent_ref, total_ref):
-    total_ref[0] = far_a[...].astype(jnp.float32) + far_b[...].astype(jnp.float32)
-    total_ref[1] = near_a[...].astype(jnp.float32) + near_b[...].astype(jnp.float32)
+def sum_kernel(orders, core_ref, *rest):
+    parts, (kept_ref, sent_ref, total_ref) = rest[:-3], rest[-3:]
+    core = core_ref[0]
+    for member, order in enumerate(orders):
+
+        @pl.when(core == member)
+        def _(order=order):
+            for kind in range(2):
+                chosen = [part for part, distance in zip(parts, order) if (distance < len(order)) == bool(kind)]
+                total_ref[kind] = sum((part[...].astype(jnp.float32) for part in chosen), jnp.zeros(total_ref.shape[1:], jnp.float32))
+
     row_count = kept_ref.shape[1]
-    core = core_ref[0]
     kept_ref[...] = total_ref[:, pl.ds(pl.multiple_of(core * row_count, row_count), row_count)]
     sent_ref[...] = total_ref[:, pl.ds(pl.multiple_of((1 - core) * row_count, row_count), row_count)]
 
@@ -231,11 +239,11 @@
     piece = lax.div(lax.rem(place, OWNERS), 2)
     variant = lax.div(place, OWNERS)
     swap = [(index, index ^ 1) for index in range(device_count)]
-    far = pieces
-    steps = [(0, far, far + 2), (1, 1, 3), (1, far + 1, far + 3), (0, 0, 2)]
-    routes = [
-        [(index, index ^ (2 * distances[index % 2])) for index in range(device_count)] for _, *distances in steps
-    ]
+    orders = ((4, 5, 6, 0), (7, 2, 3, 1))
+    steps = list(zip(*orders))
+
+    def route(distances, cross):
+        return [(index, (index ^ (2 * distances[index % 2])) ^ cross) for index in range(device_count)]
 
     slice_shape, group_shape = (slice_rows, column_count), delta_scales.shape[2:]
     own_codes, own_scales, own_zeros = delta_codes[0, 0], delta_scales[0, 0], delta_zeros[0, 0]
@@ -259,15 +267,15 @@
         (other_hidden, other_scales, other_zeros, own_codes, normed)
     )
     other_codes = lax.ppermute(codes, "variant", swap)
-    first, second = pl.pallas_call(
-        pieces_kernel,
-        out_shape=[jax.ShapeDtypeStruct((2 * row_count, width // pieces), jnp.bfloat16)] * 2,
+    outgoing = pl.pallas_call(
+        functools.partial(pieces_kernel, orders),
+        out_shape=[jax.ShapeDtypeStruct((2 * row_count, width // pieces), jnp.bfloat16)] * len(steps),
         in_specs=[SMEM, SMEM, VMEM, VMEM, VMEM],
-        out_specs=[VMEM] * 2,
+        out_specs=[VMEM] * len(steps),
         scratch_shapes=[pltpu.VMEM((2 * row_count, width), jnp.bfloat16)],
         compiler_params=pltpu.CompilerParams(vmem_limit_bytes=16 << 20),
         name="pieces",
-    )((piece ^ (2 * core))[None], core[None], normed, other_hidden, gains)
+    )(piece[None], core[None], normed, other_hidden, gains)
     weight = pl.pallas_call(
         weight_kernel,
         out_shape=jax.ShapeDtypeStruct((2 * slice_rows, column_count), jnp.bfloat16),
@@ -294,7 +302,7 @@
         other_zeros,
     )
     weight, positions = lax.optimization_barrier((weight, positions))
-    incoming = [lax.ppermute((first, second)[index], "variant", route) for (index, _, _), route in zip(steps, routes)]
+    incoming = [lax.ppermute(rows, "variant", route(distances, 0)) for rows, distances in zip(outgoing, steps)]
     parts = [None] * len(steps)
     for step in range(len(steps)):
         product = pl.pallas_call(
@@ -305,9 +313,9 @@
             compiler_params=pltpu.CompilerParams(vmem_limit_bytes=16 << 20),
             name="product",
         )(incoming[step], weight)
-        parts[step] = lax.ppermute(product, "variant", routes[step])
+        parts[step] = lax.ppermute(product, "variant", route(steps[step], 1))
     kept, sent = pl.pallas_call(
-        sum_kernel,
+        functools.partial(sum_kernel, orders[::-1]),
         out_shape=[jax.ShapeDtypeStruct((2, row_count, column_count), jnp.float32)] * 2,
         in_specs=[SMEM] + [VMEM] * len(parts),
         out_specs=[VMEM] * 2,

time: 29.3 us -> 27.4 us (0.935)
  waiting for transfers between devices: 10.9 us -> 6.43 us
  starting transfers between devices: 11.3 us -> 13.9 us
    ppermute x8, waiting for transfers between devices: 9.74 us -> 5.59 us  [the longest x4 3.45 us: paired(): lax.ppermute(rows, 'variant', route(distances, 0))]
    ppermute x8, starting transfers between devices: 10.1 us -> 12 us  [the longest x4 9.6 us: paired(): lax.ppermute(rows, 'variant', route(distances, 0))]
    ppermute x1, starting transfers between devices: 0.07 us -> 0.82 us  [paired(): received = lax.ppermute(sent, 'variant', swap)]
    ppermute x1, waiting for transfers between devices: 1.16 us -> 0.83 us  [paired(): received = lax.ppermute(sent, 'variant', swap)]
  transfers between devices with their start and end apart: 13 -> 13, of which waited for: 4 -> 4; matrix products, arithmetic and copies ran while one was open for 1% -> 1% of each run, Pallas kernels for 19% -> 21%
where the time goes in v5:
time: 27.4 us; the launch traced here: 27.1 us
  starting transfers between devices  13.9 us (51%)
  waiting for transfers between devices  6.43 us (23%)
  Pallas kernels  6.39 us (23%)
    ppermute x4, starting transfers between devices, paired(): lax.ppermute(rows, 'variant', route(distances, 0))  9.6 us
    ppermute x4, waiting for transfers between devices, paired(): lax.ppermute(rows, 'variant', route(distances, 0))  3.45 us
    ppermute x4, starting transfers between devices, paired(): parts[step] = lax.ppermute(product, 'variant', route(steps[step], 1))  2.4 us
    pallas_call x1, Pallas kernels, paired(): pl.pallas_call(weight_kernel, out_shape=jax.ShapeDtypeStruct((2 * slice_r...  2.32 us
    ppermute x4, waiting for transfers between devices, paired(): parts[step] = lax.ppermute(product, 'variant', route(steps[step], 1))  2.14 us
    pallas_call x4, Pallas kernels, paired(): pl.pallas_call(product_kernel, out_shape=jax.ShapeDtypeStruct((2 * row_co...  1.79 us
    pallas_call x1, Pallas kernels, paired(): pl.pallas_call(norm_kernel, out_shape=[jax.ShapeDtypeStruct((row_count, w...  1.22 us
    ppermute x1, waiting for transfers between devices, paired(): received = lax.ppermute(sent, 'variant', swap)  0.83 us
  transfers between devices with their start and end apart: 13, of which 4 were waited for; matrix products, arithmetic and copies ran while one was open for 1% of the time, Pallas kernels for 21%

profile of v5, /device:TPU:0, one launch (start us, length us, event | category | flops | bytes accessed | tf_op | source)
XLA Modules:
  0.0 27.1 jit_solution(2189331106124534546)
XLA Ops:
  0.0 0.5 %collective-permute-start = (bf16[16,8192]{1,0:T(8,128)(2,1)}, bf16[16,8192]{1,0:T(8,128)(2,1)S(1)}, u32[]{:S(2)}, u32[]{:S(2)}) collective-permute-start(bf16[16,8192]{1,0:T(8,128)(2,1)} %rows_ref.1), channel_id=1, source_target_pairs={{0,1},{1,0},{2,3},{3,2},{4,5},{5,4},{6,7},{7,6},{8,9},{9,8},{10,11... | collective-permute-start | bytes 786440 | tf_op jit(solution)/shard_map/ppermute | solution.py:250
  0.5 0.5 %collective-permute-start.2 = (f32[8,512]{1,0:T(8,128)}, f32[8,512]{1,0:T(8,128)S(1)}, u32[]{:S(2)}, u32[]{:S(2)}) collective-permute-start(f32[8,512]{1,0:T(8,128)} %bitcast.13), channel_id=1, source_target_pairs={{0,1},{1,0},{2,3},{3,2},{4,5},{5,4},{6,7},{7,6},{8,9},{9,8},{10,11... | collective-permute-start | bytes 49160 | tf_op jit(solution)/shard_map/ppermute | solution.py:252
  1.0 1.2 %norm.1 = (bf16[16,8192]{1,0:T(8,128)(2,1)S(1)}, f32[1,8192]{1,0:T(1,128)S(1)}) custom-call(bf16[16,8192]{1,0:T(8,128)(2,1)} %rows_ref.1, bf16[8192]{0:T(1024)(128)(2,1)} %gain_ref.1), custom_call_target="tpu_custom_call" | custom-call | tf_op jit(solution)/shard_map/norm/pallas_call | solution.py:253
  2.2 0.1 collective-permute-start.4
  2.4 0.3 pieces.1
  2.6 4.1 %collective-permute-start.3 = (bf16[32,2048]{1,0:T(8,128)(2,1)S(1)}, bf16[32,2048]{1,0:T(8,128)(2,1)S(1)}, u32[]{:S(2)}, u32[]{:S(2)}) collective-permute-start(bf16[32,2048]{1,0:T(8,128)(2,1)S(1)} %get-tuple-element.24), channel_id=1, source_target_pairs={{0,8},{1,15},{2,10},{3,13},{4,12},{5,11},{6,14},{7,9},{8,0},{9,7},... | collective-permute-start | bytes 393224 | tf_op jit(solution)/shard_map/ppermute | solution.py:305
  6.7 1.3 %collective-permute-start.6 = (bf16[32,2048]{1,0:T(8,128)(2,1)S(1)}, bf16[32,2048]{1,0:T(8,128)(2,1)S(1)}, u32[]{:S(2)}, u32[]{:S(2)}) collective-permute-start(bf16[32,2048]{1,0:T(8,128)(2,1)S(1)} %get-tuple-element.29), channel_id=1, source_target_pairs={{0,10},{1,5},{2,8},{3,7},{4,14},{5,1},{6,12},{7,3},{8,2},{9,13},{1... | collective-permute-start | bytes 393224 | tf_op jit(solution)/shard_map/ppermute | solution.py:305
  8.0 3.6 %collective-permute-start.8 = (bf16[32,2048]{1,0:T(8,128)(2,1)S(1)}, bf16[32,2048]{1,0:T(8,128)(2,1)S(1)}, u32[]{:S(2)}, u32[]{:S(2)}) collective-permute-start(bf16[32,2048]{1,0:T(8,128)(2,1)S(1)} %get-tuple-element.30), channel_id=1, source_target_pairs={{0,12},{1,7},{2,14},{3,5},{4,8},{5,3},{6,10},{7,1},{8,4},{9,15},{1... | collective-permute-start | bytes 393224 | tf_op jit(solution)/shard_map/ppermute | solution.py:305
  11.6 0.7 %collective-permute-start.10 = (bf16[32,2048]{1,0:T(8,128)(2,1)S(1)}, bf16[32,2048]{1,0:T(8,128)(2,1)S(1)}, u32[]{:S(2)}, u32[]{:S(2)}) collective-permute-start(bf16[32,2048]{1,0:T(8,128)(2,1)S(1)} %get-tuple-element.31), channel_id=1, source_target_pairs={{0,0},{1,3},{2,2},{3,1},{4,4},{5,7},{6,6},{7,5},{8,8},{9,11},{10,1... | collective-permute-start | bytes 393224 | tf_op jit(solution)/shard_map/ppermute | solution.py:305
  12.3 2.3 %weight.1.weight_ref = bf16[2048,512]{1,0:T(8,128)(2,1)S(1)} custom-call(s32[1]{0:T(128)} %bitcast.2.core_ref, s32[1]{0:T(128)} %bitcast.7.first_ref, bf16[1024,512]{1,0:T(8,128)(2,1)} %bitcast.10, f32[8,512]{1,0:T(8,128)} %bitcast.12, f32[8,512]{1,0:T(8,128)} %bitcast.14, bf16[8192,512]{1,0:T(8,128)(2,1)} %base_ref.1, ...), custom_call_target="tpu_custom_call" | custom-call | tf_op jit(solution)/shard_map/weight/pallas_call | solution.py:279
  14.6 0.4 %product.4 = bf16[32,512]{1,0:T(8,128)(2,1)S(1)} custom-call(bf16[32,2048]{1,0:T(8,128)(2,1)S(1)} %collective-permute-done.3.rows_ref, bf16[2048,512]{1,0:T(8,128)(2,1)S(1)} %weight.1.weight_ref), custom_call_target="tpu_custom_call" | custom-call | tf_op jit(solution)/shard_map/product/pallas_call | solution.py:308
  15.1 3.4 %collective-permute-done.6.rows_ref = bf16[32,2048]{1,0:T(8,128)(2,1)S(1)} collective-permute-done((bf16[32,2048]{1,0:T(8,128)(2,1)S(1)}, bf16[32,2048]{1,0:T(8,128)(2,1)S(1)}, u32[]{:S(2)}, u32[]{:S(2)}) %collective-permute-start.6) | collective-permute-done | bytes 131104 | tf_op jit(solution)/shard_map/ppermute | solution.py:305
  18.5 0.4 %product.5 = bf16[32,512]{1,0:T(8,128)(2,1)S(1)} custom-call(bf16[32,2048]{1,0:T(8,128)(2,1)S(1)} %collective-permute-done.6.rows_ref, bf16[2048,512]{1,0:T(8,128)(2,1)S(1)} %weight.1.weight_ref), custom_call_target="tpu_custom_call" | custom-call | tf_op jit(solution)/shard_map/product/pallas_call | solution.py:308
  19.0 0.5 %collective-permute-start.7 = (bf16[32,512]{1,0:T(8,128)(2,1)S(1)}, bf16[32,512]{1,0:T(8,128)(2,1)S(1)}, u32[]{:S(2)}, u32[]{:S(2)}) collective-permute-start(bf16[32,512]{1,0:T(8,128)(2,1)S(1)} %product.5), channel_id=1, source_target_pairs={{0,11},{1,4},{2,9},{3,6},{4,15},{5,0},{6,13},{7,2},{8,3},{9,12},{1... | collective-permute-start | bytes 98312 | tf_op jit(solution)/shard_map/ppermute | solution.py:316
  19.5 0.4 %product.6 = bf16[32,512]{1,0:T(8,128)(2,1)S(1)} custom-call(bf16[32,2048]{1,0:T(8,128)(2,1)S(1)} %collective-permute-done.8.rows_ref, bf16[2048,512]{1,0:T(8,128)(2,1)S(1)} %weight.1.weight_ref), custom_call_target="tpu_custom_call" | custom-call | tf_op jit(solution)/shard_map/product/pallas_call | solution.py:308
  20.0 0.5 %collective-permute-start.9 = (bf16[32,512]{1,0:T(8,128)(2,1)S(1)}, bf16[32,512]{1,0:T(8,128)(2,1)S(1)}, u32[]{:S(2)}, u32[]{:S(2)}) collective-permute-start(bf16[32,512]{1,0:T(8,128)(2,1)S(1)} %product.6), channel_id=1, source_target_pairs={{0,13},{1,6},{2,15},{3,4},{4,9},{5,2},{6,11},{7,0},{8,5},{9,14},{1... | collective-permute-start | bytes 98312 | tf_op jit(solution)/shard_map/ppermute | solution.py:316
  20.5 0.4 %product.7 = bf16[32,512]{1,0:T(8,128)(2,1)S(1)} custom-call(bf16[32,2048]{1,0:T(8,128)(2,1)S(1)} %collective-permute-done.10.rows_ref, bf16[2048,512]{1,0:T(8,128)(2,1)S(1)} %weight.1.weight_ref), custom_call_target="tpu_custom_call" | custom-call | tf_op jit(solution)/shard_map/product/pallas_call | solution.py:308
  21.0 1.3 %collective-permute-start.11 = (bf16[32,512]{1,0:T(8,128)(2,1)S(1)}, bf16[32,512]{1,0:T(8,128)(2,1)S(1)}, u32[]{:S(2)}, u32[]{:S(2)}) collective-permute-start(bf16[32,512]{1,0:T(8,128)(2,1)S(1)} %product.7), channel_id=1, source_target_pairs={{0,1},{1,2},{2,3},{3,0},{4,5},{5,6},{6,7},{7,4},{8,9},{9,10},{10,1... | collective-permute-start | bytes 98312 | tf_op jit(solution)/shard_map/ppermute | solution.py:316
  22.3 0.1 fusion
  22.4 1.8 %collective-permute-done.9.rest_2_ = bf16[32,512]{1,0:T(8,128)(2,1)S(1)} collective-permute-done((bf16[32,512]{1,0:T(8,128)(2,1)S(1)}, bf16[32,512]{1,0:T(8,128)(2,1)S(1)}, u32[]{:S(2)}, u32[]{:S(2)}) %collective-permute-start.9) | collective-permute-done | bytes 32800 | tf_op jit(solution)/shard_map/ppermute | solution.py:316
  24.3 0.3 %collective-permute-done.11.rest_3_ = bf16[32,512]{1,0:T(8,128)(2,1)S(1)} collective-permute-done((bf16[32,512]{1,0:T(8,128)(2,1)S(1)}, bf16[32,512]{1,0:T(8,128)(2,1)S(1)}, u32[]{:S(2)}, u32[]{:S(2)}) %collective-permute-start.11) | collective-permute-done | bytes 32800 | tf_op jit(solution)/shard_map/ppermute | solution.py:316
  24.6 0.8 %collective-permute-start.12 = (f32[2,16,512]{2,1,0:T(8,128)S(1)}, f32[2,16,512]{2,1,0:T(8,128)S(1)}, u32[]{:S(2)}, u32[]{:S(2)}) collective-permute-start(f32[2,16,512]{2,1,0:T(8,128)S(1)} %get-tuple-element.33), channel_id=1, source_target_pairs={{0,1},{1,0},{2,3},{3,2},{4,5},{5,4},{6,7},{7,6},{8,9},{9,8},{10,11... | collective-permute-start | bytes 196616 | tf_op jit(solution)/shard_map/ppermute | solution.py:326
  25.5 0.8 %collective-permute-done.12.received_ref = f32[2,16,512]{2,1,0:T(8,128)S(1)} collective-permute-done((f32[2,16,512]{2,1,0:T(8,128)S(1)}, f32[2,16,512]{2,1,0:T(8,128)S(1)}, u32[]{:S(2)}, u32[]{:S(2)}) %collective-permute-start.12) | collective-permute-done | bytes 65568 | tf_op jit(solution)/shard_map/ppermute | solution.py:326
  26.3 0.8 %finish.1 = bf16[16,512]{1,0:T(8,128)(2,1)} custom-call(s32[1]{0:T(128)} %bitcast.variant_ref, s32[1,16]{1,0:T(1,128)S(1)} %bitcast.8, f32[2,16,512]{2,1,0:T(8,128)S(1)} %get-tuple-element.32.kept_ref, f32[2,16,512]{2,1,0:T(8,128)S(1)} %collective-permute-done.12.received_ref, f32[16,128]{1,0:T(8,128)S(1)} %get-tuple-element.38.cosine_ref, ...), custom_call_target="tpu_custom_call" | custom-call | tf_op jit(solution)/shard_map/finish/pallas_call | solution.py:328
  (19 shorter events, 0.2 us)
Async XLA Ops:
  0.0 2.2 %collective-permute-start = (bf16[16,8192]{1,0:T(8,128)(2,1)}, bf16[16,8192]{1,0:T(8,128)(2,1)S(1)}, u32[]{:S(2)}, u32[]{:S(2)}) collective-permute-start(bf16[16,8192]{1,0:T(8,128)(2,1)} %rows_ref.1), channel_id=1, source_target_pairs={{0,1},{1,0},{2,3},{3,2},{4,5},{5,4},{6,7},{7,6},{8,9},{9,8},{10,11... | collective-permute-start | bytes 786440 | tf_op jit(solution)/shard_map/ppermute | solution.py:250
  0.5 1.7 %collective-permute-start.1 = (f32[8,512]{1,0:T(8,128)}, f32[8,512]{1,0:T(8,128)S(1)}, u32[]{:S(2)}, u32[]{:S(2)}) collective-permute-start(f32[8,512]{1,0:T(8,128)} %bitcast.11), channel_id=1, source_target_pairs={{0,1},{1,0},{2,3},{3,2},{4,5},{5,4},{6,7},{7,6},{8,9},{9,8},{10,11... | collective-permute-start | bytes 49160 | tf_op jit(solution)/shard_map/ppermute | solution.py:251
  0.5 1.7 %collective-permute-start.2 = (f32[8,512]{1,0:T(8,128)}, f32[8,512]{1,0:T(8,128)S(1)}, u32[]{:S(2)}, u32[]{:S(2)}) collective-permute-start(f32[8,512]{1,0:T(8,128)} %bitcast.13), channel_id=1, source_target_pairs={{0,1},{1,0},{2,3},{3,2},{4,5},{5,4},{6,7},{7,6},{8,9},{9,8},{10,11... | collective-permute-start | bytes 49160 | tf_op jit(solution)/shard_map/ppermute | solution.py:252
  2.2 10.0 %collective-permute-start.4 = (bf16[1024,512]{1,0:T(8,128)(2,1)}, bf16[1024,512]{1,0:T(8,128)(2,1)S(1)}, u32[]{:S(2)}, u32[]{:S(2)}) collective-permute-start(bf16[1024,512]{1,0:T(8,128)(2,1)} %bitcast.9), channel_id=1, source_target_pairs={{0,1},{1,0},{2,3},{3,2},{4,5},{5,4},{6,7},{7,6},{8,9},{9,8},{10,11... | collective-permute-start | bytes 3145736 | tf_op jit(solution)/shard_map/ppermute | solution.py:269
  2.6 12.0 %collective-permute-start.3 = (bf16[32,2048]{1,0:T(8,128)(2,1)S(1)}, bf16[32,2048]{1,0:T(8,128)(2,1)S(1)}, u32[]{:S(2)}, u32[]{:S(2)}) collective-permute-start(bf16[32,2048]{1,0:T(8,128)(2,1)S(1)} %get-tuple-element.24), channel_id=1, source_target_pairs={{0,8},{1,15},{2,10},{3,13},{4,12},{5,11},{6,14},{7,9},{8,0},{9,7},... | collective-permute-start | bytes 393224 | tf_op jit(solution)/shard_map/ppermute | solution.py:305
  6.7 11.8 %collective-permute-start.6 = (bf16[32,2048]{1,0:T(8,128)(2,1)S(1)}, bf16[32,2048]{1,0:T(8,128)(2,1)S(1)}, u32[]{:S(2)}, u32[]{:S(2)}) collective-permute-start(bf16[32,2048]{1,0:T(8,128)(2,1)S(1)} %get-tuple-element.29), channel_id=1, source_target_pairs={{0,10},{1,5},{2,8},{3,7},{4,14},{5,1},{6,12},{7,3},{8,2},{9,13},{1... | collective-permute-start | bytes 393224 | tf_op jit(solution)/shard_map/ppermute | solution.py:305
  8.0 11.5 %collective-permute-start.8 = (bf16[32,2048]{1,0:T(8,128)(2,1)S(1)}, bf16[32,2048]{1,0:T(8,128)(2,1)S(1)}, u32[]{:S(2)}, u32[]{:S(2)}) collective-permute-start(bf16[32,2048]{1,0:T(8,128)(2,1)S(1)} %get-tuple-element.30), channel_id=1, source_target_pairs={{0,12},{1,7},{2,14},{3,5},{4,8},{5,3},{6,10},{7,1},{8,4},{9,15},{1... | collective-permute-start | bytes 393224 | tf_op jit(solution)/shard_map/ppermute | solution.py:305
  11.6 8.9 %collective-permute-start.10 = (bf16[32,2048]{1,0:T(8,128)(2,1)S(1)}, bf16[32,2048]{1,0:T(8,128)(2,1)S(1)}, u32[]{:S(2)}, u32[]{:S(2)}) collective-permute-start(bf16[32,2048]{1,0:T(8,128)(2,1)S(1)} %get-tuple-element.31), channel_id=1, source_target_pairs={{0,0},{1,3},{2,2},{3,1},{4,4},{5,7},{6,6},{7,5},{8,8},{9,11},{10,1... | collective-permute-start | bytes 393224 | tf_op jit(solution)/shard_map/ppermute | solution.py:305
  12.3 10.0 %copy-start.1 = (s32[16]{0:T(128)S(1)}, s32[16]{0:T(128)}, u32[]{:S(2)}) copy-start(s32[16]{0:T(128)} %param.15) | copy-start | bytes 196
  12.3 14.1 %copy-start = (s32[16,1]{0,1:T(1,128)S(1)}, s32[16,1]{0,1:T(1,128)}, u32[]{:S(2)}) copy-start(s32[16,1]{0,1:T(1,128)} %param.14) | copy-start | bytes 196
  15.1 7.3 %collective-permute-start.5 = (bf16[32,512]{1,0:T(8,128)(2,1)S(1)}, bf16[32,512]{1,0:T(8,128)(2,1)S(1)}, u32[]{:S(2)}, u32[]{:S(2)}) collective-permute-start(bf16[32,512]{1,0:T(8,128)(2,1)S(1)} %product.4), channel_id=1, source_target_pairs={{0,9},{1,14},{2,11},{3,12},{4,13},{5,10},{6,15},{7,8},{8,1},{9,6},... | collective-permute-start | bytes 98312 | tf_op jit(solution)/shard_map/ppermute | solution.py:316
  19.0 3.4 %collective-permute-start.7 = (bf16[32,512]{1,0:T(8,128)(2,1)S(1)}, bf16[32,512]{1,0:T(8,128)(2,1)S(1)}, u32[]{:S(2)}, u32[]{:S(2)}) collective-permute-start(bf16[32,512]{1,0:T(8,128)(2,1)S(1)} %product.5), channel_id=1, source_target_pairs={{0,11},{1,4},{2,9},{3,6},{4,15},{5,0},{6,13},{7,2},{8,3},{9,12},{1... | collective-permute-start | bytes 98312 | tf_op jit(solution)/shard_map/ppermute | solution.py:316
  20.0 4.3 %collective-permute-start.9 = (bf16[32,512]{1,0:T(8,128)(2,1)S(1)}, bf16[32,512]{1,0:T(8,128)(2,1)S(1)}, u32[]{:S(2)}, u32[]{:S(2)}) collective-permute-start(bf16[32,512]{1,0:T(8,128)(2,1)S(1)} %product.6), channel_id=1, source_target_pairs={{0,13},{1,6},{2,15},{3,4},{4,9},{5,2},{6,11},{7,0},{8,5},{9,14},{1... | collective-permute-start | bytes 98312 | tf_op jit(solution)/shard_map/ppermute | solution.py:316
  21.0 3.6 %collective-permute-start.11 = (bf16[32,512]{1,0:T(8,128)(2,1)S(1)}, bf16[32,512]{1,0:T(8,128)(2,1)S(1)}, u32[]{:S(2)}, u32[]{:S(2)}) collective-permute-start(bf16[32,512]{1,0:T(8,128)(2,1)S(1)} %product.7), channel_id=1, source_target_pairs={{0,1},{1,2},{2,3},{3,0},{4,5},{5,6},{6,7},{7,4},{8,9},{9,10},{10,1... | collective-permute-start | bytes 98312 | tf_op jit(solution)/shard_map/ppermute | solution.py:316
  24.6 1.7 %collective-permute-start.12 = (f32[2,16,512]{2,1,0:T(8,128)S(1)}, f32[2,16,512]{2,1,0:T(8,128)S(1)}, u32[]{:S(2)}, u32[]{:S(2)}) collective-permute-start(f32[2,16,512]{2,1,0:T(8,128)S(1)} %get-tuple-element.33), channel_id=1, source_target_pairs={{0,1},{1,0},{2,3},{3,2},{4,5},{5,4},{6,7},{7,6},{8,9},{9,8},{10,11... | collective-permute-start | bytes 196616 | tf_op jit(solution)/shard_map/ppermute | solution.py:326

commit v6 on v5

--- a/solution.py
+++ b/solution.py
@@ -239,7 +239,7 @@
     piece = lax.div(lax.rem(place, OWNERS), 2)
     variant = lax.div(place, OWNERS)
     swap = [(index, index ^ 1) for index in range(device_count)]
-    orders = ((4, 5, 6, 0), (7, 2, 3, 1))
+    orders = ((7, 5, 4, 0), (6, 3, 2, 1))
     steps = list(zip(*orders))
 
     def route(distances, cross):

time: 27.4 us -> 26.9 us (0.982)
  starting transfers between devices: 13.9 us -> 12.4 us
  waiting for transfers between devices: 6.43 us -> 7.54 us
    ppermute x4, starting transfers between devices: 2.4 us -> 1.62 us  [paired(): parts[step] = lax.ppermute(product, 'variant', route(steps[step], 1))]
    ppermute x1, starting transfers between devices: 0.82 us -> 0.07 us  [paired(): received = lax.ppermute(sent, 'variant', swap)]
    ppermute x4, waiting for transfers between devices: 2.14 us -> 2.77 us  [paired(): parts[step] = lax.ppermute(product, 'variant', route(steps[step], 1))]
    ppermute x1, waiting for transfers between devices: 0.83 us -> 1.16 us  [paired(): received = lax.ppermute(sent, 'variant', swap)]
  transfers between devices with their start and end apart: 13 -> 13, of which waited for: 4 -> 3; matrix products, arithmetic and copies ran while one was open for 1% -> 1% of each run, Pallas kernels for 21% -> 21%
where the time goes in v6:
time: 26.9 us; the launch traced here: 26.7 us
  starting transfers between devices  12.4 us (46%)
  waiting for transfers between devices  7.54 us (28%)
  Pallas kernels  6.4 us (24%)
    ppermute x4, starting transfers between devices, paired(): lax.ppermute(rows, 'variant', route(distances, 0))  9.57 us
    ppermute x4, waiting for transfers between devices, paired(): lax.ppermute(rows, 'variant', route(distances, 0))  3.59 us
    ppermute x4, waiting for transfers between devices, paired(): parts[step] = lax.ppermute(product, 'variant', route(steps[step], 1))  2.77 us
    pallas_call x1, Pallas kernels, paired(): pl.pallas_call(weight_kernel, out_shape=jax.ShapeDtypeStruct((2 * slice_r...  2.32 us
    pallas_call x4, Pallas kernels, paired(): pl.pallas_call(product_kernel, out_shape=jax.ShapeDtypeStruct((2 * row_co...  1.8 us
    ppermute x4, starting transfers between devices, paired(): parts[step] = lax.ppermute(product, 'variant', route(steps[step], 1))  1.62 us
    pallas_call x1, Pallas kernels, paired(): pl.pallas_call(norm_kernel, out_shape=[jax.ShapeDtypeStruct((row_count, w...  1.22 us
    ppermute x1, waiting for transfers between devices, paired(): received = lax.ppermute(sent, 'variant', swap)  1.16 us
  transfers between devices with their start and end apart: 13, of which 3 were waited for; matrix products, arithmetic and copies ran while one was open for 1% of the time, Pallas kernels for 21%

profile of v6, /device:TPU:0, one launch (start us, length us, event | category | flops | bytes accessed | tf_op | source)
XLA Modules:
  0.0 26.7 jit_solution(15994400087087300108)
XLA Ops:
  0.0 0.5 %collective-permute-start = (bf16[16,8192]{1,0:T(8,128)(2,1)}, bf16[16,8192]{1,0:T(8,128)(2,1)S(1)}, u32[]{:S(2)}, u32[]{:S(2)}) collective-permute-start(bf16[16,8192]{1,0:T(8,128)(2,1)} %rows_ref.1), channel_id=1, source_target_pairs={{0,1},{1,0},{2,3},{3,2},{4,5},{5,4},{6,7},{7,6},{8,9},{9,8},{10,11... | collective-permute-start | bytes 786440 | tf_op jit(solution)/shard_map/ppermute | solution.py:250
  0.5 0.1 collective-permute-start.1
  0.5 0.5 %collective-permute-start.2 = (f32[8,512]{1,0:T(8,128)}, f32[8,512]{1,0:T(8,128)S(1)}, u32[]{:S(2)}, u32[]{:S(2)}) collective-permute-start(f32[8,512]{1,0:T(8,128)} %bitcast.13), channel_id=1, source_target_pairs={{0,1},{1,0},{2,3},{3,2},{4,5},{5,4},{6,7},{7,6},{8,9},{9,8},{10,11... | collective-permute-start | bytes 49160 | tf_op jit(solution)/shard_map/ppermute | solution.py:252
  1.0 1.2 %norm.1 = (bf16[16,8192]{1,0:T(8,128)(2,1)S(1)}, f32[1,8192]{1,0:T(1,128)S(1)}) custom-call(bf16[16,8192]{1,0:T(8,128)(2,1)} %rows_ref.1, bf16[8192]{0:T(1024)(128)(2,1)} %gain_ref.1), custom_call_target="tpu_custom_call" | custom-call | tf_op jit(solution)/shard_map/norm/pallas_call | solution.py:253
  2.2 0.1 collective-permute-start.4
  2.4 0.3 pieces.1
  2.6 6.0 %collective-permute-start.3 = (bf16[32,2048]{1,0:T(8,128)(2,1)S(1)}, bf16[32,2048]{1,0:T(8,128)(2,1)S(1)}, u32[]{:S(2)}, u32[]{:S(2)}) collective-permute-start(bf16[32,2048]{1,0:T(8,128)(2,1)S(1)} %get-tuple-element.24), channel_id=1, source_target_pairs={{0,14},{1,13},{2,12},{3,15},{4,10},{5,9},{6,8},{7,11},{8,6},{9,5},... | collective-permute-start | bytes 393224 | tf_op jit(solution)/shard_map/ppermute | solution.py:305
  8.7 2.9 %collective-permute-start.8 = (bf16[32,2048]{1,0:T(8,128)(2,1)S(1)}, bf16[32,2048]{1,0:T(8,128)(2,1)S(1)}, u32[]{:S(2)}, u32[]{:S(2)}) collective-permute-start(bf16[32,2048]{1,0:T(8,128)(2,1)S(1)} %get-tuple-element.30), channel_id=1, source_target_pairs={{0,8},{1,5},{2,10},{3,7},{4,12},{5,1},{6,14},{7,3},{8,0},{9,13},{1... | collective-permute-start | bytes 393224 | tf_op jit(solution)/shard_map/ppermute | solution.py:305
  11.6 0.7 %collective-permute-start.10 = (bf16[32,2048]{1,0:T(8,128)(2,1)S(1)}, bf16[32,2048]{1,0:T(8,128)(2,1)S(1)}, u32[]{:S(2)}, u32[]{:S(2)}) collective-permute-start(bf16[32,2048]{1,0:T(8,128)(2,1)S(1)} %get-tuple-element.31), channel_id=1, source_target_pairs={{0,0},{1,3},{2,2},{3,1},{4,4},{5,7},{6,6},{7,5},{8,8},{9,11},{10,1... | collective-permute-start | bytes 393224 | tf_op jit(solution)/shard_map/ppermute | solution.py:305
  12.3 2.3 %weight.1.weight_ref = bf16[2048,512]{1,0:T(8,128)(2,1)S(1)} custom-call(s32[1]{0:T(128)} %bitcast.2.core_ref, s32[1]{0:T(128)} %bitcast.7.first_ref, bf16[1024,512]{1,0:T(8,128)(2,1)} %bitcast.10, f32[8,512]{1,0:T(8,128)} %bitcast.12, f32[8,512]{1,0:T(8,128)} %bitcast.14, bf16[8192,512]{1,0:T(8,128)(2,1)} %base_ref.1, ...), custom_call_target="tpu_custom_call" | custom-call | tf_op jit(solution)/shard_map/weight/pallas_call | solution.py:279
  14.6 0.4 %product.4 = bf16[32,512]{1,0:T(8,128)(2,1)S(1)} custom-call(bf16[32,2048]{1,0:T(8,128)(2,1)S(1)} %collective-permute-done.3.rows_ref, bf16[2048,512]{1,0:T(8,128)(2,1)S(1)} %weight.1.weight_ref), custom_call_target="tpu_custom_call" | custom-call | tf_op jit(solution)/shard_map/product/pallas_call | solution.py:308
  15.1 0.8 %collective-permute-start.5 = (bf16[32,512]{1,0:T(8,128)(2,1)S(1)}, bf16[32,512]{1,0:T(8,128)(2,1)S(1)}, u32[]{:S(2)}, u32[]{:S(2)}) collective-permute-start(bf16[32,512]{1,0:T(8,128)(2,1)S(1)} %product.4), channel_id=1, source_target_pairs={{0,15},{1,12},{2,13},{3,14},{4,11},{5,8},{6,9},{7,10},{8,7},{9,4},... | collective-permute-start | bytes 98312 | tf_op jit(solution)/shard_map/ppermute | solution.py:316
  15.8 3.6 %collective-permute-done.6.rows_ref = bf16[32,2048]{1,0:T(8,128)(2,1)S(1)} collective-permute-done((bf16[32,2048]{1,0:T(8,128)(2,1)S(1)}, bf16[32,2048]{1,0:T(8,128)(2,1)S(1)}, u32[]{:S(2)}, u32[]{:S(2)}) %collective-permute-start.6) | collective-permute-done | bytes 131104 | tf_op jit(solution)/shard_map/ppermute | solution.py:305
  19.4 0.4 %product.5 = bf16[32,512]{1,0:T(8,128)(2,1)S(1)} custom-call(bf16[32,2048]{1,0:T(8,128)(2,1)S(1)} %collective-permute-done.6.rows_ref, bf16[2048,512]{1,0:T(8,128)(2,1)S(1)} %weight.1.weight_ref), custom_call_target="tpu_custom_call" | custom-call | tf_op jit(solution)/shard_map/product/pallas_call | solution.py:308
  19.9 0.4 %product.6 = bf16[32,512]{1,0:T(8,128)(2,1)S(1)} custom-call(bf16[32,2048]{1,0:T(8,128)(2,1)S(1)} %collective-permute-done.8.rows_ref, bf16[2048,512]{1,0:T(8,128)(2,1)S(1)} %weight.1.weight_ref), custom_call_target="tpu_custom_call" | custom-call | tf_op jit(solution)/shard_map/product/pallas_call | solution.py:308
  20.3 0.3 %collective-permute-start.9 = (bf16[32,512]{1,0:T(8,128)(2,1)S(1)}, bf16[32,512]{1,0:T(8,128)(2,1)S(1)}, u32[]{:S(2)}, u32[]{:S(2)}) collective-permute-start(bf16[32,512]{1,0:T(8,128)(2,1)S(1)} %product.6), channel_id=1, source_target_pairs={{0,9},{1,4},{2,11},{3,6},{4,13},{5,0},{6,15},{7,2},{8,1},{9,12},{1... | collective-permute-start | bytes 98312 | tf_op jit(solution)/shard_map/ppermute | solution.py:316
  20.7 0.4 %product.7 = bf16[32,512]{1,0:T(8,128)(2,1)S(1)} custom-call(bf16[32,2048]{1,0:T(8,128)(2,1)S(1)} %collective-permute-done.10.rows_ref, bf16[2048,512]{1,0:T(8,128)(2,1)S(1)} %weight.1.weight_ref), custom_call_target="tpu_custom_call" | custom-call | tf_op jit(solution)/shard_map/product/pallas_call | solution.py:308
  21.1 0.5 %collective-permute-start.11 = (bf16[32,512]{1,0:T(8,128)(2,1)S(1)}, bf16[32,512]{1,0:T(8,128)(2,1)S(1)}, u32[]{:S(2)}, u32[]{:S(2)}) collective-permute-start(bf16[32,512]{1,0:T(8,128)(2,1)S(1)} %product.7), channel_id=1, source_target_pairs={{0,1},{1,2},{2,3},{3,0},{4,5},{5,6},{6,7},{7,4},{8,9},{9,10},{10,1... | collective-permute-start | bytes 98312 | tf_op jit(solution)/shard_map/ppermute | solution.py:316
  21.6 0.1 fusion
  21.8 2.8 %collective-permute-done.7.rest_1_ = bf16[32,512]{1,0:T(8,128)(2,1)S(1)} collective-permute-done((bf16[32,512]{1,0:T(8,128)(2,1)S(1)}, bf16[32,512]{1,0:T(8,128)(2,1)S(1)}, u32[]{:S(2)}, u32[]{:S(2)}) %collective-permute-start.7) | collective-permute-done | bytes 32800 | tf_op jit(solution)/shard_map/ppermute | solution.py:316
  24.6 0.1 collective-permute-start.12
  24.7 0.1 pad_maximum_fusion
  24.7 1.2 %collective-permute-done.12.received_ref = f32[2,16,512]{2,1,0:T(8,128)S(1)} collective-permute-done((f32[2,16,512]{2,1,0:T(8,128)S(1)}, f32[2,16,512]{2,1,0:T(8,128)S(1)}, u32[]{:S(2)}, u32[]{:S(2)}) %collective-permute-start.12) | collective-permute-done | bytes 65568 | tf_op jit(solution)/shard_map/ppermute | solution.py:326
  25.9 0.8 %finish.1 = bf16[16,512]{1,0:T(8,128)(2,1)} custom-call(s32[1]{0:T(128)} %bitcast.variant_ref, s32[1,16]{1,0:T(1,128)S(1)} %bitcast.8, f32[2,16,512]{2,1,0:T(8,128)S(1)} %get-tuple-element.32.kept_ref, f32[2,16,512]{2,1,0:T(8,128)S(1)} %collective-permute-done.12.received_ref, f32[16,128]{1,0:T(8,128)S(1)} %get-tuple-element.38.cosine_ref, ...), custom_call_target="tpu_custom_call" | custom-call | tf_op jit(solution)/shard_map/finish/pallas_call | solution.py:328
  (19 shorter events, 0.1 us)
Async XLA Ops:
  0.0 2.2 %collective-permute-start = (bf16[16,8192]{1,0:T(8,128)(2,1)}, bf16[16,8192]{1,0:T(8,128)(2,1)S(1)}, u32[]{:S(2)}, u32[]{:S(2)}) collective-permute-start(bf16[16,8192]{1,0:T(8,128)(2,1)} %rows_ref.1), channel_id=1, source_target_pairs={{0,1},{1,0},{2,3},{3,2},{4,5},{5,4},{6,7},{7,6},{8,9},{9,8},{10,11... | collective-permute-start | bytes 786440 | tf_op jit(solution)/shard_map/ppermute | solution.py:250
  0.5 1.7 %collective-permute-start.1 = (f32[8,512]{1,0:T(8,128)}, f32[8,512]{1,0:T(8,128)S(1)}, u32[]{:S(2)}, u32[]{:S(2)}) collective-permute-start(f32[8,512]{1,0:T(8,128)} %bitcast.11), channel_id=1, source_target_pairs={{0,1},{1,0},{2,3},{3,2},{4,5},{5,4},{6,7},{7,6},{8,9},{9,8},{10,11... | collective-permute-start | bytes 49160 | tf_op jit(solution)/shard_map/ppermute | solution.py:251
  0.5 1.7 %collective-permute-start.2 = (f32[8,512]{1,0:T(8,128)}, f32[8,512]{1,0:T(8,128)S(1)}, u32[]{:S(2)}, u32[]{:S(2)}) collective-permute-start(f32[8,512]{1,0:T(8,128)} %bitcast.13), channel_id=1, source_target_pairs={{0,1},{1,0},{2,3},{3,2},{4,5},{5,4},{6,7},{7,6},{8,9},{9,8},{10,11... | collective-permute-start | bytes 49160 | tf_op jit(solution)/shard_map/ppermute | solution.py:252
  2.2 10.0 %collective-permute-start.4 = (bf16[1024,512]{1,0:T(8,128)(2,1)}, bf16[1024,512]{1,0:T(8,128)(2,1)S(1)}, u32[]{:S(2)}, u32[]{:S(2)}) collective-permute-start(bf16[1024,512]{1,0:T(8,128)(2,1)} %bitcast.9), channel_id=1, source_target_pairs={{0,1},{1,0},{2,3},{3,2},{4,5},{5,4},{6,7},{7,6},{8,9},{9,8},{10,11... | collective-permute-start | bytes 3145736 | tf_op jit(solution)/shard_map/ppermute | solution.py:269
  2.6 12.0 %collective-permute-start.3 = (bf16[32,2048]{1,0:T(8,128)(2,1)S(1)}, bf16[32,2048]{1,0:T(8,128)(2,1)S(1)}, u32[]{:S(2)}, u32[]{:S(2)}) collective-permute-start(bf16[32,2048]{1,0:T(8,128)(2,1)S(1)} %get-tuple-element.24), channel_id=1, source_target_pairs={{0,14},{1,13},{2,12},{3,15},{4,10},{5,9},{6,8},{7,11},{8,6},{9,5},... | collective-permute-start | bytes 393224 | tf_op jit(solution)/shard_map/ppermute | solution.py:305
  8.7 10.8 %collective-permute-start.6 = (bf16[32,2048]{1,0:T(8,128)(2,1)S(1)}, bf16[32,2048]{1,0:T(8,128)(2,1)S(1)}, u32[]{:S(2)}, u32[]{:S(2)}) collective-permute-start(bf16[32,2048]{1,0:T(8,128)(2,1)S(1)} %get-tuple-element.29), channel_id=1, source_target_pairs={{0,10},{1,7},{2,8},{3,5},{4,14},{5,3},{6,12},{7,1},{8,2},{9,15},{1... | collective-permute-start | bytes 393224 | tf_op jit(solution)/shard_map/ppermute | solution.py:305
  8.7 11.2 %collective-permute-start.8 = (bf16[32,2048]{1,0:T(8,128)(2,1)S(1)}, bf16[32,2048]{1,0:T(8,128)(2,1)S(1)}, u32[]{:S(2)}, u32[]{:S(2)}) collective-permute-start(bf16[32,2048]{1,0:T(8,128)(2,1)S(1)} %get-tuple-element.30), channel_id=1, source_target_pairs={{0,8},{1,5},{2,10},{3,7},{4,12},{5,1},{6,14},{7,3},{8,0},{9,13},{1... | collective-permute-start | bytes 393224 | tf_op jit(solution)/shard_map/ppermute | solution.py:305
  11.6 9.1 %collective-permute-start.10 = (bf16[32,2048]{1,0:T(8,128)(2,1)S(1)}, bf16[32,2048]{1,0:T(8,128)(2,1)S(1)}, u32[]{:S(2)}, u32[]{:S(2)}) collective-permute-start(bf16[32,2048]{1,0:T(8,128)(2,1)S(1)} %get-tuple-element.31), channel_id=1, source_target_pairs={{0,0},{1,3},{2,2},{3,1},{4,4},{5,7},{6,6},{7,5},{8,8},{9,11},{10,1... | collective-permute-start | bytes 393224 | tf_op jit(solution)/shard_map/ppermute | solution.py:305
  12.2 9.4 %copy-start.1 = (s32[16]{0:T(128)S(1)}, s32[16]{0:T(128)}, u32[]{:S(2)}) copy-start(s32[16]{0:T(128)} %param.15) | copy-start | bytes 196
  12.3 13.7 %copy-start = (s32[16,1]{0,1:T(1,128)S(1)}, s32[16,1]{0,1:T(1,128)}, u32[]{:S(2)}) copy-start(s32[16,1]{0,1:T(1,128)} %param.14) | copy-start | bytes 196
  15.1 6.7 %collective-permute-start.5 = (bf16[32,512]{1,0:T(8,128)(2,1)S(1)}, bf16[32,512]{1,0:T(8,128)(2,1)S(1)}, u32[]{:S(2)}, u32[]{:S(2)}) collective-permute-start(bf16[32,512]{1,0:T(8,128)(2,1)S(1)} %product.4), channel_id=1, source_target_pairs={{0,15},{1,12},{2,13},{3,14},{4,11},{5,8},{6,9},{7,10},{8,7},{9,4},... | collective-permute-start | bytes 98312 | tf_op jit(solution)/shard_map/ppermute | solution.py:316
  19.9 4.7 %collective-permute-start.7 = (bf16[32,512]{1,0:T(8,128)(2,1)S(1)}, bf16[32,512]{1,0:T(8,128)(2,1)S(1)}, u32[]{:S(2)}, u32[]{:S(2)}) collective-permute-start(bf16[32,512]{1,0:T(8,128)(2,1)S(1)} %product.5), channel_id=1, source_target_pairs={{0,11},{1,6},{2,9},{3,4},{4,15},{5,2},{6,13},{7,0},{8,3},{9,14},{1... | collective-permute-start | bytes 98312 | tf_op jit(solution)/shard_map/ppermute | solution.py:316
  20.3 4.2 %collective-permute-start.9 = (bf16[32,512]{1,0:T(8,128)(2,1)S(1)}, bf16[32,512]{1,0:T(8,128)(2,1)S(1)}, u32[]{:S(2)}, u32[]{:S(2)}) collective-permute-start(bf16[32,512]{1,0:T(8,128)(2,1)S(1)} %product.6), channel_id=1, source_target_pairs={{0,9},{1,4},{2,11},{3,6},{4,13},{5,0},{6,15},{7,2},{8,1},{9,12},{1... | collective-permute-start | bytes 98312 | tf_op jit(solution)/shard_map/ppermute | solution.py:316
  21.1 3.4 %collective-permute-start.11 = (bf16[32,512]{1,0:T(8,128)(2,1)S(1)}, bf16[32,512]{1,0:T(8,128)(2,1)S(1)}, u32[]{:S(2)}, u32[]{:S(2)}) collective-permute-start(bf16[32,512]{1,0:T(8,128)(2,1)S(1)} %product.7), channel_id=1, source_target_pairs={{0,1},{1,2},{2,3},{3,0},{4,5},{5,6},{6,7},{7,4},{8,9},{9,10},{10,1... | collective-permute-start | bytes 98312 | tf_op jit(solution)/shard_map/ppermute | solution.py:316
  24.6 1.3 %collective-permute-start.12 = (f32[2,16,512]{2,1,0:T(8,128)S(1)}, f32[2,16,512]{2,1,0:T(8,128)S(1)}, u32[]{:S(2)}, u32[]{:S(2)}) collective-permute-start(f32[2,16,512]{2,1,0:T(8,128)S(1)} %get-tuple-element.33), channel_id=1, source_target_pairs={{0,1},{1,0},{2,3},{3,2},{4,5},{5,4},{6,7},{7,6},{8,9},{9,8},{10,11... | collective-permute-start | bytes 196616 | tf_op jit(solution)/shard_map/ppermute | solution.py:326

commit v7 on v6

--- a/solution.py
+++ b/solution.py
@@ -242,8 +242,10 @@
     orders = ((7, 5, 4, 0), (6, 3, 2, 1))
     steps = list(zip(*orders))
 
-    def route(distances, cross):
-        return [(index, (index ^ (2 * distances[index % 2])) ^ cross) for index in range(device_count)]
+    crossed = (0, 0, 1, 0)
+
+    def route(distances, cross, turned=0):
+        return [(index, (index ^ (2 * distances[(index % 2) ^ turned])) ^ cross) for index in range(device_count)]
 
     slice_shape, group_shape = (slice_rows, column_count), delta_scales.shape[2:]
     own_codes, own_scales, own_zeros = delta_codes[0, 0], delta_scales[0, 0], delta_zeros[0, 0]
@@ -302,7 +304,7 @@
         other_zeros,
     )
     weight, positions = lax.optimization_barrier((weight, positions))
-    incoming = [lax.ppermute(rows, "variant", route(distances, 0)) for rows, distances in zip(outgoing, steps)]
+    incoming = [lax.ppermute(rows, "variant", route(distances, cross)) for rows, distances, cross in zip(outgoing, steps, crossed)]
     parts = [None] * len(steps)
     for step in range(len(steps)):
         product = pl.pallas_call(
@@ -313,7 +315,7 @@
             compiler_params=pltpu.CompilerParams(vmem_limit_bytes=16 << 20),
             name="product",
         )(incoming[step], weight)
-        parts[step] = lax.ppermute(product, "variant", route(steps[step], 1))
+        parts[step] = lax.ppermute(product, "variant", route(steps[step], 1 ^ crossed[step], crossed[step]))
     kept, sent = pl.pallas_call(
         functools.partial(sum_kernel, orders[::-1]),
         out_shape=[jax.ShapeDtypeStruct((2, row_count, column_count), jnp.float32)] * 2,

time: 26.9 us -> 26.8 us (level)
  waiting for transfers between devices: 7.54 us -> 5.25 us
  starting transfers between devices: 12.4 us -> 14.5 us
    ppermute x8, waiting for transfers between devices: 6.36 us -> 4.07 us  [the longest x4 2.59 us: paired(): lax.ppermute(product, 'variant', route(steps[step], 1 ^ crossed[step], cr...]
    ppermute x8, starting transfers between devices: 11.2 us -> 13.3 us  [the longest x4 6.72 us: paired(): lax.ppermute(rows, 'variant', route(distances, cross))]
  transfers between devices with their start and end apart: 13 -> 13, of which waited for: 3 -> 5; matrix products, arithmetic and copies ran while one was open for 1% -> 1% of each run, Pallas kernels for 21% -> 21%
where the time goes in v7:
time: 26.8 us; the launch traced here: 26.5 us
  starting transfers between devices  14.5 us (54%)
  Pallas kernels  6.4 us (24%)
  waiting for transfers between devices  5.25 us (20%)
    ppermute x4, starting transfers between devices, paired(): lax.ppermute(rows, 'variant', route(distances, cross))  6.72 us
    ppermute x4, starting transfers between devices, paired(): lax.ppermute(product, 'variant', route(steps[step], 1 ^ crossed[step], cr...  6.6 us
    ppermute x4, waiting for transfers between devices, paired(): lax.ppermute(product, 'variant', route(steps[step], 1 ^ crossed[step], cr...  2.59 us
    pallas_call x1, Pallas kernels, paired(): pl.pallas_call(weight_kernel, out_shape=jax.ShapeDtypeStruct((2 * slice_r...  2.32 us
    pallas_call x4, Pallas kernels, paired(): pl.pallas_call(product_kernel, out_shape=jax.ShapeDtypeStruct((2 * row_co...  1.79 us
    ppermute x4, waiting for transfers between devices, paired(): lax.ppermute(rows, 'variant', route(distances, cross))  1.48 us
    pallas_call x1, Pallas kernels, paired(): pl.pallas_call(norm_kernel, out_shape=[jax.ShapeDtypeStruct((row_count, w...  1.22 us
    ppermute x1, waiting for transfers between devices, paired(): received = lax.ppermute(sent, 'variant', swap)  1.16 us
  transfers between devices with their start and end apart: 13, of which 5 were waited for; matrix products, arithmetic and copies ran while one was open for 1% of the time, Pallas kernels for 21%

profile of v7, /device:TPU:0, one launch (start us, length us, event | category | flops | bytes accessed | tf_op | source)
XLA Modules:
  0.0 26.5 jit_solution(10317921647980950421)
XLA Ops:
  0.0 0.5 %collective-permute-start = (bf16[16,8192]{1,0:T(8,128)(2,1)}, bf16[16,8192]{1,0:T(8,128)(2,1)S(1)}, u32[]{:S(2)}, u32[]{:S(2)}) collective-permute-start(bf16[16,8192]{1,0:T(8,128)(2,1)} %rows_ref.1), channel_id=1, source_target_pairs={{0,1},{1,0},{2,3},{3,2},{4,5},{5,4},{6,7},{7,6},{8,9},{9,8},{10,11... | collective-permute-start | bytes 786440 | tf_op jit(solution)/shard_map/ppermute | solution.py:252
  0.5 0.5 %collective-permute-start.2 = (f32[8,512]{1,0:T(8,128)}, f32[8,512]{1,0:T(8,128)S(1)}, u32[]{:S(2)}, u32[]{:S(2)}) collective-permute-start(f32[8,512]{1,0:T(8,128)} %bitcast.13), channel_id=1, source_target_pairs={{0,1},{1,0},{2,3},{3,2},{4,5},{5,4},{6,7},{7,6},{8,9},{9,8},{10,11... | collective-permute-start | bytes 49160 | tf_op jit(solution)/shard_map/ppermute | solution.py:254
  1.0 1.2 %norm.1 = (bf16[16,8192]{1,0:T(8,128)(2,1)S(1)}, f32[1,8192]{1,0:T(1,128)S(1)}) custom-call(bf16[16,8192]{1,0:T(8,128)(2,1)} %rows_ref.1, bf16[8192]{0:T(1024)(128)(2,1)} %gain_ref.1), custom_call_target="tpu_custom_call" | custom-call | tf_op jit(solution)/shard_map/norm/pallas_call | solution.py:255
  2.2 0.1 collective-permute-start.4
  2.4 0.3 %pieces.1 = (bf16[32,2048]{1,0:T(8,128)(2,1)S(1)}, bf16[32,2048]{1,0:T(8,128)(2,1)S(1)}, bf16[32,2048]{1,0:T(8,128)(2,1)S(1)}, bf16[32,2048]{1,0:T(8,128)(2,1)S(1)}) custom-call(s32[1]{0:T(128)} %bitcast.3.piece_ref, s32[1]{0:T(128)} %bitcast.2.core_ref, bf16[16,8192]{1,0:T(8,128)(2,1)S(1)} %get-tuple-element.21.own_ref, ...), custom_call_target="tpu_custom_call" | custom-call | tf_op jit(solution)/shard_map/pieces/pallas_call | solution.py:272
  2.6 6.0 %collective-permute-start.3 = (bf16[32,2048]{1,0:T(8,128)(2,1)S(1)}, bf16[32,2048]{1,0:T(8,128)(2,1)S(1)}, u32[]{:S(2)}, u32[]{:S(2)}) collective-permute-start(bf16[32,2048]{1,0:T(8,128)(2,1)S(1)} %get-tuple-element.24), channel_id=1, source_target_pairs={{0,14},{1,13},{2,12},{3,15},{4,10},{5,9},{6,8},{7,11},{8,6},{9,5},... | collective-permute-start | bytes 393224 | tf_op jit(solution)/shard_map/ppermute | solution.py:307
  8.7 0.7 %collective-permute-start.10 = (bf16[32,2048]{1,0:T(8,128)(2,1)S(1)}, bf16[32,2048]{1,0:T(8,128)(2,1)S(1)}, u32[]{:S(2)}, u32[]{:S(2)}) collective-permute-start(bf16[32,2048]{1,0:T(8,128)(2,1)S(1)} %get-tuple-element.31), channel_id=1, source_target_pairs={{0,0},{1,3},{2,2},{3,1},{4,4},{5,7},{6,6},{7,5},{8,8},{9,11},{10,1... | collective-permute-start | bytes 393224 | tf_op jit(solution)/shard_map/ppermute | solution.py:307
  9.4 2.3 %weight.1.weight_ref = bf16[2048,512]{1,0:T(8,128)(2,1)S(1)} custom-call(s32[1]{0:T(128)} %bitcast.2.core_ref, s32[1]{0:T(128)} %bitcast.7.first_ref, bf16[1024,512]{1,0:T(8,128)(2,1)} %bitcast.10, f32[8,512]{1,0:T(8,128)} %bitcast.12, f32[8,512]{1,0:T(8,128)} %bitcast.14, bf16[8192,512]{1,0:T(8,128)(2,1)} %base_ref.1, ...), custom_call_target="tpu_custom_call" | custom-call | tf_op jit(solution)/shard_map/weight/pallas_call | solution.py:281
  11.7 1.3 %collective-permute-done.3.rows_ref = bf16[32,2048]{1,0:T(8,128)(2,1)S(1)} collective-permute-done((bf16[32,2048]{1,0:T(8,128)(2,1)S(1)}, bf16[32,2048]{1,0:T(8,128)(2,1)S(1)}, u32[]{:S(2)}, u32[]{:S(2)}) %collective-permute-start.3) | collective-permute-done | bytes 131104 | tf_op jit(solution)/shard_map/ppermute | solution.py:307
  13.0 0.4 %product.4 = bf16[32,512]{1,0:T(8,128)(2,1)S(1)} custom-call(bf16[32,2048]{1,0:T(8,128)(2,1)S(1)} %collective-permute-done.3.rows_ref, bf16[2048,512]{1,0:T(8,128)(2,1)S(1)} %weight.1.weight_ref), custom_call_target="tpu_custom_call" | custom-call | tf_op jit(solution)/shard_map/product/pallas_call | solution.py:310
  13.4 5.2 %collective-permute-start.5 = (bf16[32,512]{1,0:T(8,128)(2,1)S(1)}, bf16[32,512]{1,0:T(8,128)(2,1)S(1)}, u32[]{:S(2)}, u32[]{:S(2)}) collective-permute-start(bf16[32,512]{1,0:T(8,128)(2,1)S(1)} %product.4), channel_id=1, source_target_pairs={{0,15},{1,12},{2,13},{3,14},{4,11},{5,8},{6,9},{7,10},{8,7},{9,4},... | collective-permute-start | bytes 98312 | tf_op jit(solution)/shard_map/ppermute | solution.py:318
  18.7 0.2 collective-permute-done.6.rows_ref
  18.9 0.4 %product.5 = bf16[32,512]{1,0:T(8,128)(2,1)S(1)} custom-call(bf16[32,2048]{1,0:T(8,128)(2,1)S(1)} %collective-permute-done.6.rows_ref, bf16[2048,512]{1,0:T(8,128)(2,1)S(1)} %weight.1.weight_ref), custom_call_target="tpu_custom_call" | custom-call | tf_op jit(solution)/shard_map/product/pallas_call | solution.py:310
  19.4 0.5 %product.6 = bf16[32,512]{1,0:T(8,128)(2,1)S(1)} custom-call(bf16[32,2048]{1,0:T(8,128)(2,1)S(1)} %collective-permute-done.8.rows_ref, bf16[2048,512]{1,0:T(8,128)(2,1)S(1)} %weight.1.weight_ref), custom_call_target="tpu_custom_call" | custom-call | tf_op jit(solution)/shard_map/product/pallas_call | solution.py:310
  19.8 0.4 %collective-permute-start.9 = (bf16[32,512]{1,0:T(8,128)(2,1)S(1)}, bf16[32,512]{1,0:T(8,128)(2,1)S(1)}, u32[]{:S(2)}, u32[]{:S(2)}) collective-permute-start(bf16[32,512]{1,0:T(8,128)(2,1)S(1)} %product.6), channel_id=1, source_target_pairs={{0,4},{1,9},{2,6},{3,11},{4,0},{5,13},{6,2},{7,15},{8,12},{9,1},{1... | collective-permute-start | bytes 98312 | tf_op jit(solution)/shard_map/ppermute | solution.py:318
  20.2 0.4 %product.7 = bf16[32,512]{1,0:T(8,128)(2,1)S(1)} custom-call(bf16[32,2048]{1,0:T(8,128)(2,1)S(1)} %collective-permute-done.10.rows_ref, bf16[2048,512]{1,0:T(8,128)(2,1)S(1)} %weight.1.weight_ref), custom_call_target="tpu_custom_call" | custom-call | tf_op jit(solution)/shard_map/product/pallas_call | solution.py:310
  20.6 1.0 %collective-permute-start.11 = (bf16[32,512]{1,0:T(8,128)(2,1)S(1)}, bf16[32,512]{1,0:T(8,128)(2,1)S(1)}, u32[]{:S(2)}, u32[]{:S(2)}) collective-permute-start(bf16[32,512]{1,0:T(8,128)(2,1)S(1)} %product.7), channel_id=1, source_target_pairs={{0,1},{1,2},{2,3},{3,0},{4,5},{5,6},{6,7},{7,4},{8,9},{9,10},{10,1... | collective-permute-start | bytes 98312 | tf_op jit(solution)/shard_map/ppermute | solution.py:318
  21.6 0.1 fusion
  21.8 1.8 %collective-permute-done.7.rest_1_ = bf16[32,512]{1,0:T(8,128)(2,1)S(1)} collective-permute-done((bf16[32,512]{1,0:T(8,128)(2,1)S(1)}, bf16[32,512]{1,0:T(8,128)(2,1)S(1)}, u32[]{:S(2)}, u32[]{:S(2)}) %collective-permute-start.7) | collective-permute-done | bytes 32800 | tf_op jit(solution)/shard_map/ppermute | solution.py:318
  23.6 0.8 %collective-permute-done.9.rest_2_ = bf16[32,512]{1,0:T(8,128)(2,1)S(1)} collective-permute-done((bf16[32,512]{1,0:T(8,128)(2,1)S(1)}, bf16[32,512]{1,0:T(8,128)(2,1)S(1)}, u32[]{:S(2)}, u32[]{:S(2)}) %collective-permute-start.9) | collective-permute-done | bytes 32800 | tf_op jit(solution)/shard_map/ppermute | solution.py:318
  24.4 0.1 collective-permute-start.12
  24.5 0.1 pad_maximum_fusion
  24.6 1.2 %collective-permute-done.12.received_ref = f32[2,16,512]{2,1,0:T(8,128)S(1)} collective-permute-done((f32[2,16,512]{2,1,0:T(8,128)S(1)}, f32[2,16,512]{2,1,0:T(8,128)S(1)}, u32[]{:S(2)}, u32[]{:S(2)}) %collective-permute-start.12) | collective-permute-done | bytes 65568 | tf_op jit(solution)/shard_map/ppermute | solution.py:328
  25.7 0.8 %finish.1 = bf16[16,512]{1,0:T(8,128)(2,1)} custom-call(s32[1]{0:T(128)} %bitcast.variant_ref, s32[1,16]{1,0:T(1,128)S(1)} %bitcast.8, f32[2,16,512]{2,1,0:T(8,128)S(1)} %get-tuple-element.32.kept_ref, f32[2,16,512]{2,1,0:T(8,128)S(1)} %collective-permute-done.12.received_ref, f32[16,128]{1,0:T(8,128)S(1)} %get-tuple-element.38.cosine_ref, ...), custom_call_target="tpu_custom_call" | custom-call | tf_op jit(solution)/shard_map/finish/pallas_call | solution.py:330
  (19 shorter events, 0.2 us)
Async XLA Ops:
  0.0 2.2 %collective-permute-start = (bf16[16,8192]{1,0:T(8,128)(2,1)}, bf16[16,8192]{1,0:T(8,128)(2,1)S(1)}, u32[]{:S(2)}, u32[]{:S(2)}) collective-permute-start(bf16[16,8192]{1,0:T(8,128)(2,1)} %rows_ref.1), channel_id=1, source_target_pairs={{0,1},{1,0},{2,3},{3,2},{4,5},{5,4},{6,7},{7,6},{8,9},{9,8},{10,11... | collective-permute-start | bytes 786440 | tf_op jit(solution)/shard_map/ppermute | solution.py:252
  0.5 1.7 %collective-permute-start.1 = (f32[8,512]{1,0:T(8,128)}, f32[8,512]{1,0:T(8,128)S(1)}, u32[]{:S(2)}, u32[]{:S(2)}) collective-permute-start(f32[8,512]{1,0:T(8,128)} %bitcast.11), channel_id=1, source_target_pairs={{0,1},{1,0},{2,3},{3,2},{4,5},{5,4},{6,7},{7,6},{8,9},{9,8},{10,11... | collective-permute-start | bytes 49160 | tf_op jit(solution)/shard_map/ppermute | solution.py:253
  0.5 1.7 %collective-permute-start.2 = (f32[8,512]{1,0:T(8,128)}, f32[8,512]{1,0:T(8,128)S(1)}, u32[]{:S(2)}, u32[]{:S(2)}) collective-permute-start(f32[8,512]{1,0:T(8,128)} %bitcast.13), channel_id=1, source_target_pairs={{0,1},{1,0},{2,3},{3,2},{4,5},{5,4},{6,7},{7,6},{8,9},{9,8},{10,11... | collective-permute-start | bytes 49160 | tf_op jit(solution)/shard_map/ppermute | solution.py:254
  2.2 7.2 %collective-permute-start.4 = (bf16[1024,512]{1,0:T(8,128)(2,1)}, bf16[1024,512]{1,0:T(8,128)(2,1)S(1)}, u32[]{:S(2)}, u32[]{:S(2)}) collective-permute-start(bf16[1024,512]{1,0:T(8,128)(2,1)} %bitcast.9), channel_id=1, source_target_pairs={{0,1},{1,0},{2,3},{3,2},{4,5},{5,4},{6,7},{7,6},{8,9},{9,8},{10,11... | collective-permute-start | bytes 3145736 | tf_op jit(solution)/shard_map/ppermute | solution.py:271
  2.6 10.4 %collective-permute-start.3 = (bf16[32,2048]{1,0:T(8,128)(2,1)S(1)}, bf16[32,2048]{1,0:T(8,128)(2,1)S(1)}, u32[]{:S(2)}, u32[]{:S(2)}) collective-permute-start(bf16[32,2048]{1,0:T(8,128)(2,1)S(1)} %get-tuple-element.24), channel_id=1, source_target_pairs={{0,14},{1,13},{2,12},{3,15},{4,10},{5,9},{6,8},{7,11},{8,6},{9,5},... | collective-permute-start | bytes 393224 | tf_op jit(solution)/shard_map/ppermute | solution.py:307
  8.7 10.2 %collective-permute-start.6 = (bf16[32,2048]{1,0:T(8,128)(2,1)S(1)}, bf16[32,2048]{1,0:T(8,128)(2,1)S(1)}, u32[]{:S(2)}, u32[]{:S(2)}) collective-permute-start(bf16[32,2048]{1,0:T(8,128)(2,1)S(1)} %get-tuple-element.29), channel_id=1, source_target_pairs={{0,10},{1,7},{2,8},{3,5},{4,14},{5,3},{6,12},{7,1},{8,2},{9,15},{1... | collective-permute-start | bytes 393224 | tf_op jit(solution)/shard_map/ppermute | solution.py:307
  8.7 10.7 %collective-permute-start.8 = (bf16[32,2048]{1,0:T(8,128)(2,1)S(1)}, bf16[32,2048]{1,0:T(8,128)(2,1)S(1)}, u32[]{:S(2)}, u32[]{:S(2)}) collective-permute-start(bf16[32,2048]{1,0:T(8,128)(2,1)S(1)} %get-tuple-element.30), channel_id=1, source_target_pairs={{0,9},{1,4},{2,11},{3,6},{4,13},{5,0},{6,15},{7,2},{8,1},{9,12},{1... | collective-permute-start | bytes 393224 | tf_op jit(solution)/shard_map/ppermute | solution.py:307
  8.7 11.5 %collective-permute-start.10 = (bf16[32,2048]{1,0:T(8,128)(2,1)S(1)}, bf16[32,2048]{1,0:T(8,128)(2,1)S(1)}, u32[]{:S(2)}, u32[]{:S(2)}) collective-permute-start(bf16[32,2048]{1,0:T(8,128)(2,1)S(1)} %get-tuple-element.31), channel_id=1, source_target_pairs={{0,0},{1,3},{2,2},{3,1},{4,4},{5,7},{6,6},{7,5},{8,8},{9,11},{10,1... | collective-permute-start | bytes 393224 | tf_op jit(solution)/shard_map/ppermute | solution.py:307
  9.4 12.2 %copy-start.1 = (s32[16]{0:T(128)S(1)}, s32[16]{0:T(128)}, u32[]{:S(2)}) copy-start(s32[16]{0:T(128)} %param.15) | copy-start | bytes 196
  9.4 16.3 %copy-start = (s32[16,1]{0,1:T(1,128)S(1)}, s32[16,1]{0,1:T(1,128)}, u32[]{:S(2)}) copy-start(s32[16,1]{0,1:T(1,128)} %param.14) | copy-start | bytes 196
  13.4 8.3 %collective-permute-start.5 = (bf16[32,512]{1,0:T(8,128)(2,1)S(1)}, bf16[32,512]{1,0:T(8,128)(2,1)S(1)}, u32[]{:S(2)}, u32[]{:S(2)}) collective-permute-start(bf16[32,512]{1,0:T(8,128)(2,1)S(1)} %product.4), channel_id=1, source_target_pairs={{0,15},{1,12},{2,13},{3,14},{4,11},{5,8},{6,9},{7,10},{8,7},{9,4},... | collective-permute-start | bytes 98312 | tf_op jit(solution)/shard_map/ppermute | solution.py:318
  19.3 4.3 %collective-permute-start.7 = (bf16[32,512]{1,0:T(8,128)(2,1)S(1)}, bf16[32,512]{1,0:T(8,128)(2,1)S(1)}, u32[]{:S(2)}, u32[]{:S(2)}) collective-permute-start(bf16[32,512]{1,0:T(8,128)(2,1)S(1)} %product.5), channel_id=1, source_target_pairs={{0,11},{1,6},{2,9},{3,4},{4,15},{5,2},{6,13},{7,0},{8,3},{9,14},{1... | collective-permute-start | bytes 98312 | tf_op jit(solution)/shard_map/ppermute | solution.py:318
  19.8 4.5 %collective-permute-start.9 = (bf16[32,512]{1,0:T(8,128)(2,1)S(1)}, bf16[32,512]{1,0:T(8,128)(2,1)S(1)}, u32[]{:S(2)}, u32[]{:S(2)}) collective-permute-start(bf16[32,512]{1,0:T(8,128)(2,1)S(1)} %product.6), channel_id=1, source_target_pairs={{0,4},{1,9},{2,6},{3,11},{4,0},{5,13},{6,2},{7,15},{8,12},{9,1},{1... | collective-permute-start | bytes 98312 | tf_op jit(solution)/shard_map/ppermute | solution.py:318
  20.6 3.7 %collective-permute-start.11 = (bf16[32,512]{1,0:T(8,128)(2,1)S(1)}, bf16[32,512]{1,0:T(8,128)(2,1)S(1)}, u32[]{:S(2)}, u32[]{:S(2)}) collective-permute-start(bf16[32,512]{1,0:T(8,128)(2,1)S(1)} %product.7), channel_id=1, source_target_pairs={{0,1},{1,2},{2,3},{3,0},{4,5},{5,6},{6,7},{7,4},{8,9},{9,10},{10,1... | collective-permute-start | bytes 98312 | tf_op jit(solution)/shard_map/ppermute | solution.py:318
  24.4 1.3 %collective-permute-start.12 = (f32[2,16,512]{2,1,0:T(8,128)S(1)}, f32[2,16,512]{2,1,0:T(8,128)S(1)}, u32[]{:S(2)}, u32[]{:S(2)}) collective-permute-start(f32[2,16,512]{2,1,0:T(8,128)S(1)} %get-tuple-element.33), channel_id=1, source_target_pairs={{0,1},{1,0},{2,3},{3,2},{4,5},{5,4},{6,7},{7,6},{8,9},{9,8},{10,11... | collective-permute-start | bytes 196616 | tf_op jit(solution)/shard_map/ppermute | solution.py:328

commit v8 on v7

--- a/solution.py
+++ b/solution.py
@@ -242,7 +242,7 @@
     orders = ((7, 5, 4, 0), (6, 3, 2, 1))
     steps = list(zip(*orders))
 
-    crossed = (0, 0, 1, 0)
+    crossed = (1, 0, 1, 0)
 
     def route(distances, cross, turned=0):
         return [(index, (index ^ (2 * distances[(index % 2) ^ turned])) ^ cross) for index in range(device_count)]

time: 26.8 us -> 27.4 us (1.022)
  waiting for transfers between devices: 5.25 us -> 8.22 us
  starting transfers between devices: 14.5 us -> 12.2 us
    ppermute x4, starting transfers between devices: 6.6 us -> 4.14 us  [paired(): lax.ppermute(product, 'variant', route(steps[step], 1 ^ crossed[step], cr...]
    ppermute x4, waiting for transfers between devices: 1.48 us -> 3.57 us  [paired(): lax.ppermute(rows, 'variant', route(distances, cross))]
    ppermute x4, waiting for transfers between devices: 2.59 us -> 3.48 us  [paired(): lax.ppermute(product, 'variant', route(steps[step], 1 ^ crossed[step], cr...]
  transfers between devices with their start and end apart: 13 -> 13, of which waited for: 5 -> 6; matrix products, arithmetic and copies ran while one was open for 1% -> 1% of each run, Pallas kernels for 21% -> 21%
where the time goes in v8:
time: 27.4 us; the launch traced here: 27.2 us
  starting transfers between devices  12.2 us (45%)
  waiting for transfers between devices  8.22 us (30%)
  Pallas kernels  6.39 us (23%)
    ppermute x4, starting transfers between devices, paired(): lax.ppermute(rows, 'variant', route(distances, cross))  6.89 us
    ppermute x4, starting transfers between devices, paired(): lax.ppermute(product, 'variant', route(steps[step], 1 ^ crossed[step], cr...  4.14 us
    ppermute x4, waiting for transfers between devices, paired(): lax.ppermute(rows, 'variant', route(distances, cross))  3.57 us
    ppermute x4, waiting for transfers between devices, paired(): lax.ppermute(product, 'variant', route(steps[step], 1 ^ crossed[step], cr...  3.48 us
    pallas_call x1, Pallas kernels, paired(): pl.pallas_call(weight_kernel, out_shape=jax.ShapeDtypeStruct((2 * slice_r...  2.32 us
    pallas_call x4, Pallas kernels, paired(): pl.pallas_call(product_kernel, out_shape=jax.ShapeDtypeStruct((2 * row_co...  1.79 us
    pallas_call x1, Pallas kernels, paired(): pl.pallas_call(norm_kernel, out_shape=[jax.ShapeDtypeStruct((row_count, w...  1.22 us
    ppermute x1, waiting for transfers between devices, paired(): received = lax.ppermute(sent, 'variant', swap)  1.16 us
  transfers between devices with their start and end apart: 13, of which 6 were waited for; matrix products, arithmetic and copies ran while one was open for 1% of the time, Pallas kernels for 21%

profile of v8, /device:TPU:0, one launch (start us, length us, event | category | flops | bytes accessed | tf_op | source)
XLA Modules:
  0.0 27.2 jit_solution(119691648062662066)
XLA Ops:
  0.0 0.5 %collective-permute-start = (bf16[16,8192]{1,0:T(8,128)(2,1)}, bf16[16,8192]{1,0:T(8,128)(2,1)S(1)}, u32[]{:S(2)}, u32[]{:S(2)}) collective-permute-start(bf16[16,8192]{1,0:T(8,128)(2,1)} %rows_ref.1), channel_id=1, source_target_pairs={{0,1},{1,0},{2,3},{3,2},{4,5},{5,4},{6,7},{7,6},{8,9},{9,8},{10,11... | collective-permute-start | bytes 786440 | tf_op jit(solution)/shard_map/ppermute | solution.py:252
  0.5 0.5 %collective-permute-start.2 = (f32[8,512]{1,0:T(8,128)}, f32[8,512]{1,0:T(8,128)S(1)}, u32[]{:S(2)}, u32[]{:S(2)}) collective-permute-start(f32[8,512]{1,0:T(8,128)} %bitcast.13), channel_id=1, source_target_pairs={{0,1},{1,0},{2,3},{3,2},{4,5},{5,4},{6,7},{7,6},{8,9},{9,8},{10,11... | collective-permute-start | bytes 49160 | tf_op jit(solution)/shard_map/ppermute | solution.py:254
  1.0 1.2 %norm.1 = (bf16[16,8192]{1,0:T(8,128)(2,1)S(1)}, f32[1,8192]{1,0:T(1,128)S(1)}) custom-call(bf16[16,8192]{1,0:T(8,128)(2,1)} %rows_ref.1, bf16[8192]{0:T(1024)(128)(2,1)} %gain_ref.1), custom_call_target="tpu_custom_call" | custom-call | tf_op jit(solution)/shard_map/norm/pallas_call | solution.py:255
  2.2 0.1 collective-permute-start.4
  2.4 0.3 pieces.1
  2.6 5.7 %collective-permute-start.3 = (bf16[32,2048]{1,0:T(8,128)(2,1)S(1)}, bf16[32,2048]{1,0:T(8,128)(2,1)S(1)}, u32[]{:S(2)}, u32[]{:S(2)}) collective-permute-start(bf16[32,2048]{1,0:T(8,128)(2,1)S(1)} %get-tuple-element.24), channel_id=1, source_target_pairs={{0,15},{1,12},{2,13},{3,14},{4,11},{5,8},{6,9},{7,10},{8,7},{9,4},... | collective-permute-start | bytes 393224 | tf_op jit(solution)/shard_map/ppermute | solution.py:307
  8.3 0.5 %collective-permute-start.8 = (bf16[32,2048]{1,0:T(8,128)(2,1)S(1)}, bf16[32,2048]{1,0:T(8,128)(2,1)S(1)}, u32[]{:S(2)}, u32[]{:S(2)}) collective-permute-start(bf16[32,2048]{1,0:T(8,128)(2,1)S(1)} %get-tuple-element.30), channel_id=1, source_target_pairs={{0,9},{1,4},{2,11},{3,6},{4,13},{5,0},{6,15},{7,2},{8,1},{9,12},{1... | collective-permute-start | bytes 393224 | tf_op jit(solution)/shard_map/ppermute | solution.py:307
  8.9 0.7 %collective-permute-start.10 = (bf16[32,2048]{1,0:T(8,128)(2,1)S(1)}, bf16[32,2048]{1,0:T(8,128)(2,1)S(1)}, u32[]{:S(2)}, u32[]{:S(2)}) collective-permute-start(bf16[32,2048]{1,0:T(8,128)(2,1)S(1)} %get-tuple-element.31), channel_id=1, source_target_pairs={{0,0},{1,3},{2,2},{3,1},{4,4},{5,7},{6,6},{7,5},{8,8},{9,11},{10,1... | collective-permute-start | bytes 393224 | tf_op jit(solution)/shard_map/ppermute | solution.py:307
  9.6 2.3 %weight.1.weight_ref = bf16[2048,512]{1,0:T(8,128)(2,1)S(1)} custom-call(s32[1]{0:T(128)} %bitcast.2.core_ref, s32[1]{0:T(128)} %bitcast.7.first_ref, bf16[1024,512]{1,0:T(8,128)(2,1)} %bitcast.10, f32[8,512]{1,0:T(8,128)} %bitcast.12, f32[8,512]{1,0:T(8,128)} %bitcast.14, bf16[8192,512]{1,0:T(8,128)(2,1)} %base_ref.1, ...), custom_call_target="tpu_custom_call" | custom-call | tf_op jit(solution)/shard_map/weight/pallas_call | solution.py:281
  11.9 0.3 %collective-permute-done.3.rows_ref = bf16[32,2048]{1,0:T(8,128)(2,1)S(1)} collective-permute-done((bf16[32,2048]{1,0:T(8,128)(2,1)S(1)}, bf16[32,2048]{1,0:T(8,128)(2,1)S(1)}, u32[]{:S(2)}, u32[]{:S(2)}) %collective-permute-start.3) | collective-permute-done | bytes 131104 | tf_op jit(solution)/shard_map/ppermute | solution.py:307
  12.2 0.4 %product.4 = bf16[32,512]{1,0:T(8,128)(2,1)S(1)} custom-call(bf16[32,2048]{1,0:T(8,128)(2,1)S(1)} %collective-permute-done.3.rows_ref, bf16[2048,512]{1,0:T(8,128)(2,1)S(1)} %weight.1.weight_ref), custom_call_target="tpu_custom_call" | custom-call | tf_op jit(solution)/shard_map/product/pallas_call | solution.py:310
  12.7 3.3 %collective-permute-start.5 = (bf16[32,512]{1,0:T(8,128)(2,1)S(1)}, bf16[32,512]{1,0:T(8,128)(2,1)S(1)}, u32[]{:S(2)}, u32[]{:S(2)}) collective-permute-start(bf16[32,512]{1,0:T(8,128)(2,1)S(1)} %product.4), channel_id=1, source_target_pairs={{0,12},{1,15},{2,14},{3,13},{4,8},{5,11},{6,10},{7,9},{8,4},{9,7},... | collective-permute-start | bytes 98312 | tf_op jit(solution)/shard_map/ppermute | solution.py:318
  16.0 3.2 %collective-permute-done.6.rows_ref = bf16[32,2048]{1,0:T(8,128)(2,1)S(1)} collective-permute-done((bf16[32,2048]{1,0:T(8,128)(2,1)S(1)}, bf16[32,2048]{1,0:T(8,128)(2,1)S(1)}, u32[]{:S(2)}, u32[]{:S(2)}) %collective-permute-start.6) | collective-permute-done | bytes 131104 | tf_op jit(solution)/shard_map/ppermute | solution.py:307
  19.2 0.4 %product.5 = bf16[32,512]{1,0:T(8,128)(2,1)S(1)} custom-call(bf16[32,2048]{1,0:T(8,128)(2,1)S(1)} %collective-permute-done.6.rows_ref, bf16[2048,512]{1,0:T(8,128)(2,1)S(1)} %weight.1.weight_ref), custom_call_target="tpu_custom_call" | custom-call | tf_op jit(solution)/shard_map/product/pallas_call | solution.py:310
  19.7 0.3 %collective-permute-start.7 = (bf16[32,512]{1,0:T(8,128)(2,1)S(1)}, bf16[32,512]{1,0:T(8,128)(2,1)S(1)}, u32[]{:S(2)}, u32[]{:S(2)}) collective-permute-start(bf16[32,512]{1,0:T(8,128)(2,1)S(1)} %product.5), channel_id=1, source_target_pairs={{0,11},{1,6},{2,9},{3,4},{4,15},{5,2},{6,13},{7,0},{8,3},{9,14},{1... | collective-permute-start | bytes 98312 | tf_op jit(solution)/shard_map/ppermute | solution.py:318
  20.0 0.4 %product.6 = bf16[32,512]{1,0:T(8,128)(2,1)S(1)} custom-call(bf16[32,2048]{1,0:T(8,128)(2,1)S(1)} %collective-permute-done.8.rows_ref, bf16[2048,512]{1,0:T(8,128)(2,1)S(1)} %weight.1.weight_ref), custom_call_target="tpu_custom_call" | custom-call | tf_op jit(solution)/shard_map/product/pallas_call | solution.py:310
  20.4 0.3 %collective-permute-start.9 = (bf16[32,512]{1,0:T(8,128)(2,1)S(1)}, bf16[32,512]{1,0:T(8,128)(2,1)S(1)}, u32[]{:S(2)}, u32[]{:S(2)}) collective-permute-start(bf16[32,512]{1,0:T(8,128)(2,1)S(1)} %product.6), channel_id=1, source_target_pairs={{0,4},{1,9},{2,6},{3,11},{4,0},{5,13},{6,2},{7,15},{8,12},{9,1},{1... | collective-permute-start | bytes 98312 | tf_op jit(solution)/shard_map/ppermute | solution.py:318
  20.7 0.4 %product.7 = bf16[32,512]{1,0:T(8,128)(2,1)S(1)} custom-call(bf16[32,2048]{1,0:T(8,128)(2,1)S(1)} %collective-permute-done.10.rows_ref, bf16[2048,512]{1,0:T(8,128)(2,1)S(1)} %weight.1.weight_ref), custom_call_target="tpu_custom_call" | custom-call | tf_op jit(solution)/shard_map/product/pallas_call | solution.py:310
  21.2 0.2 collective-permute-start.11
  21.4 0.1 fusion
  21.6 2.4 %collective-permute-done.7.rest_1_ = bf16[32,512]{1,0:T(8,128)(2,1)S(1)} collective-permute-done((bf16[32,512]{1,0:T(8,128)(2,1)S(1)}, bf16[32,512]{1,0:T(8,128)(2,1)S(1)}, u32[]{:S(2)}, u32[]{:S(2)}) %collective-permute-start.7) | collective-permute-done | bytes 32800 | tf_op jit(solution)/shard_map/ppermute | solution.py:318
  23.9 1.0 %collective-permute-done.9.rest_2_ = bf16[32,512]{1,0:T(8,128)(2,1)S(1)} collective-permute-done((bf16[32,512]{1,0:T(8,128)(2,1)S(1)}, bf16[32,512]{1,0:T(8,128)(2,1)S(1)}, u32[]{:S(2)}, u32[]{:S(2)}) %collective-permute-start.9) | collective-permute-done | bytes 32800 | tf_op jit(solution)/shard_map/ppermute | solution.py:318
  25.2 1.2 %collective-permute-done.12.received_ref = f32[2,16,512]{2,1,0:T(8,128)S(1)} collective-permute-done((f32[2,16,512]{2,1,0:T(8,128)S(1)}, f32[2,16,512]{2,1,0:T(8,128)S(1)}, u32[]{:S(2)}, u32[]{:S(2)}) %collective-permute-start.12) | collective-permute-done | bytes 65568 | tf_op jit(solution)/shard_map/ppermute | solution.py:328
  26.4 0.8 %finish.1 = bf16[16,512]{1,0:T(8,128)(2,1)} custom-call(s32[1]{0:T(128)} %bitcast.variant_ref, s32[1,16]{1,0:T(1,128)S(1)} %bitcast.8, f32[2,16,512]{2,1,0:T(8,128)S(1)} %get-tuple-element.32.kept_ref, f32[2,16,512]{2,1,0:T(8,128)S(1)} %collective-permute-done.12.received_ref, f32[16,128]{1,0:T(8,128)S(1)} %get-tuple-element.38.cosine_ref, ...), custom_call_target="tpu_custom_call" | custom-call | tf_op jit(solution)/shard_map/finish/pallas_call | solution.py:330
  (19 shorter events, 0.3 us)
Async XLA Ops:
  0.0 2.2 %collective-permute-start = (bf16[16,8192]{1,0:T(8,128)(2,1)}, bf16[16,8192]{1,0:T(8,128)(2,1)S(1)}, u32[]{:S(2)}, u32[]{:S(2)}) collective-permute-start(bf16[16,8192]{1,0:T(8,128)(2,1)} %rows_ref.1), channel_id=1, source_target_pairs={{0,1},{1,0},{2,3},{3,2},{4,5},{5,4},{6,7},{7,6},{8,9},{9,8},{10,11... | collective-permute-start | bytes 786440 | tf_op jit(solution)/shard_map/ppermute | solution.py:252
  0.5 1.7 %collective-permute-start.1 = (f32[8,512]{1,0:T(8,128)}, f32[8,512]{1,0:T(8,128)S(1)}, u32[]{:S(2)}, u32[]{:S(2)}) collective-permute-start(f32[8,512]{1,0:T(8,128)} %bitcast.11), channel_id=1, source_target_pairs={{0,1},{1,0},{2,3},{3,2},{4,5},{5,4},{6,7},{7,6},{8,9},{9,8},{10,11... | collective-permute-start | bytes 49160 | tf_op jit(solution)/shard_map/ppermute | solution.py:253
  0.5 1.7 %collective-permute-start.2 = (f32[8,512]{1,0:T(8,128)}, f32[8,512]{1,0:T(8,128)S(1)}, u32[]{:S(2)}, u32[]{:S(2)}) collective-permute-start(f32[8,512]{1,0:T(8,128)} %bitcast.13), channel_id=1, source_target_pairs={{0,1},{1,0},{2,3},{3,2},{4,5},{5,4},{6,7},{7,6},{8,9},{9,8},{10,11... | collective-permute-start | bytes 49160 | tf_op jit(solution)/shard_map/ppermute | solution.py:254
  2.2 7.3 %collective-permute-start.4 = (bf16[1024,512]{1,0:T(8,128)(2,1)}, bf16[1024,512]{1,0:T(8,128)(2,1)S(1)}, u32[]{:S(2)}, u32[]{:S(2)}) collective-permute-start(bf16[1024,512]{1,0:T(8,128)(2,1)} %bitcast.9), channel_id=1, source_target_pairs={{0,1},{1,0},{2,3},{3,2},{4,5},{5,4},{6,7},{7,6},{8,9},{9,8},{10,11... | collective-permute-start | bytes 3145736 | tf_op jit(solution)/shard_map/ppermute | solution.py:271
  2.6 9.6 %collective-permute-start.3 = (bf16[32,2048]{1,0:T(8,128)(2,1)S(1)}, bf16[32,2048]{1,0:T(8,128)(2,1)S(1)}, u32[]{:S(2)}, u32[]{:S(2)}) collective-permute-start(bf16[32,2048]{1,0:T(8,128)(2,1)S(1)} %get-tuple-element.24), channel_id=1, source_target_pairs={{0,15},{1,12},{2,13},{3,14},{4,11},{5,8},{6,9},{7,10},{8,7},{9,4},... | collective-permute-start | bytes 393224 | tf_op jit(solution)/shard_map/ppermute | solution.py:307
  8.3 10.9 %collective-permute-start.6 = (bf16[32,2048]{1,0:T(8,128)(2,1)S(1)}, bf16[32,2048]{1,0:T(8,128)(2,1)S(1)}, u32[]{:S(2)}, u32[]{:S(2)}) collective-permute-start(bf16[32,2048]{1,0:T(8,128)(2,1)S(1)} %get-tuple-element.29), channel_id=1, source_target_pairs={{0,10},{1,7},{2,8},{3,5},{4,14},{5,3},{6,12},{7,1},{8,2},{9,15},{1... | collective-permute-start | bytes 393224 | tf_op jit(solution)/shard_map/ppermute | solution.py:307
  8.3 11.6 %collective-permute-start.8 = (bf16[32,2048]{1,0:T(8,128)(2,1)S(1)}, bf16[32,2048]{1,0:T(8,128)(2,1)S(1)}, u32[]{:S(2)}, u32[]{:S(2)}) collective-permute-start(bf16[32,2048]{1,0:T(8,128)(2,1)S(1)} %get-tuple-element.30), channel_id=1, source_target_pairs={{0,9},{1,4},{2,11},{3,6},{4,13},{5,0},{6,15},{7,2},{8,1},{9,12},{1... | collective-permute-start | bytes 393224 | tf_op jit(solution)/shard_map/ppermute | solution.py:307
  8.9 11.9 %collective-permute-start.10 = (bf16[32,2048]{1,0:T(8,128)(2,1)S(1)}, bf16[32,2048]{1,0:T(8,128)(2,1)S(1)}, u32[]{:S(2)}, u32[]{:S(2)}) collective-permute-start(bf16[32,2048]{1,0:T(8,128)(2,1)S(1)} %get-tuple-element.31), channel_id=1, source_target_pairs={{0,0},{1,3},{2,2},{3,1},{4,4},{5,7},{6,6},{7,5},{8,8},{9,11},{10,1... | collective-permute-start | bytes 393224 | tf_op jit(solution)/shard_map/ppermute | solution.py:307
  9.6 11.9 %copy-start.1 = (s32[16]{0:T(128)S(1)}, s32[16]{0:T(128)}, u32[]{:S(2)}) copy-start(s32[16]{0:T(128)} %param.15) | copy-start | bytes 196
  9.6 16.8 %copy-start = (s32[16,1]{0,1:T(1,128)S(1)}, s32[16,1]{0,1:T(1,128)}, u32[]{:S(2)}) copy-start(s32[16,1]{0,1:T(1,128)} %param.14) | copy-start | bytes 196
  12.7 8.9 %collective-permute-start.5 = (bf16[32,512]{1,0:T(8,128)(2,1)S(1)}, bf16[32,512]{1,0:T(8,128)(2,1)S(1)}, u32[]{:S(2)}, u32[]{:S(2)}) collective-permute-start(bf16[32,512]{1,0:T(8,128)(2,1)S(1)} %product.4), channel_id=1, source_target_pairs={{0,12},{1,15},{2,14},{3,13},{4,8},{5,11},{6,10},{7,9},{8,4},{9,7},... | collective-permute-start | bytes 98312 | tf_op jit(solution)/shard_map/ppermute | solution.py:318
  19.7 4.3 %collective-permute-start.7 = (bf16[32,512]{1,0:T(8,128)(2,1)S(1)}, bf16[32,512]{1,0:T(8,128)(2,1)S(1)}, u32[]{:S(2)}, u32[]{:S(2)}) collective-permute-start(bf16[32,512]{1,0:T(8,128)(2,1)S(1)} %product.5), channel_id=1, source_target_pairs={{0,11},{1,6},{2,9},{3,4},{4,15},{5,2},{6,13},{7,0},{8,3},{9,14},{1... | collective-permute-start | bytes 98312 | tf_op jit(solution)/shard_map/ppermute | solution.py:318
  20.4 4.6 %collective-permute-start.9 = (bf16[32,512]{1,0:T(8,128)(2,1)S(1)}, bf16[32,512]{1,0:T(8,128)(2,1)S(1)}, u32[]{:S(2)}, u32[]{:S(2)}) collective-permute-start(bf16[32,512]{1,0:T(8,128)(2,1)S(1)} %product.6), channel_id=1, source_target_pairs={{0,4},{1,9},{2,6},{3,11},{4,0},{5,13},{6,2},{7,15},{8,12},{9,1},{1... | collective-permute-start | bytes 98312 | tf_op jit(solution)/shard_map/ppermute | solution.py:318
  21.2 3.9 %collective-permute-start.11 = (bf16[32,512]{1,0:T(8,128)(2,1)S(1)}, bf16[32,512]{1,0:T(8,128)(2,1)S(1)}, u32[]{:S(2)}, u32[]{:S(2)}) collective-permute-start(bf16[32,512]{1,0:T(8,128)(2,1)S(1)} %product.7), channel_id=1, source_target_pairs={{0,1},{1,2},{2,3},{3,0},{4,5},{5,6},{6,7},{7,4},{8,9},{9,10},{10,1... | collective-permute-start | bytes 98312 | tf_op jit(solution)/shard_map/ppermute | solution.py:318
  25.1 1.3 %collective-permute-start.12 = (f32[2,16,512]{2,1,0:T(8,128)S(1)}, f32[2,16,512]{2,1,0:T(8,128)S(1)}, u32[]{:S(2)}, u32[]{:S(2)}) collective-permute-start(f32[2,16,512]{2,1,0:T(8,128)S(1)} %get-tuple-element.33), channel_id=1, source_target_pairs={{0,1},{1,0},{2,3},{3,2},{4,5},{5,4},{6,7},{7,6},{8,9},{9,8},{10,11... | collective-permute-start | bytes 196616 | tf_op jit(solution)/shard_map/ppermute | solution.py:328
